TPU v7x, 32 devices: a whole 2x2x4 slice. The times are simulated.
32 devices in a mesh: tm: 4 (over x, core), space: 8 (over z, y).
Axes of the slice: x: 2, y: 2, z: 4, core: 2. Of those that a mesh axis runs over, the one named last changes fastest.
Arguments:
- guesses: float32 [4, 128, 4096], P('tm', 'space'), may hold values from -6 to 6
- cond_x: float32 [128, 4096], P('space'), may hold values from 0.025 to 0.24
- cond_y: float32 [128, 4096], P('space'), may hold values from 0.005 to 0.05
- source: float32 [128, 4096], P('space'), may hold values from -0.6 to 0.6
- inflow: float32 [64, 2048], P('space'), may hold values from -6 to 6
Outputs:
- corrected: float32 [4, 128, 4096], P('tm', 'space')
All inputs are finite; a program needn't handle non-finite values.
Results may differ from a plain program's by a relative error of at most 0.00002.
Values sent between devices are 32-bit elements; how exact they have to be, the bound alone decides.
No kernel may reach another device: no remote copies, remote signals or barrier semaphores. Data moves between devices by JAX's collectives and lax.ppermute only.
A program may use at most 128 MiB of HBM per device.

v0:
```python
import jax
import jax.numpy as jnp
from jax import lax
from jax.sharding import PartitionSpec as P


def padded(value, sides, width):
    for axis, dim in sides:
        devices, length = (lax.axis_size(axis), value.shape[dim])
        up = [(i, (i + 1) % devices) for i in range(devices - 1)]
        down = [(j, i) for i, j in up]
        last = lax.slice_in_dim(value, length - width, length, axis=dim)
        leading = lax.slice_in_dim(value, 0, width, axis=dim)
        before = lax.ppermute(last, axis, up)
        after = lax.ppermute(leading, axis, down)
        value = jnp.concatenate([before, value, after], axis=dim)
    return value


def from_behind(value, axis, steps):
    count = lax.axis_size(axis)
    leading, last = (max(0, -steps), min(count, count - steps))
    return lax.ppermute(value, axis, [(source, source + steps) for source in range(leading, last)])


def interior(field_ext, cond_rows, cond_cols):
    centre = field_ext[1:-1]
    flux_sum = cond_rows[1:-1] * (field_ext[2:] - centre) - cond_rows[:-2] * (
        centre - field_ext[:-2]
    )
    widened = jnp.pad(centre, ((0, 0), (1, 1)))
    cond_own = cond_cols[1:-1]
    cond_west = jnp.pad(cond_own, ((0, 0), (1, 0)))[:, :-1]
    flux_sum = (
        flux_sum + cond_own * (widened[:, 2:] - centre) - cond_west * (centre - widened[:, :-2])
    )
    return centre + flux_sum


def propagate(field, coef_pad):
    strip_rows = field.shape[0]
    cond_rows = coef_pad[0, 3 : strip_rows + 5]
    cond_cols = coef_pad[1, 3 : strip_rows + 5]
    source_rows = coef_pad[2, 4 : strip_rows + 4]
    for section in range(4):
        extended = padded(field, (("space", 0),), 1)
        field = interior(extended, cond_rows, cond_cols) + source_rows
    return field


def restrict(field):
    lead = field.shape[:-2]
    shaped = field.reshape(lead + (field.shape[-2] // 2, 2, field.shape[-1] // 2, 2))
    return jnp.mean(shaped, axis=(-3, -1))


def shards(guesses, cond_x, cond_y, source, inflow):
    strip_rows = cond_x.shape[0]
    columns = cond_x.shape[1]
    stacked = jnp.stack([cond_x, cond_y, source])
    edge_rows = from_behind(cond_x[strip_rows - 2 :], "space", 1)
    cond_upper = jnp.concatenate([jnp.zeros((2, columns), jnp.float32), edge_rows], axis=0)
    blank_rows = jnp.zeros((4, columns), jnp.float32)
    upper = jnp.stack([cond_upper, blank_rows, blank_rows])
    lower = jnp.zeros((3, 4, columns), jnp.float32)
    coef_pad = jnp.concatenate([upper, stacked, lower], axis=1)
    first_group = lax.axis_index("tm") == 0
    c_point = guesses[0]
    first_pass = propagate(c_point, coef_pad)
    received = from_behind(first_pass, "tm", 1)
    relaxed = jnp.where(first_group, c_point, received)
    second_pass = propagate(relaxed, coef_pad)
    fine_next = from_behind(second_pass, "tm", 1)
    residual = restrict(fine_next - relaxed)
    residual = jnp.where(first_group, 0.0, residual)
    coarse_coef = restrict(coef_pad[:2, 2 : strip_rows + 6])

    def chain_round(index, error_field):
        extended = padded(error_field, (("space", 0),), 1)
        stepped = interior(extended, coarse_coef[0], coarse_coef[1])
        arrived = from_behind(stepped, "tm", 1)
        return jnp.where(first_group, inflow, arrived + residual)

    start_error = jnp.where(first_group, inflow, jnp.zeros_like(residual))
    error_field = lax.fori_loop(0, lax.axis_size("tm") - 1, chain_round, start_error)
    widened = jnp.repeat(jnp.repeat(error_field, 2, axis=0), 2, axis=1)
    return (relaxed + widened)[None]


def solution(mesh):
    return jax.shard_map(
        shards,
        mesh=mesh,
        in_specs=(
            P("tm", "space", None),
            P("space", None),
            P("space", None),
            P("space", None),
            P("space", None),
        ),
        out_specs=P("tm", "space", None),
        check_vma=False,
    )
```

profile of v0, /device:TPU:9, one launch (start us, length us, event | category | flops | bytes accessed | tf_op | source)
XLA Modules:
  0.0 243.4 jit_solution(10681423357051758690)
XLA Ops:
  0.9 3.1 %collective-permute-start.4 = (f32[2,4096]{1,0:T(2,128)S(1)}, f32[2,4096]{1,0:T(2,128)S(1)}, u32[]{:S(2)}, u32[]{:S(2)}) collective-permute-start(f32[2,4096]{1,0:T(2,128)S(1)} %slice.302), channel_id=1, source_target_pairs={{0,1},{1,2},{2,3},{3,4},{4,5},{5,6},{6,7},{8,9},{9,10},{10,11},{11... | collective-permute-start | bytes 98312 | tf_op jit(solution)/shard_map/ppermute | solution.py:23
  5.1 3.0 %collective-permute-start.3 = (f32[1,4096]{1,0:T(1,128)S(1)}, f32[1,4096]{1,0:T(1,128)S(1)}, u32[]{:S(2)}, u32[]{:S(2)}) collective-permute-start(f32[1,4096]{1,0:T(1,128)S(1)} %get-tuple-element.125), channel_id=1, source_target_pairs={{1,0},{2,1},{3,2},{4,3},{5,4},{6,5},{7,6},{9,8},{10,9},{11,10},{12... | collective-permute-start | bytes 49160 | tf_op jit(solution)/shard_map/ppermute | solution.py:15
  10.5 3.0 %collective-permute-done.5 = f32[1,4096]{1,0:T(1,128)S(1)} collective-permute-done((f32[1,4096]{1,0:T(1,128)S(1)}, f32[1,4096]{1,0:T(1,128)S(1)}, u32[]{:S(2)}, u32[]{:S(2)}) %collective-permute-start.5) | collective-permute-done | bytes 16416 | tf_op jit(solution)/shard_map/ppermute | solution.py:14
  17.8 3.4 %collective-permute-start.7 = (f32[1,4096]{1,0:T(1,128)S(1)}, f32[1,4096]{1,0:T(1,128)S(1)}, u32[]{:S(2)}, u32[]{:S(2)}) collective-permute-start(f32[1,4096]{1,0:T(1,128)S(1)} %get-tuple-element.124), channel_id=1, source_target_pairs={{0,1},{1,2},{2,3},{3,4},{4,5},{5,6},{6,7},{8,9},{9,10},{10,11},{11... | collective-permute-start | bytes 49160 | tf_op jit(solution)/shard_map/ppermute | solution.py:14
  26.7 3.4 %collective-permute-start.9 = (f32[1,4096]{1,0:T(1,128)S(1)}, f32[1,4096]{1,0:T(1,128)S(1)}, u32[]{:S(2)}, u32[]{:S(2)}) collective-permute-start(f32[1,4096]{1,0:T(1,128)S(1)} %get-tuple-element.122), channel_id=1, source_target_pairs={{0,1},{1,2},{2,3},{3,4},{4,5},{5,6},{6,7},{8,9},{9,10},{10,11},{11... | collective-permute-start | bytes 49160 | tf_op jit(solution)/shard_map/ppermute | solution.py:14
  35.6 3.4 %collective-permute-start.11 = (f32[1,4096]{1,0:T(1,128)S(1)}, f32[1,4096]{1,0:T(1,128)S(1)}, u32[]{:S(2)}, u32[]{:S(2)}) collective-permute-start(f32[1,4096]{1,0:T(1,128)S(1)} %get-tuple-element.120), channel_id=1, source_target_pairs={{0,1},{1,2},{2,3},{3,4},{4,5},{5,6},{6,7},{8,9},{9,10},{10,11},{11... | collective-permute-start | bytes 49160 | tf_op jit(solution)/shard_map/ppermute | solution.py:14
  42.5 8.8 %collective-permute-start.12 = (f32[16,4096]{1,0:T(8,128)S(1)}, f32[16,4096]{1,0:T(8,128)S(1)}, u32[]{:S(2)}, u32[]{:S(2)}) collective-permute-start(f32[16,4096]{1,0:T(8,128)S(1)} %fusion.55), channel_id=1, source_target_pairs={{0,8},{8,16},{16,24},{1,9},{9,17},{17,25},{2,10},{10,18},{18,26},{... | collective-permute-start | bytes 786440 | tf_op jit(solution)/shard_map/ppermute | solution.py:23
  51.3 3.3 %collective-permute-done.12 = f32[16,4096]{1,0:T(8,128)S(1)} collective-permute-done((f32[16,4096]{1,0:T(8,128)S(1)}, f32[16,4096]{1,0:T(8,128)S(1)}, u32[]{:S(2)}, u32[]{:S(2)}) %collective-permute-start.12) | collective-permute-done | bytes 262176 | tf_op jit(solution)/shard_map/ppermute | solution.py:23
  57.6 3.4 %collective-permute-start.14 = (f32[1,4096]{1,0:T(1,128)S(1)}, f32[1,4096]{1,0:T(1,128)S(1)}, u32[]{:S(2)}, u32[]{:S(2)}) collective-permute-start(f32[1,4096]{1,0:T(1,128)S(1)} %get-tuple-element.118), channel_id=1, source_target_pairs={{0,1},{1,2},{2,3},{3,4},{4,5},{5,6},{6,7},{8,9},{9,10},{10,11},{11... | collective-permute-start | bytes 49160 | tf_op jit(solution)/shard_map/ppermute | solution.py:14
  66.4 3.4 %collective-permute-start.16 = (f32[1,4096]{1,0:T(1,128)S(1)}, f32[1,4096]{1,0:T(1,128)S(1)}, u32[]{:S(2)}, u32[]{:S(2)}) collective-permute-start(f32[1,4096]{1,0:T(1,128)S(1)} %get-tuple-element.116), channel_id=1, source_target_pairs={{0,1},{1,2},{2,3},{3,4},{4,5},{5,6},{6,7},{8,9},{9,10},{10,11},{11... | collective-permute-start | bytes 49160 | tf_op jit(solution)/shard_map/ppermute | solution.py:14
  75.3 3.4 %collective-permute-start.18 = (f32[1,4096]{1,0:T(1,128)S(1)}, f32[1,4096]{1,0:T(1,128)S(1)}, u32[]{:S(2)}, u32[]{:S(2)}) collective-permute-start(f32[1,4096]{1,0:T(1,128)S(1)} %get-tuple-element.114), channel_id=1, source_target_pairs={{0,1},{1,2},{2,3},{3,4},{4,5},{5,6},{6,7},{8,9},{9,10},{10,11},{11... | collective-permute-start | bytes 49160 | tf_op jit(solution)/shard_map/ppermute | solution.py:14
  84.2 3.4 %collective-permute-start.20 = (f32[1,4096]{1,0:T(1,128)S(1)}, f32[1,4096]{1,0:T(1,128)S(1)}, u32[]{:S(2)}, u32[]{:S(2)}) collective-permute-start(f32[1,4096]{1,0:T(1,128)S(1)} %get-tuple-element.112), channel_id=1, source_target_pairs={{0,1},{1,2},{2,3},{3,4},{4,5},{5,6},{6,7},{8,9},{9,10},{10,11},{11... | collective-permute-start | bytes 49160 | tf_op jit(solution)/shard_map/ppermute | solution.py:14
  89.2 44.6 %reshape.31 = f32[2,10,2,2048,2]{4,3,0,2,1:T(8,128)} reshape(f32[2,20,4096]{2,0,1:T(2,128)S(1)} %copy.158) | data formatting | bytes 1310720 | tf_op jit(solution)/shard_map/reshape | solution.py:53
  133.8 16.4 %reduce_sum.18 = f32[2,10,2048]{2,0,1:T(2,128)S(1)} reduce(f32[2,10,2,2048,2]{4,3,0,2,1:T(8,128)} %reshape.31, f32[]{:T(128)} %constant.32.clone.1), dimensions={2,4}, to_apply=%region_0.1 | reduce | flops 122880 | bytes 819204 | tf_op jit(solution)/shard_map/reduce_sum | solution.py:54
  150.6 8.6 %collective-permute-start.21 = (f32[16,4096]{1,0:T(8,128)S(1)}, f32[16,4096]{1,0:T(8,128)S(1)}, u32[]{:S(2)}, u32[]{:S(2)}) collective-permute-start(f32[16,4096]{1,0:T(8,128)S(1)} %fusion.19), channel_id=1, source_target_pairs={{0,8},{8,16},{16,24},{1,9},{9,17},{17,25},{2,10},{10,18},{18,26},{... | collective-permute-start | bytes 786440 | tf_op jit(solution)/shard_map/ppermute | solution.py:23
  162.3 23.7 %reshape.32 = f32[8,2,2048,2]{3,2,1,0:T(8,128)} reshape(f32[16,4096]{1,0:T(8,128)S(1)} %sub.231) | data formatting | bytes 524288 | tf_op jit(solution)/shard_map/reshape | solution.py:53
  186.0 8.0 %reduce_sum.19 = f32[8,2048]{1,0:T(8,128)S(1)} reduce(f32[8,2,2048,2]{3,2,1,0:T(8,128)} %reshape.32, f32[]{:T(128)} %constant.32.clone.1), dimensions={1,3}, to_apply=%region_1.2 | reduce | flops 49152 | bytes 327684 | tf_op jit(solution)/shard_map/reduce_sum | solution.py:54
  194.1 46.7 %while.12 = (s32[]{:T(128)}, f32[8,2048]{1,0:T(8,128)S(1)}, pred[]{:T(512)}, f32[2,10,2048]{2,1,0:T(8,128)S(1)}, f32[8,2048]{1,0:T(8,128)S(1)}, /*index=5*/f32[8,2048]{1,0:T(8,128)S(1)}, s32[]{:T(128)}) while((s32[]{:T(128)}, f32[8,2048]{1,0:T(8,128)S(1)}, pred[]{:T(512)}, f32[2,10,2048]{2,1,0:T(8,128)S(1)}, f32[8,2048]{1,0:T(8,128)S(1)}, ...), condition=%wide.region_3.4_spmd, body=%wide.region_2.3_spmd.sunk | while | flops 262146 | bytes 1097926 | solution.py:85
  194.1 3.6 %collective-permute-start = (f32[1,2048]{1,0:T(1,128)S(1)}, f32[1,2048]{1,0:T(1,128)S(1)}, u32[]{:S(2)}, u32[]{:S(2)}) collective-permute-start(f32[1,2048]{1,0:T(1,128)S(1)} %get-tuple-element.168), channel_id=1, source_target_pairs={{0,1},{1,2},{2,3},{3,4},{4,5},{5,6},{6,7},{8,9},{9,10},{10,11},{11... | collective-permute-start | bytes 24584 | tf_op jit(solution)/shard_map/while/body/eval_jaxpr/ppermute | solution.py:14
  202.5 5.5 %collective-permute-start.2 = (f32[8,2048]{1,0:T(8,128)S(1)}, f32[8,2048]{1,0:T(8,128)S(1)}, u32[]{:S(2)}, u32[]{:S(2)}) collective-permute-start(f32[8,2048]{1,0:T(8,128)S(1)} %fusion.98), channel_id=1, source_target_pairs={{0,8},{8,16},{16,24},{1,9},{9,17},{17,25},{2,10},{10,18},{18,26},{... | collective-permute-start | bytes 196616 | tf_op jit(solution)/shard_map/while/body/eval_jaxpr/ppermute | solution.py:23
  209.4 4.5 %collective-permute-start = (f32[1,2048]{1,0:T(1,128)S(1)}, f32[1,2048]{1,0:T(1,128)S(1)}, u32[]{:S(2)}, u32[]{:S(2)}) collective-permute-start(f32[1,2048]{1,0:T(1,128)S(1)} %get-tuple-element.168), channel_id=1, source_target_pairs={{0,1},{1,2},{2,3},{3,4},{4,5},{5,6},{6,7},{8,9},{9,10},{10,11},{11... | collective-permute-start | bytes 24584 | tf_op jit(solution)/shard_map/while/body/eval_jaxpr/ppermute | solution.py:14
  218.5 5.7 %collective-permute-start.2 = (f32[8,2048]{1,0:T(8,128)S(1)}, f32[8,2048]{1,0:T(8,128)S(1)}, u32[]{:S(2)}, u32[]{:S(2)}) collective-permute-start(f32[8,2048]{1,0:T(8,128)S(1)} %fusion.98), channel_id=1, source_target_pairs={{0,8},{8,16},{16,24},{1,9},{9,17},{17,25},{2,10},{10,18},{18,26},{... | collective-permute-start | bytes 196616 | tf_op jit(solution)/shard_map/while/body/eval_jaxpr/ppermute | solution.py:23
  225.6 3.6 %collective-permute-start = (f32[1,2048]{1,0:T(1,128)S(1)}, f32[1,2048]{1,0:T(1,128)S(1)}, u32[]{:S(2)}, u32[]{:S(2)}) collective-permute-start(f32[1,2048]{1,0:T(1,128)S(1)} %get-tuple-element.168), channel_id=1, source_target_pairs={{0,1},{1,2},{2,3},{3,4},{4,5},{5,6},{6,7},{8,9},{9,10},{10,11},{11... | collective-permute-start | bytes 24584 | tf_op jit(solution)/shard_map/while/body/eval_jaxpr/ppermute | solution.py:14
  234.0 5.4 %collective-permute-start.2 = (f32[8,2048]{1,0:T(8,128)S(1)}, f32[8,2048]{1,0:T(8,128)S(1)}, u32[]{:S(2)}, u32[]{:S(2)}) collective-permute-start(f32[8,2048]{1,0:T(8,128)S(1)} %fusion.98), channel_id=1, source_target_pairs={{0,8},{8,16},{16,24},{1,9},{9,17},{17,25},{2,10},{10,18},{18,26},{... | collective-permute-start | bytes 196616 | tf_op jit(solution)/shard_map/while/body/eval_jaxpr/ppermute | solution.py:23
  (91 shorter events, 68.0 us)
Async XLA Ops:
  0.9 9.5 %collective-permute-start.4 = (f32[2,4096]{1,0:T(2,128)S(1)}, f32[2,4096]{1,0:T(2,128)S(1)}, u32[]{:S(2)}, u32[]{:S(2)}) collective-permute-start(f32[2,4096]{1,0:T(2,128)S(1)} %slice.302), channel_id=1, source_target_pairs={{0,1},{1,2},{2,3},{3,4},{4,5},{5,6},{6,7},{8,9},{9,10},{10,11},{11... | collective-permute-start | bytes 98312 | tf_op jit(solution)/shard_map/ppermute | solution.py:23
  5.1 5.4 %collective-permute-start.3 = (f32[1,4096]{1,0:T(1,128)S(1)}, f32[1,4096]{1,0:T(1,128)S(1)}, u32[]{:S(2)}, u32[]{:S(2)}) collective-permute-start(f32[1,4096]{1,0:T(1,128)S(1)} %get-tuple-element.125), channel_id=1, source_target_pairs={{1,0},{2,1},{3,2},{4,3},{5,4},{6,5},{7,6},{9,8},{10,9},{11,10},{12... | collective-permute-start | bytes 49160 | tf_op jit(solution)/shard_map/ppermute | solution.py:15
  8.1 5.4 %collective-permute-start.5 = (f32[1,4096]{1,0:T(1,128)S(1)}, f32[1,4096]{1,0:T(1,128)S(1)}, u32[]{:S(2)}, u32[]{:S(2)}) collective-permute-start(f32[1,4096]{1,0:T(1,128)S(1)} %get-tuple-element.126), channel_id=1, source_target_pairs={{0,1},{1,2},{2,3},{3,4},{4,5},{5,6},{6,7},{8,9},{9,10},{10,11},{11... | collective-permute-start | bytes 49160 | tf_op jit(solution)/shard_map/ppermute | solution.py:14
  15.9 5.3 %collective-permute-start.6 = (f32[1,4096]{1,0:T(1,128)S(1)}, f32[1,4096]{1,0:T(1,128)S(1)}, u32[]{:S(2)}, u32[]{:S(2)}) collective-permute-start(f32[1,4096]{1,0:T(1,128)S(1)} %get-tuple-element.123), channel_id=1, source_target_pairs={{1,0},{2,1},{3,2},{4,3},{5,4},{6,5},{7,6},{9,8},{10,9},{11,10},{12... | collective-permute-start | bytes 49160 | tf_op jit(solution)/shard_map/ppermute | solution.py:15
  17.8 5.4 %collective-permute-start.7 = (f32[1,4096]{1,0:T(1,128)S(1)}, f32[1,4096]{1,0:T(1,128)S(1)}, u32[]{:S(2)}, u32[]{:S(2)}) collective-permute-start(f32[1,4096]{1,0:T(1,128)S(1)} %get-tuple-element.124), channel_id=1, source_target_pairs={{0,1},{1,2},{2,3},{3,4},{4,5},{5,6},{6,7},{8,9},{9,10},{10,11},{11... | collective-permute-start | bytes 49160 | tf_op jit(solution)/shard_map/ppermute | solution.py:14
  24.8 5.3 %collective-permute-start.8 = (f32[1,4096]{1,0:T(1,128)S(1)}, f32[1,4096]{1,0:T(1,128)S(1)}, u32[]{:S(2)}, u32[]{:S(2)}) collective-permute-start(f32[1,4096]{1,0:T(1,128)S(1)} %get-tuple-element.121), channel_id=1, source_target_pairs={{1,0},{2,1},{3,2},{4,3},{5,4},{6,5},{7,6},{9,8},{10,9},{11,10},{12... | collective-permute-start | bytes 49160 | tf_op jit(solution)/shard_map/ppermute | solution.py:15
  26.7 5.4 %collective-permute-start.9 = (f32[1,4096]{1,0:T(1,128)S(1)}, f32[1,4096]{1,0:T(1,128)S(1)}, u32[]{:S(2)}, u32[]{:S(2)}) collective-permute-start(f32[1,4096]{1,0:T(1,128)S(1)} %get-tuple-element.122), channel_id=1, source_target_pairs={{0,1},{1,2},{2,3},{3,4},{4,5},{5,6},{6,7},{8,9},{9,10},{10,11},{11... | collective-permute-start | bytes 49160 | tf_op jit(solution)/shard_map/ppermute | solution.py:14
  33.6 5.3 %collective-permute-start.10 = (f32[1,4096]{1,0:T(1,128)S(1)}, f32[1,4096]{1,0:T(1,128)S(1)}, u32[]{:S(2)}, u32[]{:S(2)}) collective-permute-start(f32[1,4096]{1,0:T(1,128)S(1)} %get-tuple-element.119), channel_id=1, source_target_pairs={{1,0},{2,1},{3,2},{4,3},{5,4},{6,5},{7,6},{9,8},{10,9},{11,10},{12... | collective-permute-start | bytes 49160 | tf_op jit(solution)/shard_map/ppermute | solution.py:15
  35.6 5.4 %collective-permute-start.11 = (f32[1,4096]{1,0:T(1,128)S(1)}, f32[1,4096]{1,0:T(1,128)S(1)}, u32[]{:S(2)}, u32[]{:S(2)}) collective-permute-start(f32[1,4096]{1,0:T(1,128)S(1)} %get-tuple-element.120), channel_id=1, source_target_pairs={{0,1},{1,2},{2,3},{3,4},{4,5},{5,6},{6,7},{8,9},{9,10},{10,11},{11... | collective-permute-start | bytes 49160 | tf_op jit(solution)/shard_map/ppermute | solution.py:14
  42.5 12.1 %collective-permute-start.12 = (f32[16,4096]{1,0:T(8,128)S(1)}, f32[16,4096]{1,0:T(8,128)S(1)}, u32[]{:S(2)}, u32[]{:S(2)}) collective-permute-start(f32[16,4096]{1,0:T(8,128)S(1)} %fusion.55), channel_id=1, source_target_pairs={{0,8},{8,16},{16,24},{1,9},{9,17},{17,25},{2,10},{10,18},{18,26},{... | collective-permute-start | bytes 786440 | tf_op jit(solution)/shard_map/ppermute | solution.py:23
  55.6 5.3 %collective-permute-start.13 = (f32[1,4096]{1,0:T(1,128)S(1)}, f32[1,4096]{1,0:T(1,128)S(1)}, u32[]{:S(2)}, u32[]{:S(2)}) collective-permute-start(f32[1,4096]{1,0:T(1,128)S(1)} %get-tuple-element.117), channel_id=1, source_target_pairs={{1,0},{2,1},{3,2},{4,3},{5,4},{6,5},{7,6},{9,8},{10,9},{11,10},{12... | collective-permute-start | bytes 49160 | tf_op jit(solution)/shard_map/ppermute | solution.py:15
  57.6 5.4 %collective-permute-start.14 = (f32[1,4096]{1,0:T(1,128)S(1)}, f32[1,4096]{1,0:T(1,128)S(1)}, u32[]{:S(2)}, u32[]{:S(2)}) collective-permute-start(f32[1,4096]{1,0:T(1,128)S(1)} %get-tuple-element.118), channel_id=1, source_target_pairs={{0,1},{1,2},{2,3},{3,4},{4,5},{5,6},{6,7},{8,9},{9,10},{10,11},{11... | collective-permute-start | bytes 49160 | tf_op jit(solution)/shard_map/ppermute | solution.py:14
  66.4 5.4 %collective-permute-start.16 = (f32[1,4096]{1,0:T(1,128)S(1)}, f32[1,4096]{1,0:T(1,128)S(1)}, u32[]{:S(2)}, u32[]{:S(2)}) collective-permute-start(f32[1,4096]{1,0:T(1,128)S(1)} %get-tuple-element.116), channel_id=1, source_target_pairs={{0,1},{1,2},{2,3},{3,4},{4,5},{5,6},{6,7},{8,9},{9,10},{10,11},{11... | collective-permute-start | bytes 49160 | tf_op jit(solution)/shard_map/ppermute | solution.py:14
  73.4 5.4 %collective-permute-start.17 = (f32[1,4096]{1,0:T(1,128)S(1)}, f32[1,4096]{1,0:T(1,128)S(1)}, u32[]{:S(2)}, u32[]{:S(2)}) collective-permute-start(f32[1,4096]{1,0:T(1,128)S(1)} %get-tuple-element.113), channel_id=1, source_target_pairs={{1,0},{2,1},{3,2},{4,3},{5,4},{6,5},{7,6},{9,8},{10,9},{11,10},{12... | collective-permute-start | bytes 49160 | tf_op jit(solution)/shard_map/ppermute | solution.py:15
  75.3 5.4 %collective-permute-start.18 = (f32[1,4096]{1,0:T(1,128)S(1)}, f32[1,4096]{1,0:T(1,128)S(1)}, u32[]{:S(2)}, u32[]{:S(2)}) collective-permute-start(f32[1,4096]{1,0:T(1,128)S(1)} %get-tuple-element.114), channel_id=1, source_target_pairs={{0,1},{1,2},{2,3},{3,4},{4,5},{5,6},{6,7},{8,9},{9,10},{10,11},{11... | collective-permute-start | bytes 49160 | tf_op jit(solution)/shard_map/ppermute | solution.py:14
  82.2 68.0 %collective-permute-start.19 = (f32[1,4096]{1,0:T(1,128)S(1)}, f32[1,4096]{1,0:T(1,128)S(1)}, u32[]{:S(2)}, u32[]{:S(2)}) collective-permute-start(f32[1,4096]{1,0:T(1,128)S(1)} %get-tuple-element.111), channel_id=1, source_target_pairs={{1,0},{2,1},{3,2},{4,3},{5,4},{6,5},{7,6},{9,8},{10,9},{11,10},{12... | collective-permute-start | bytes 49160 | tf_op jit(solution)/shard_map/ppermute | solution.py:15
  84.2 66.1 %collective-permute-start.20 = (f32[1,4096]{1,0:T(1,128)S(1)}, f32[1,4096]{1,0:T(1,128)S(1)}, u32[]{:S(2)}, u32[]{:S(2)}) collective-permute-start(f32[1,4096]{1,0:T(1,128)S(1)} %get-tuple-element.112), channel_id=1, source_target_pairs={{0,1},{1,2},{2,3},{3,4},{4,5},{5,6},{6,7},{8,9},{9,10},{10,11},{11... | collective-permute-start | bytes 49160 | tf_op jit(solution)/shard_map/ppermute | solution.py:14
  150.6 11.7 %collective-permute-start.21 = (f32[16,4096]{1,0:T(8,128)S(1)}, f32[16,4096]{1,0:T(8,128)S(1)}, u32[]{:S(2)}, u32[]{:S(2)}) collective-permute-start(f32[16,4096]{1,0:T(8,128)S(1)} %fusion.19), channel_id=1, source_target_pairs={{0,8},{8,16},{16,24},{1,9},{9,17},{17,25},{2,10},{10,18},{18,26},{... | collective-permute-start | bytes 786440 | tf_op jit(solution)/shard_map/ppermute | solution.py:23
  194.1 6.2 %collective-permute-start = (f32[1,2048]{1,0:T(1,128)S(1)}, f32[1,2048]{1,0:T(1,128)S(1)}, u32[]{:S(2)}, u32[]{:S(2)}) collective-permute-start(f32[1,2048]{1,0:T(1,128)S(1)} %get-tuple-element.168), channel_id=1, source_target_pairs={{0,1},{1,2},{2,3},{3,4},{4,5},{5,6},{6,7},{8,9},{9,10},{10,11},{11... | collective-permute-start | bytes 24584 | tf_op jit(solution)/shard_map/while/body/eval_jaxpr/ppermute | solution.py:14
  202.5 6.9 %collective-permute-start.2 = (f32[8,2048]{1,0:T(8,128)S(1)}, f32[8,2048]{1,0:T(8,128)S(1)}, u32[]{:S(2)}, u32[]{:S(2)}) collective-permute-start(f32[8,2048]{1,0:T(8,128)S(1)} %fusion.98), channel_id=1, source_target_pairs={{0,8},{8,16},{16,24},{1,9},{9,17},{17,25},{2,10},{10,18},{18,26},{... | collective-permute-start | bytes 196616 | tf_op jit(solution)/shard_map/while/body/eval_jaxpr/ppermute | solution.py:23
  209.4 6.5 %collective-permute-start = (f32[1,2048]{1,0:T(1,128)S(1)}, f32[1,2048]{1,0:T(1,128)S(1)}, u32[]{:S(2)}, u32[]{:S(2)}) collective-permute-start(f32[1,2048]{1,0:T(1,128)S(1)} %get-tuple-element.168), channel_id=1, source_target_pairs={{0,1},{1,2},{2,3},{3,4},{4,5},{5,6},{6,7},{8,9},{9,10},{10,11},{11... | collective-permute-start | bytes 24584 | tf_op jit(solution)/shard_map/while/body/eval_jaxpr/ppermute | solution.py:14
  218.5 7.0 %collective-permute-start.2 = (f32[8,2048]{1,0:T(8,128)S(1)}, f32[8,2048]{1,0:T(8,128)S(1)}, u32[]{:S(2)}, u32[]{:S(2)}) collective-permute-start(f32[8,2048]{1,0:T(8,128)S(1)} %fusion.98), channel_id=1, source_target_pairs={{0,8},{8,16},{16,24},{1,9},{9,17},{17,25},{2,10},{10,18},{18,26},{... | collective-permute-start | bytes 196616 | tf_op jit(solution)/shard_map/while/body/eval_jaxpr/ppermute | solution.py:23
  225.6 6.2 %collective-permute-start = (f32[1,2048]{1,0:T(1,128)S(1)}, f32[1,2048]{1,0:T(1,128)S(1)}, u32[]{:S(2)}, u32[]{:S(2)}) collective-permute-start(f32[1,2048]{1,0:T(1,128)S(1)} %get-tuple-element.168), channel_id=1, source_target_pairs={{0,1},{1,2},{2,3},{3,4},{4,5},{5,6},{6,7},{8,9},{9,10},{10,11},{11... | collective-permute-start | bytes 24584 | tf_op jit(solution)/shard_map/while/body/eval_jaxpr/ppermute | solution.py:14
  234.0 6.7 %collective-permute-start.2 = (f32[8,2048]{1,0:T(8,128)S(1)}, f32[8,2048]{1,0:T(8,128)S(1)}, u32[]{:S(2)}, u32[]{:S(2)}) collective-permute-start(f32[8,2048]{1,0:T(8,128)S(1)} %fusion.98), channel_id=1, source_target_pairs={{0,8},{8,16},{16,24},{1,9},{9,17},{17,25},{2,10},{10,18},{18,26},{... | collective-permute-start | bytes 196616 | tf_op jit(solution)/shard_map/while/body/eval_jaxpr/ppermute | solution.py:23
  (8 other events, 100.2 us)
where the time goes:
time: 247 us; the launch traced here: 243 us
  starting transfers between devices  98.3 us (40%)
  local copies, waits for them, and re-layouts  73 us (30%)
  other arithmetic  39.6 us (16%)
  waiting for transfers between devices  31.8 us (13%)
    reshape x2, local copies, waits for them, and re-layouts, restrict(): field.reshape(lead + (field.shape[-2] // 2, 2, field.shape[-1] // 2, 2))  68.3 us
    ppermute x11, starting transfers between devices, padded(): before = lax.ppermute(last, axis, up)  37.6 us
    ppermute x6, starting transfers between devices, from_behind(): lax.ppermute(value, axis, [(source, source + steps) for source in range(l...  37.2 us
    reduce_sum x2, other arithmetic, restrict(): return jnp.mean(shaped, axis=(-3, -1))  24.4 us
    ppermute x11, starting transfers between devices, padded(): after = lax.ppermute(leading, axis, down)  23.5 us
    ppermute x11, waiting for transfers between devices, padded(): before = lax.ppermute(last, axis, up)  15 us
    add x8, other arithmetic, propagate(): field = interior(extended, cond_rows, cond_cols) + source_rows  11.7 us
    ppermute x6, waiting for transfers between devices, from_behind(): lax.ppermute(value, axis, [(source, source + steps) for source in range(l...  10.1 us
  transfers between devices with their start and end apart: 28, of which 15 were waited for; matrix products, arithmetic and copies ran while one was open for 26% of the time, Pallas kernels for 0%

commit v1 on v0

--- a/solution.py
+++ b/solution.py
@@ -1,7 +1,16 @@
+import functools
+
 import jax
 import jax.numpy as jnp
 from jax import lax
+from jax.experimental import pallas as pl
+from jax.experimental.pallas import tpu as pltpu
 from jax.sharding import PartitionSpec as P
+
+FINE_STEPS = 4
+HALO = 12
+LANE = 128
+VMEM_LIMIT = 40 * 1024 * 1024
 
 
 def padded(value, sides, width):
@@ -42,7 +51,7 @@
     cond_rows = coef_pad[0, 3 : strip_rows + 5]
     cond_cols = coef_pad[1, 3 : strip_rows + 5]
     source_rows = coef_pad[2, 4 : strip_rows + 4]
-    for section in range(4):
+    for section in range(FINE_STEPS):
         extended = padded(field, (("space", 0),), 1)
         field = interior(extended, cond_rows, cond_cols) + source_rows
     return field
@@ -54,7 +63,7 @@
     return jnp.mean(shaped, axis=(-3, -1))
 
 
-def shards(guesses, cond_x, cond_y, source, inflow):
+def general_shards(guesses, cond_x, cond_y, source, inflow):
     strip_rows = cond_x.shape[0]
     columns = cond_x.shape[1]
     stacked = jnp.stack([cond_x, cond_y, source])
@@ -87,6 +96,261 @@
     return (relaxed + widened)[None]
 
 
+def window_start(index, own, columns, lanes):
+    return jnp.clip(own * index - LANE, 0, columns - lanes)
+
+
+def pack_kernel(ids, guess, cond_x, cond_y, source, inflow, send, halo_a, halo_b, coefs, inflow_win, wide):
+    blocks, rows, lanes = send.shape
+    columns = guess.shape[1]
+    own = columns // blocks
+    for block in range(blocks):
+        start = min(max(own * block - LANE, 0), columns - lanes)
+        send[block] = guess[:, start : start + lanes]
+    half = lax.broadcasted_iota(jnp.int32, (rows // 2, LANE), 1) // 2
+    for part in range(columns // (2 * LANE)):
+        piece = inflow[:, part * LANE : (part + 1) * LANE]
+        for side in range(2):
+            at = (2 * part + side) * LANE
+            wide[:, at : at + LANE] = jnp.take_along_axis(piece, half + side * (LANE // 2), axis=1)
+    window = pl.ds(pl.multiple_of(ids[0], LANE), lanes)
+    for slot, ref in enumerate((cond_x, cond_y, source)):
+        coefs[slot] = ref[:, window]
+    inflow_win[...] = wide[:, window]
+
+    def fill(bottom, top):
+        for slot in range(3):
+            bottom[slot * HALO : (slot + 1) * HALO] = coefs[slot, rows - HALO :]
+            top[slot * HALO : (slot + 1) * HALO] = coefs[slot, :HALO]
+        bottom[3 * HALO :] = inflow_win[rows // 2 - 4 :]
+        top[3 * HALO :] = inflow_win[:4]
+
+    @pl.when(ids[2] == 1)
+    def _():
+        fill(halo_a, halo_b)
+
+    @pl.when(ids[2] == 0)
+    def _():
+        fill(halo_b, halo_a)
+
+
+FIELD_ROWS = (12, 8, 4)
+
+
+def edge_kernel(ids, fields, edge_a, edge_b):
+    rows = fields.shape[1]
+
+    def fill(bottom, top):
+        at = 0
+        for group, deep in enumerate(FIELD_ROWS):
+            bottom[at : at + deep] = fields[group, rows - deep :]
+            top[at : at + deep] = fields[group, :deep]
+            at += deep
+
+    @pl.when(ids[2] == 1)
+    def _():
+        fill(edge_a, edge_b)
+
+    @pl.when(ids[2] == 0)
+    def _():
+        fill(edge_b, edge_a)
+
+
+def spread(value):
+    rows, lanes = value.shape
+    row_even = lax.broadcasted_iota(jnp.int32, value.shape, 0) % 2 == 0
+    lane_even = lax.broadcasted_iota(jnp.int32, value.shape, 1) % 2 == 0
+    value = value + jnp.where(row_even, pltpu.roll(value, rows - 1, 0), pltpu.roll(value, 1, 0))
+    value = value + jnp.where(lane_even, pltpu.roll(value, lanes - 1, 1), pltpu.roll(value, 1, 1))
+    return value * 0.25
+
+
+def sweep(get, cond_x, cond_y, put, first, last, chunks, width, limit):
+    count = last - first
+    lane = lax.broadcasted_iota(jnp.int32, (count, LANE), 1)
+    row = lax.broadcasted_iota(jnp.int32, (count, LANE), 0) + first
+    inside = row < limit
+
+    def load(chunk):
+        value = get(chunk)
+        return value, pltpu.roll(value, LANE - width, 1)
+
+    value, east = load(0)
+    west_flux = jnp.zeros((count, LANE), jnp.float32)
+    for chunk in range(chunks):
+        at = slice(chunk * LANE, (chunk + 1) * LANE)
+        if chunk + 1 < chunks:
+            next_value, next_east = load(chunk + 1)
+        else:
+            next_value, next_east = None, jnp.zeros((count, LANE), jnp.float32)
+        beside = jnp.where(lane >= LANE - width, next_east, east)
+        flux_y = cond_y[first:last, at] * (beside - value)
+        rolled = pltpu.roll(flux_y, width, 1)
+        flux_w = jnp.where(lane < width, west_flux, rolled)
+        below = pltpu.roll(value, count - width, 0)
+        flux_x = cond_x[first:last, at] * (below - value)
+        above = pltpu.roll(flux_x, width, 0)
+        result = value + ((flux_x - above) + (flux_y - flux_w))
+        put(chunk, at, result, inside)
+        value, east, west_flux = next_value, next_east, rolled
+
+
+def main_kernel(
+    ids, fields, coefs, inflow_win, coef_a, coef_b, edge_a, edge_b, out,
+    cond_x, cond_y, source, coarse_x, coarse_y, guess, work, first_pass, second_pass, error,
+):
+    groups, rows, lanes = fields.shape
+    own = out.shape[2]
+    high = rows + 2 * HALO
+    chunks = lanes // LANE
+    limit = jnp.where(ids[3] == 1, HALO + rows, high)
+    twice = lax.broadcasted_iota(jnp.int32, (8, LANE), 0) // 2
+
+    def assemble(upper_c, lower_c, upper_f, lower_f):
+        for slot, ref in enumerate((cond_x, cond_y, source)):
+            ref[:HALO] = upper_c[slot * HALO : (slot + 1) * HALO]
+            ref[HALO + rows :] = lower_c[slot * HALO : (slot + 1) * HALO]
+        at = 0
+        for group, deep in enumerate(FIELD_ROWS):
+            if deep < HALO:
+                blank = jnp.zeros((HALO - deep, lanes), jnp.float32)
+                guess[group, : HALO - deep] = blank
+                guess[group, HALO + rows + deep :] = blank
+            guess[group, HALO - deep : HALO] = upper_f[at : at + deep]
+            guess[group, HALO + rows : HALO + rows + deep] = lower_f[at : at + deep]
+            at += deep
+        blank = jnp.zeros((HALO - 8, lanes), jnp.float32)
+        error[0, : HALO - 8] = blank
+        error[0, HALO + rows + 8 :] = blank
+        for chunk in range(chunks):
+            at = slice(chunk * LANE, (chunk + 1) * LANE)
+            both = jnp.concatenate([upper_c[3 * HALO :, at], lower_c[3 * HALO :, at]], axis=0)
+            error[0, HALO - 8 : HALO, at] = jnp.take_along_axis(both, twice, axis=0)
+            error[0, HALO + rows : HALO + rows + 8, at] = jnp.take_along_axis(both, twice + 4, axis=0)
+
+    @pl.when(ids[2] == 1)
+    def _():
+        assemble(coef_b, coef_a, edge_b, edge_a)
+
+    @pl.when(ids[2] == 0)
+    def _():
+        assemble(coef_a, coef_b, edge_a, edge_b)
+
+    own_rows = slice(HALO, HALO + rows)
+    for slot, ref in enumerate((cond_x, cond_y, source)):
+        ref[own_rows] = coefs[slot]
+    for group in range(groups - 1):
+        guess[group, own_rows] = fields[group]
+    for chunk in range(chunks):
+        at = slice(chunk * LANE, (chunk + 1) * LANE)
+        for side in range(2):
+            top = HALO + 8 * side
+            error[0, top : top + 8, at] = jnp.take_along_axis(inflow_win[:, at], twice + 4 * side, axis=0)
+        coarse_x[:, at] = spread(cond_x[:, at])
+        coarse_y[:, at] = spread(cond_y[:, at])
+
+    def step(from_ref, to_ref, first, last):
+        def put(chunk, at, result, inside):
+            result = result + source[first:last, at]
+            to_ref[first:last, at] = jnp.where(inside, result, 0.0)
+
+        def get(chunk):
+            return from_ref[first:last, chunk * LANE : (chunk + 1) * LANE]
+
+        sweep(get, cond_x, cond_y, put, first, last, chunks, 1, limit)
+
+    def propagated(start, end, first, last):
+        step(start, work.at[0], first, last)
+        step(work.at[0], work.at[1], first, last)
+        step(work.at[1], work.at[0], first, last)
+        step(work.at[0], end, first, last)
+
+    near, far = HALO - 4, HALO + rows + 4
+    propagated(guess.at[0], first_pass.at[0], 0, high)
+    propagated(guess.at[1], first_pass.at[1], 0, high)
+    propagated(guess.at[2], first_pass.at[2], near, far)
+    propagated(first_pass.at[0], second_pass.at[0], 0, high)
+    propagated(first_pass.at[1], second_pass.at[1], near, far)
+
+    ends = (first_pass.at[0], second_pass.at[0], second_pass.at[1])
+    for group in range(1, groups):
+        first, last = (0, high) if group < groups - 1 else (near, far)
+        before = error.at[group - 1]
+
+        def put(chunk, at, result, inside):
+            residual = spread(ends[group - 1][first:last, at] - first_pass[group - 1, first:last, at])
+            error[group, first:last, at] = jnp.where(inside, result + residual, 0.0)
+
+        def get(chunk):
+            return before[first:last, chunk * LANE : (chunk + 1) * LANE]
+
+        sweep(get, coarse_x, coarse_y, put, first, last, chunks, 2, limit)
+
+    window = pl.ds(pl.multiple_of(ids[1], LANE), own)
+    for group in range(groups):
+        relaxed = guess.at[0] if group == 0 else first_pass.at[group - 1]
+        out[group] = relaxed[own_rows, window] + error[group, own_rows, window]
+
+
+def unpack_kernel(blocks, out):
+    own = blocks.shape[2]
+    for block in range(blocks.shape[0]):
+        out[0, :, block * own : (block + 1) * own] = blocks[block]
+
+
+def call(kernel, outs, scratch, *operands):
+    vmem = pl.BlockSpec(memory_space=pltpu.VMEM)
+    smem = pl.BlockSpec(memory_space=pltpu.SMEM)
+    return pl.pallas_call(
+        kernel,
+        out_shape=[jax.ShapeDtypeStruct(shape, jnp.float32) for shape in outs],
+        in_specs=[smem if value.dtype == jnp.int32 else vmem for value in operands],
+        out_specs=[vmem] * len(outs),
+        scratch_shapes=[pltpu.VMEM(shape, jnp.float32) for shape in scratch],
+        compiler_params=pltpu.CompilerParams(vmem_limit_bytes=VMEM_LIMIT),
+    )(*operands)
+
+
+def shards(guesses, cond_x, cond_y, source, inflow):
+    groups, strips = lax.axis_size("tm"), lax.axis_size("space")
+    rows, columns = cond_x.shape
+    fits = groups == len(FIELD_ROWS) + 1 and strips % 2 == 0 and rows == 16
+    if not fits or columns % (groups * LANE) != 0 or columns < (groups + 2) * LANE:
+        return general_shards(guesses, cond_x, cond_y, source, inflow)
+    own = columns // groups
+    lanes = own + 2 * LANE
+    high = rows + 2 * HALO
+    member, strip = lax.axis_index("tm"), lax.axis_index("space")
+    start = window_start(member, own, columns, lanes)
+    ids = jnp.stack([start, own * member - start, 1 - strip % 2, (strip == strips - 1).astype(jnp.int32)])
+    ids = ids.astype(jnp.int32)
+    pairs_a = [(i, i ^ 1) for i in range(strips)]
+    pairs_b = [(i, j) for k in range(1, strips - 1, 2) for i, j in ((k, k + 1), (k + 1, k))]
+
+    send, halo_a, halo_b, coefs, inflow_win = call(
+        pack_kernel,
+        [(groups, rows, lanes), (3 * HALO + 4, lanes), (3 * HALO + 4, lanes), (3, rows, lanes), (rows // 2, lanes)],
+        [(rows // 2, columns)],
+        ids, guesses[0], cond_x, cond_y, source, inflow,
+    )
+    coef_b = lax.ppermute(halo_b, "space", pairs_b)
+    coef_a = lax.ppermute(halo_a, "space", pairs_a)
+    fields = lax.all_to_all(send, "tm", 0, 0, tiled=True)
+    deep = sum(FIELD_ROWS)
+    sent_a, sent_b = call(edge_kernel, [(deep, lanes)] * 2, [], ids, fields)
+    edge_b = lax.ppermute(sent_b, "space", pairs_b)
+    edge_a = lax.ppermute(sent_a, "space", pairs_a)
+    (blocks,) = call(
+        main_kernel,
+        [(groups, rows, own)],
+        [(high, lanes)] * 5
+        + [(groups - 1, high, lanes), (2, high, lanes), (groups - 1, high, lanes), (groups - 2, high, lanes), (groups, high, lanes)],
+        ids, fields, coefs, inflow_win, coef_a, coef_b, edge_a, edge_b,
+    )
+    blocks = lax.all_to_all(blocks, "tm", 0, 0, tiled=True)
+    return call(unpack_kernel, [(1, rows, columns)], [], blocks)[0]
+
+
 def solution(mesh):
     return jax.shard_map(
         shards,

time: 247 us -> 53.7 us (0.22)
  the two profiles are of different devices: /device:TPU:9 before, /device:TPU:0 now
where the time goes in v1:
time: 53.7 us; the launch traced here: 53.3 us
  Pallas kernels  19.3 us (36%)
  waiting for transfers between devices  10.4 us (19%)
  starting transfers between devices  10.1 us (19%)
  blocking collectives  8.75 us (16%)
  local copies, waits for them, and re-layouts  4.64 us (9%)
    pallas_call x4, Pallas kernels, call(): pl.pallas_call(kernel, out_shape=[jax.ShapeDtypeStruct(shape, jnp.float32...  19.3 us
    all_to_all x1, blocking collectives, shards(): blocks = lax.all_to_all(blocks, 'tm', 0, 0, tiled=True)  8.75 us
    ppermute x1, waiting for transfers between devices, shards(): edge_a = lax.ppermute(sent_a, 'space', pairs_a)  4.79 us
    unnamed x10, local copies, waits for them, and re-layouts  4.64 us
    all_to_all x1, starting transfers between devices, shards(): fields = lax.all_to_all(send, 'tm', 0, 0, tiled=True)  4.21 us
    all_to_all x1, waiting for transfers between devices, shards(): fields = lax.all_to_all(send, 'tm', 0, 0, tiled=True)  3.77 us
    ppermute x1, starting transfers between devices, shards(): coef_a = lax.ppermute(halo_a, 'space', pairs_a)  2.3 us
    ppermute x1, starting transfers between devices, shards(): edge_a = lax.ppermute(sent_a, 'space', pairs_a)  2.27 us
  transfers between devices with their start and end apart: 5, of which 3 were waited for; matrix products, arithmetic and copies ran while one was open for 0% of the time, Pallas kernels for 1%

profile of v1, /device:TPU:0, one launch (start us, length us, event | category | flops | bytes accessed | tf_op | source)
XLA Modules:
  0.0 53.3 jit_solution(13251025217783363323)
XLA Ops:
  0.0 0.1 pad_add_fusion.ids
  0.1 0.0 copy-start
  0.1 0.9 %copy-done = f32[1,16,4096]{2,1,0:T(8,128)S(1)} copy-done((f32[1,16,4096]{2,1,0:T(8,128)S(1)}, f32[1,16,4096]{2,1,0:T(8,128)}, u32[]{:S(2)}) %copy-start) | copy-done | bytes 262168
  1.0 0.0 copy-start.1
  1.0 0.9 %copy-done.1 = f32[16,4096]{1,0:T(8,128)S(1)} copy-done((f32[16,4096]{1,0:T(8,128)S(1)}, f32[16,4096]{1,0:T(8,128)}, u32[]{:S(2)}) %copy-start.1) | copy-done | bytes 262168
  2.0 0.0 copy-start.2
  2.0 0.9 %copy-done.2 = f32[16,4096]{1,0:T(8,128)S(1)} copy-done((f32[16,4096]{1,0:T(8,128)S(1)}, f32[16,4096]{1,0:T(8,128)}, u32[]{:S(2)}) %copy-start.2) | copy-done | bytes 262168
  2.9 0.9 %copy-done.3 = f32[16,4096]{1,0:T(8,128)S(1)} copy-done((f32[16,4096]{1,0:T(8,128)S(1)}, f32[16,4096]{1,0:T(8,128)}, u32[]{:S(2)}) %copy-start.3) | copy-done | bytes 262168
  3.9 0.8 %copy-done.4 = f32[8,2048]{1,0:T(8,128)S(1)} copy-done((f32[8,2048]{1,0:T(8,128)S(1)}, f32[8,2048]{1,0:T(8,128)}, u32[]{:S(2)}) %copy-start.4) | copy-done | bytes 65560
  4.7 1.4 %shard_map.55 = (f32[4,16,1280]{2,1,0:T(8,128)}, f32[40,1280]{1,0:T(8,128)S(1)}, f32[40,1280]{1,0:T(8,128)S(1)}, f32[3,16,1280]{2,1,0:T(8,128)S(1)}, f32[8,1280]{1,0:T(8,128)S(1)}) custom-call(s32[4]{0:T(128)S(1)} %pad_add_fusion.ids, f32[16,4096]{1,0:T(8,128)S(1)} %bitcast.5, f32[16,4096]{1,0:T(8,128)S(1)} %copy-done.1, f32[16,4096]{1,0:T(8,128)S(1)} %copy-done.2, ...), custom_call_target="tpu_custom_call" | custom-call | tf_op jit(solution)/shard_map/pallas_call | solution.py:304
  6.1 4.2 %all-to-all-start = ((f32[4,16,1280]{2,1,0:T(8,128)}), f32[4,16,1280]{2,1,0:T(8,128)S(1)}, u32[]{:S(2)}, u32[]{:S(2)}) async-start(f32[4,16,1280]{2,1,0:T(8,128)} %get-tuple-element.12), calls=%async_computation | async-start | bytes 655360 | tf_op jit(solution)/shard_map/all_to_all | solution.py:338
  10.3 2.3 %collective-permute-start = (f32[40,1280]{1,0:T(8,128)S(1)}, f32[40,1280]{1,0:T(8,128)S(1)}, u32[]{:S(2)}, u32[]{:S(2)}) collective-permute-start(f32[40,1280]{1,0:T(8,128)S(1)} %get-tuple-element.15), channel_id=1, source_target_pairs={{0,1},{1,0},{2,3},{3,2},{4,5},{5,4},{6,7},{7,6},{8,9},{9,8},{10,11... | collective-permute-start | bytes 614408 | tf_op jit(solution)/shard_map/ppermute | solution.py:337
  12.6 0.7 %collective-permute-start.1 = (f32[40,1280]{1,0:T(8,128)S(1)}, f32[40,1280]{1,0:T(8,128)S(1)}, u32[]{:S(2)}, u32[]{:S(2)}) collective-permute-start(f32[40,1280]{1,0:T(8,128)S(1)} %get-tuple-element.16), channel_id=1, source_target_pairs={{1,2},{2,1},{3,4},{4,3},{5,6},{6,5},{9,10},{10,9},{11,12},{12,11},... | collective-permute-start | bytes 614408 | tf_op jit(solution)/shard_map/ppermute | solution.py:336
  13.3 3.8 %all-to-all-done.fields = f32[4,16,1280]{2,1,0:T(8,128)S(1)} async-done(((f32[4,16,1280]{2,1,0:T(8,128)}), f32[4,16,1280]{2,1,0:T(8,128)S(1)}, u32[]{:S(2)}, u32[]{:S(2)}) %all-to-all-start) | async-done | bytes 327712 | tf_op jit(solution)/shard_map/all_to_all | solution.py:338
  17.1 0.6 %shard_map.56 = (f32[24,1280]{1,0:T(8,128)S(1)}, f32[24,1280]{1,0:T(8,128)S(1)}) custom-call(s32[4]{0:T(128)S(1)} %pad_add_fusion.ids, f32[4,16,1280]{2,1,0:T(8,128)S(1)} %all-to-all-done.fields), custom_call_target="tpu_custom_call" | custom-call | tf_op jit(solution)/shard_map/pallas_call | solution.py:304
  17.7 2.3 %collective-permute-start.2 = (f32[24,1280]{1,0:T(8,128)S(1)}, f32[24,1280]{1,0:T(8,128)S(1)}, u32[]{:S(2)}, u32[]{:S(2)}) collective-permute-start(f32[24,1280]{1,0:T(8,128)S(1)} %get-tuple-element.17), channel_id=1, source_target_pairs={{0,1},{1,0},{2,3},{3,2},{4,5},{5,4},{6,7},{7,6},{8,9},{9,8},{10,11... | collective-permute-start | bytes 368648 | tf_op jit(solution)/shard_map/ppermute | solution.py:342
  19.9 0.7 %collective-permute-start.3 = (f32[24,1280]{1,0:T(8,128)S(1)}, f32[24,1280]{1,0:T(8,128)S(1)}, u32[]{:S(2)}, u32[]{:S(2)}) collective-permute-start(f32[24,1280]{1,0:T(8,128)S(1)} %get-tuple-element.18), channel_id=1, source_target_pairs={{1,2},{2,1},{3,4},{4,3},{5,6},{6,5},{9,10},{10,9},{11,12},{12,11},... | collective-permute-start | bytes 368648 | tf_op jit(solution)/shard_map/ppermute | solution.py:341
  20.6 1.8 %collective-permute-done.coef_a = f32[40,1280]{1,0:T(8,128)S(1)} collective-permute-done((f32[40,1280]{1,0:T(8,128)S(1)}, f32[40,1280]{1,0:T(8,128)S(1)}, u32[]{:S(2)}, u32[]{:S(2)}) %collective-permute-start) | collective-permute-done | bytes 204832 | tf_op jit(solution)/shard_map/ppermute | solution.py:337
  22.4 0.0 collective-permute-done.1.coef_b
  22.4 4.8 %collective-permute-done.2.edge_a = f32[24,1280]{1,0:T(8,128)S(1)} collective-permute-done((f32[24,1280]{1,0:T(8,128)S(1)}, f32[24,1280]{1,0:T(8,128)S(1)}, u32[]{:S(2)}, u32[]{:S(2)}) %collective-permute-start.2) | collective-permute-done | bytes 122912 | tf_op jit(solution)/shard_map/ppermute | solution.py:342
  27.2 0.0 collective-permute-done.3.edge_b
  27.2 16.5 %shard_map.57 = f32[4,16,1024]{2,1,0:T(8,128)S(1)} custom-call(s32[4]{0:T(128)S(1)} %pad_add_fusion.ids, f32[4,16,1280]{2,1,0:T(8,128)S(1)} %all-to-all-done.fields, f32[3,16,1280]{2,1,0:T(8,128)S(1)} %get-tuple-element.13.coefs, f32[8,1280]{1,0:T(8,128)S(1)} %get-tuple-element.14.inflow_win, f32[40,1280]{1,0:T(8,128)S(1)} %collective-permute-done.coef_a, ...), custom_call_target="tpu_custom_call" | custom-call | tf_op jit(solution)/shard_map/pallas_call | solution.py:304
  43.8 8.8 %all_to_all.10.blocks = f32[4,16,1024]{2,1,0:T(8,128)S(1)} all-to-all(f32[4,16,1024]{2,1,0:T(8,128)S(1)} %shard_map.57), channel_id=1, replica_groups=mesh['tm'=4,'space'=8] {'tm'}, dimensions={0} | all-to-all | bytes 524288 | tf_op jit(solution)/shard_map/all_to_all | solution.py:350
  52.5 0.7 %shard_map.58 = f32[1,16,4096]{2,1,0:T(8,128)} custom-call(f32[4,16,1024]{2,1,0:T(8,128)S(1)} %all_to_all.10.blocks), custom_call_target="tpu_custom_call" | custom-call | tf_op jit(solution)/shard_map/pallas_call | solution.py:304
  (2 shorter events, 0.0 us)
Async XLA Ops:
  0.1 1.0 %copy-start = (f32[1,16,4096]{2,1,0:T(8,128)S(1)}, f32[1,16,4096]{2,1,0:T(8,128)}, u32[]{:S(2)}) copy-start(f32[1,16,4096]{2,1,0:T(8,128)} %param.5) | copy-start | bytes 786436
  1.0 0.9 %copy-start.1 = (f32[16,4096]{1,0:T(8,128)S(1)}, f32[16,4096]{1,0:T(8,128)}, u32[]{:S(2)}) copy-start(f32[16,4096]{1,0:T(8,128)} %cond_x.1) | copy-start | bytes 786436
  2.0 0.9 %copy-start.2 = (f32[16,4096]{1,0:T(8,128)S(1)}, f32[16,4096]{1,0:T(8,128)}, u32[]{:S(2)}) copy-start(f32[16,4096]{1,0:T(8,128)} %cond_y.1) | copy-start | bytes 786436
  2.9 0.9 %copy-start.3 = (f32[16,4096]{1,0:T(8,128)S(1)}, f32[16,4096]{1,0:T(8,128)}, u32[]{:S(2)}) copy-start(f32[16,4096]{1,0:T(8,128)} %source.1) | copy-start | bytes 786436
  3.9 0.8 %copy-start.4 = (f32[8,2048]{1,0:T(8,128)S(1)}, f32[8,2048]{1,0:T(8,128)}, u32[]{:S(2)}) copy-start(f32[8,2048]{1,0:T(8,128)} %inflow.1) | copy-start | bytes 196612
  6.1 10.9 %all-to-all-start = ((f32[4,16,1280]{2,1,0:T(8,128)}), f32[4,16,1280]{2,1,0:T(8,128)S(1)}, u32[]{:S(2)}, u32[]{:S(2)}) async-start(f32[4,16,1280]{2,1,0:T(8,128)} %get-tuple-element.12), calls=%async_computation | async-start | bytes 655360 | tf_op jit(solution)/shard_map/all_to_all | solution.py:338
  10.3 12.1 %collective-permute-start = (f32[40,1280]{1,0:T(8,128)S(1)}, f32[40,1280]{1,0:T(8,128)S(1)}, u32[]{:S(2)}, u32[]{:S(2)}) collective-permute-start(f32[40,1280]{1,0:T(8,128)S(1)} %get-tuple-element.15), channel_id=1, source_target_pairs={{0,1},{1,0},{2,3},{3,2},{4,5},{5,4},{6,7},{7,6},{8,9},{9,8},{10,11... | collective-permute-start | bytes 614408 | tf_op jit(solution)/shard_map/ppermute | solution.py:337
  12.6 9.8 %collective-permute-start.1 = (f32[40,1280]{1,0:T(8,128)S(1)}, f32[40,1280]{1,0:T(8,128)S(1)}, u32[]{:S(2)}, u32[]{:S(2)}) collective-permute-start(f32[40,1280]{1,0:T(8,128)S(1)} %get-tuple-element.16), channel_id=1, source_target_pairs={{1,2},{2,1},{3,4},{4,3},{5,6},{6,5},{9,10},{10,9},{11,12},{12,11},... | collective-permute-start | bytes 614408 | tf_op jit(solution)/shard_map/ppermute | solution.py:336
  17.7 9.6 %collective-permute-start.2 = (f32[24,1280]{1,0:T(8,128)S(1)}, f32[24,1280]{1,0:T(8,128)S(1)}, u32[]{:S(2)}, u32[]{:S(2)}) collective-permute-start(f32[24,1280]{1,0:T(8,128)S(1)} %get-tuple-element.17), channel_id=1, source_target_pairs={{0,1},{1,0},{2,3},{3,2},{4,5},{5,4},{6,7},{7,6},{8,9},{9,8},{10,11... | collective-permute-start | bytes 368648 | tf_op jit(solution)/shard_map/ppermute | solution.py:342
  19.9 7.3 %collective-permute-start.3 = (f32[24,1280]{1,0:T(8,128)S(1)}, f32[24,1280]{1,0:T(8,128)S(1)}, u32[]{:S(2)}, u32[]{:S(2)}) collective-permute-start(f32[24,1280]{1,0:T(8,128)S(1)} %get-tuple-element.18), channel_id=1, source_target_pairs={{1,2},{2,1},{3,4},{4,3},{5,6},{6,5},{9,10},{10,9},{11,12},{12,11},... | collective-permute-start | bytes 368648 | tf_op jit(solution)/shard_map/ppermute | solution.py:341

commit v2 on v0

--- a/solution.py
+++ b/solution.py
@@ -1,7 +1,20 @@
+import functools
+
 import jax
 import jax.numpy as jnp
 from jax import lax
+from jax.experimental import pallas as pl
+from jax.experimental.pallas import tpu as pltpu
 from jax.sharding import PartitionSpec as P
+
+FINE_STEPS = 4
+LANE = 128
+SIDE = 64
+HALO = 16
+COEF_ROWS = (10, 9, 9)
+FIELD_ROWS = (12, 8, 4)
+COARSE_ROWS = 4
+VMEM_LIMIT = 40 * 1024 * 1024
 
 
 def padded(value, sides, width):
@@ -42,7 +55,7 @@
     cond_rows = coef_pad[0, 3 : strip_rows + 5]
     cond_cols = coef_pad[1, 3 : strip_rows + 5]
     source_rows = coef_pad[2, 4 : strip_rows + 4]
-    for section in range(4):
+    for section in range(FINE_STEPS):
         extended = padded(field, (("space", 0),), 1)
         field = interior(extended, cond_rows, cond_cols) + source_rows
     return field
@@ -54,7 +67,7 @@
     return jnp.mean(shaped, axis=(-3, -1))
 
 
-def shards(guesses, cond_x, cond_y, source, inflow):
+def general_shards(guesses, cond_x, cond_y, source, inflow):
     strip_rows = cond_x.shape[0]
     columns = cond_x.shape[1]
     stacked = jnp.stack([cond_x, cond_y, source])
@@ -87,6 +100,325 @@
     return (relaxed + widened)[None]
 
 
+def window(index, own, columns, lanes):
+    return jnp.clip(own * index - SIDE, 0, columns - lanes), jnp.clip(own * index - LANE, 0, columns - lanes - LANE)
+
+
+def shifted(load, chunk, shift):
+    amount = lax.rem(2 * LANE - shift, LANE)
+    here = pltpu.roll(load(chunk), amount, 1)
+    there = pltpu.roll(load(chunk + 1), amount, 1)
+    lane = lax.broadcasted_iota(jnp.int32, here.shape, 1)
+    return jnp.where(lane < LANE - shift, here, there)
+
+
+def piece(chunk):
+    return slice(chunk * LANE, (chunk + 1) * LANE)
+
+
+def pack_kernel(
+    ids, guess, cond_x, cond_y, source, inflow, send, halo_a, halo_b, coefs, coarse,
+    guess_in, coefs_in, sems,
+):
+    blocks, rows, lanes = send.shape
+    columns = guess.shape[1]
+    own = columns // blocks
+    around = pl.ds(pl.multiple_of(ids[0], LANE), lanes + LANE)
+    coarse_at = pl.ds(pl.multiple_of(ids[4], LANE), lanes)
+    copies = [pltpu.make_async_copy(guess, guess_in, sems.at[0])]
+    for slot, ref in enumerate((cond_x, cond_y, source)):
+        copies.append(pltpu.make_async_copy(ref.at[:, around], coefs_in.at[slot], sems.at[1 + slot]))
+    copies.append(pltpu.make_async_copy(inflow.at[:, coarse_at], coarse, sems.at[4]))
+    for copy in copies:
+        copy.start()
+    copies[0].wait()
+    for block in range(blocks):
+        start = min(max(own * block - SIDE, 0), columns - lanes)
+        send[block] = guess_in[:, start : start + lanes]
+    for copy in copies[1:]:
+        copy.wait()
+    for slot in range(3):
+        for chunk in range(lanes // LANE):
+            coefs[slot, :, piece(chunk)] = shifted(lambda k: coefs_in[slot, :, piece(k)], chunk, ids[1])
+
+    def fill(bottom, top):
+        at = 0
+        for slot, deep in enumerate(COEF_ROWS):
+            bottom[at : at + deep] = coefs[slot, rows - deep :]
+            top[at : at + deep] = coefs[slot, :deep]
+            at += deep
+        bottom[at:] = coarse[rows // 2 - COARSE_ROWS :]
+        top[at:] = coarse[:COARSE_ROWS]
+
+    @pl.when(ids[2] == 1)
+    def _():
+        fill(halo_a, halo_b)
+
+    @pl.when(ids[2] == 0)
+    def _():
+        fill(halo_b, halo_a)
+
+
+def edge_kernel(ids, fields, edge_a, edge_b):
+    rows = fields.shape[1]
+
+    def fill(bottom, top):
+        at = 0
+        for group, deep in enumerate(FIELD_ROWS):
+            bottom[at : at + deep] = fields[group, rows - deep :]
+            top[at : at + deep] = fields[group, :deep]
+            at += deep
+
+    @pl.when(ids[2] == 1)
+    def _():
+        fill(edge_a, edge_b)
+
+    @pl.when(ids[2] == 0)
+    def _():
+        fill(edge_b, edge_a)
+
+
+def spread(value):
+    rows, lanes = value.shape
+    value = value.reshape(rows // 8, 8, lanes)
+    row_even = lax.broadcasted_iota(jnp.int32, value.shape, 1) % 2 == 0
+    lane_even = lax.broadcasted_iota(jnp.int32, value.shape, 2) % 2 == 0
+    value = value + jnp.where(row_even, pltpu.roll(value, 7, 1), pltpu.roll(value, 1, 1))
+    value = value + jnp.where(lane_even, pltpu.roll(value, lanes - 1, 2), pltpu.roll(value, 1, 2))
+    return (value * 0.25).reshape(rows, lanes)
+
+
+def prepare_kernel(ids, coefs, coarse, coef_a, coef_b, cond_x, cond_y, source, coarse_x, coarse_y, error, tall):
+    rows, lanes = coefs.shape[1:]
+    chunks = lanes // LANE
+    low = HALO + rows
+    targets = (cond_x, cond_y, source)
+
+    def assemble(upper, lower):
+        at = 0
+        for ref, deep in zip(targets, COEF_ROWS):
+            for chunk in range(chunks):
+                ref[chunk, HALO - deep : HALO] = upper[at : at + deep, piece(chunk)]
+                ref[chunk, low : low + deep] = lower[at : at + deep, piece(chunk)]
+            at += deep
+        tall[:COARSE_ROWS] = upper[at:]
+        tall[COARSE_ROWS + rows // 2 :] = lower[at:]
+
+    @pl.when(ids[2] == 1)
+    def _():
+        assemble(coef_b, coef_a)
+
+    @pl.when(ids[2] == 0)
+    def _():
+        assemble(coef_a, coef_b)
+
+    tall[COARSE_ROWS : COARSE_ROWS + rows // 2] = coarse[...]
+    for slot, ref in enumerate(targets):
+        for chunk in range(chunks):
+            ref[chunk, HALO:low] = coefs[slot, :, piece(chunk)]
+    span = slice(HALO - 8, low + 8)
+    for chunk in range(chunks):
+        coarse_x[chunk, span] = spread(cond_x[chunk, span])
+        coarse_y[chunk, span] = spread(cond_y[chunk, span])
+    high = rows // 2 + 2 * COARSE_ROWS
+    half = lax.broadcasted_iota(jnp.int32, (8, LANE), 1) // 2
+    twice = lax.broadcasted_iota(jnp.int32, (8, LANE), 0) // 2
+    first, shift = ids[5], ids[6]
+
+    def load(chunk):
+        at = jnp.minimum((first + chunk) * LANE, lanes - LANE)
+        return tall[:, pl.ds(pl.multiple_of(at, LANE), LANE)]
+
+    for pair in range((chunks + 1) // 2):
+        compact = shifted(load, pair, shift)
+        for side in range(2):
+            chunk = 2 * pair + side
+            if chunk < chunks:
+                for part in range(high // 8):
+                    wide = jnp.take_along_axis(compact[8 * part : 8 * part + 8], half + side * (LANE // 2), axis=1)
+                    for end in range(2):
+                        at = HALO - 2 * COARSE_ROWS + 16 * part + 8 * end
+                        error[chunk, at : at + 8] = jnp.take_along_axis(wide, twice + 4 * end, axis=0)
+
+
+def sweep(items, cond_x, cond_y, width, limit):
+    chunks = cond_x.shape[0]
+    states = []
+    for values, put, first, count, added in items:
+        value = values[0, first : first + count]
+        states.append((value, pltpu.roll(value, LANE - width, 1), jnp.zeros_like(value)))
+    for chunk in range(chunks):
+        for item, (values, put, first, count, added) in enumerate(items):
+            value, east, west_flux = states[item]
+            lane = lax.broadcasted_iota(jnp.int32, value.shape, 1)
+            row = lax.broadcasted_iota(jnp.int32, value.shape, 0)
+            here = slice(first, first + count)
+            above = slice(first - width, first - width + count)
+            below = slice(first + width, first + width + count)
+            if chunk + 1 < chunks:
+                next_value = values[chunk + 1, here]
+                next_east = pltpu.roll(next_value, LANE - width, 1)
+            else:
+                next_value, next_east = None, jnp.zeros_like(value)
+            beside = jnp.where(lane >= LANE - width, next_east, east)
+            flux_y = cond_y[chunk, here] * (beside - value)
+            rolled = pltpu.roll(flux_y, width, 1)
+            flux_w = jnp.where(lane < width, west_flux, rolled)
+            flux_x = cond_x[chunk, here] * (values[chunk, below] - value)
+            flux_u = cond_x[chunk, above] * (value - values[chunk, above])
+            result = value + ((flux_x - flux_u) + (flux_y - flux_w)) + added(chunk, here)
+            put[chunk, here] = jnp.where(row < limit - first, result, 0.0)
+            states[item] = (next_value, next_east, rolled)
+
+
+def reach(rows, deep):
+    return HALO - deep, (rows + 2 * deep + 7) // 8 * 8
+
+
+def main_kernel(
+    ids, fields, cond_x, cond_y, source, coarse_x, coarse_y, start_error, edge_a, edge_b, out,
+    guess, work, first_pass, second_pass, error,
+):
+    groups, rows, lanes = fields.shape
+    chunks = lanes // LANE
+    low = HALO + rows
+    limit = jnp.where(ids[3] == 1, low, low + HALO)
+
+    def assemble(upper, lower):
+        at = 0
+        for group, deep in enumerate(FIELD_ROWS):
+            for chunk in range(chunks):
+                guess[group, chunk, HALO - deep : HALO] = upper[at : at + deep, piece(chunk)]
+                guess[group, chunk, low : low + deep] = lower[at : at + deep, piece(chunk)]
+            at += deep
+
+    @pl.when(ids[2] == 1)
+    def _():
+        assemble(edge_b, edge_a)
+
+    @pl.when(ids[2] == 0)
+    def _():
+        assemble(edge_a, edge_b)
+
+    for group in range(groups - 1):
+        for chunk in range(chunks):
+            guess[group, chunk, HALO:low] = fields[group, :, piece(chunk)]
+
+    def add_source(chunk, here):
+        return source[chunk, here]
+
+    def propagate_all(starts, ends, deeps):
+        for number in range(FINE_STEPS):
+            items = []
+            for slot, (start, end, deep) in enumerate(zip(starts, ends, deeps)):
+                before = start if number == 0 else work.at[slot, number % 2]
+                after = end if number == FINE_STEPS - 1 else work.at[slot, (number + 1) % 2]
+                items.append((before, after, *reach(rows, deep + FINE_STEPS - 1 - number), add_source))
+            sweep(items, cond_x, cond_y, 1, limit)
+
+    propagate_all([guess.at[g] for g in range(3)], [first_pass.at[g] for g in range(3)], (6, 4, 0))
+    propagate_all([first_pass.at[g] for g in range(2)], [second_pass.at[g] for g in range(2)], (2, 0))
+
+    ends = (first_pass.at[0], second_pass.at[0], second_pass.at[1])
+    for group in range(1, groups):
+        reached, relaxed = ends[group - 1], first_pass.at[group - 1]
+        before = start_error if group == 1 else error.at[group - 2]
+
+        def residual(chunk, here, reached=reached, relaxed=relaxed):
+            return spread(reached[chunk, here] - relaxed[chunk, here])
+
+        sweep(
+            [(before, error.at[group - 1], *reach(rows, 2 * (groups - 1 - group)), residual)],
+            coarse_x, coarse_y, 2, limit,
+        )
+
+    for group in range(groups):
+        relaxed = guess.at[0] if group == 0 else first_pass.at[group - 1]
+        correction = start_error if group == 0 else error.at[group - 1]
+
+        def load(chunk):
+            return relaxed[chunk, HALO:low] + correction[chunk, HALO:low]
+
+        for chunk in range(chunks - 1):
+            out[group, :, piece(chunk)] = shifted(load, chunk, ids[1])
+
+
+def unpack_kernel(blocks, out, sems):
+    own = blocks.shape[2]
+    copies = []
+    for block in range(blocks.shape[0]):
+        target = out.at[0, :, block * own : (block + 1) * own]
+        copies.append(pltpu.make_async_copy(blocks.at[block], target, sems.at[block]))
+    for copy in copies:
+        copy.start()
+    for copy in copies:
+        copy.wait()
+
+
+def call(kernel, outs, scratch, operands, whole=(), outside=False, copies=0):
+    vmem, smem, anywhere = (pl.BlockSpec(memory_space=space) for space in (pltpu.VMEM, pltpu.SMEM, pl.ANY))
+    specs = [
+        anywhere if slot in whole else smem if value.dtype == jnp.int32 else vmem
+        for slot, value in enumerate(operands)
+    ]
+    return pl.pallas_call(
+        kernel,
+        out_shape=[jax.ShapeDtypeStruct(shape, jnp.float32) for shape in outs],
+        in_specs=specs,
+        out_specs=[anywhere if outside else vmem] * len(outs),
+        scratch_shapes=[pltpu.VMEM(shape, jnp.float32) for shape in scratch]
+        + ([pltpu.SemaphoreType.DMA((copies,))] if copies else []),
+        compiler_params=pltpu.CompilerParams(vmem_limit_bytes=VMEM_LIMIT),
+    )(*operands)
+
+
+def shards(guesses, cond_x, cond_y, source, inflow):
+    groups, strips = lax.axis_size("tm"), lax.axis_size("space")
+    rows, columns = cond_x.shape
+    fits = groups == len(FIELD_ROWS) + 1 and strips % 2 == 0 and rows == 16
+    if not fits or columns % (2 * groups * LANE) != 0 or columns < 2 * groups * LANE:
+        return general_shards(guesses, cond_x, cond_y, source, inflow)
+    own = columns // groups
+    lanes = own + 2 * SIDE
+    chunks = lanes // LANE
+    member, strip = lax.axis_index("tm"), lax.axis_index("space")
+    start, around = window(member, own, columns, lanes)
+    coarse_start = jnp.minimum(start // 2 // LANE * LANE, columns // 2 - lanes)
+    coarse_skip = start // 2 - coarse_start
+    last = (strip == strips - 1).astype(jnp.int32)
+    ids = [around, start - around, 1 - strip % 2, last, coarse_start, coarse_skip // LANE, coarse_skip % LANE]
+    ids = jnp.stack([jnp.asarray(value, jnp.int32) for value in ids])
+    pairs_a = [(i, i ^ 1) for i in range(strips)]
+    pairs_b = [(i, j) for k in range(1, strips - 1, 2) for i, j in ((k, k + 1), (k + 1, k))]
+
+    travel = sum(COEF_ROWS) + COARSE_ROWS
+    send, halo_a, halo_b, coefs, coarse = call(
+        pack_kernel,
+        [(groups, rows, lanes), (travel, lanes), (travel, lanes), (3, rows, lanes), (rows // 2, lanes)],
+        [(rows, columns), (3, rows, lanes + LANE)],
+        [ids, guesses[0], cond_x, cond_y, source, inflow], whole=range(1, 6), copies=5,
+    )
+    coef_b = lax.ppermute(halo_b, "space", pairs_b)
+    coef_a = lax.ppermute(halo_a, "space", pairs_a)
+    fields = lax.all_to_all(send, "tm", 0, 0, tiled=True)
+    deep = sum(FIELD_ROWS)
+    sent_a, sent_b = call(edge_kernel, [(deep, lanes)] * 2, [], [ids, fields])
+    edge_b = lax.ppermute(sent_b, "space", pairs_b)
+    edge_a = lax.ppermute(sent_a, "space", pairs_a)
+    buffer = (chunks, rows + 2 * HALO, LANE)
+    prepared = call(
+        prepare_kernel, [buffer] * 6, [(rows // 2 + 2 * COARSE_ROWS, lanes)], [ids, coefs, coarse, coef_a, coef_b]
+    )
+    (blocks,) = call(
+        main_kernel,
+        [(groups, rows, own)],
+        [(3, *buffer), (3, 2, *buffer), (3, *buffer), (2, *buffer), (3, *buffer)],
+        [ids, fields, *prepared, edge_a, edge_b],
+    )
+    blocks = lax.all_to_all(blocks, "tm", 0, 0, tiled=True)
+    return call(unpack_kernel, [(1, rows, columns)], [], [blocks], outside=True, copies=groups)[0]
+
+
 def solution(mesh):
     return jax.shard_map(
         shards,

time: 247 us -> 49.9 us (0.20); the launches traced: 243 us -> 49.1 us
  starting transfers between devices: 98.3 us -> 10.5 us
  local copies, waits for them, and re-layouts: 73 us -> 4.64 us
  other arithmetic: 39.6 us -> 0 us
  waiting for transfers between devices: 31.8 us -> 5.85 us
  Pallas kernels: 0 us -> 18.4 us
  blocking collectives: 0 us -> 9.68 us
    ppermute x28 -> x4, starting transfers between devices: 98.3 us -> 6.43 us  [the longest x1 1.91 us: shards(): coef_b = lax.ppermute(halo_b, 'space', pairs_b)]
    reshape x5 -> x0, local copies, waits for them, and re-layouts: 69.3 us -> none  [the longest x2 68.3 us: restrict(): field.reshape(lead + (field.shape[-2] // 2, 2, field.shape[-1] // 2, 2))]
    ppermute x28 -> x4, waiting for transfers between devices: 31.8 us -> 3.53 us  [the longest x1 1.79 us: shards(): edge_b = lax.ppermute(sent_b, 'space', pairs_b)]
    reduce_sum x2 -> x0, other arithmetic: 24.4 us -> none  [restrict(): return jnp.mean(shaped, axis=(-3, -1))]
    pallas_call x0 -> x5, Pallas kernels: none -> 18.4 us  [call(): pl.pallas_call(kernel, out_shape=[jax.ShapeDtypeStruct(shape, jnp.float32...]
    add x11 -> x0, other arithmetic: 12.1 us -> none  [the longest x8 11.7 us: propagate(): field = interior(extended, cond_rows, cond_cols) + source_rows]
    all_to_all x0 -> x1, blocking collectives: none -> 9.68 us  [shards(): blocks = lax.all_to_all(blocks, 'tm', 0, 0, tiled=True)]
    unnamed x8 -> x10, local copies, waits for them, and re-layouts: 0.02 us -> 4.55 us
  transfers between devices with their start and end apart: 28 -> 5, of which waited for: 15 -> 3; matrix products, arithmetic and copies ran while one was open for 26% -> 0% of each run, Pallas kernels for 0% -> 3%
where the time goes in v2:
time: 49.9 us; the launch traced here: 49.1 us
  Pallas kernels  18.4 us (37%)
  starting transfers between devices  10.5 us (21%)
  blocking collectives  9.68 us (19%)
  waiting for transfers between devices  5.85 us (12%)
  local copies, waits for them, and re-layouts  4.64 us (9%)
    pallas_call x5, Pallas kernels, call(): pl.pallas_call(kernel, out_shape=[jax.ShapeDtypeStruct(shape, jnp.float32...  18.4 us
    all_to_all x1, blocking collectives, shards(): blocks = lax.all_to_all(blocks, 'tm', 0, 0, tiled=True)  9.68 us
    unnamed x10, local copies, waits for them, and re-layouts  4.55 us
    all_to_all x1, starting transfers between devices, shards(): fields = lax.all_to_all(send, 'tm', 0, 0, tiled=True)  4.1 us
    all_to_all x1, waiting for transfers between devices, shards(): fields = lax.all_to_all(send, 'tm', 0, 0, tiled=True)  2.32 us
    ppermute x1, starting transfers between devices, shards(): coef_b = lax.ppermute(halo_b, 'space', pairs_b)  1.91 us
    ppermute x1, starting transfers between devices, shards(): edge_b = lax.ppermute(sent_b, 'space', pairs_b)  1.91 us
    ppermute x1, waiting for transfers between devices, shards(): edge_b = lax.ppermute(sent_b, 'space', pairs_b)  1.79 us
  transfers between devices with their start and end apart: 5, of which 3 were waited for; matrix products, arithmetic and copies ran while one was open for 0% of the time, Pallas kernels for 3%

profile of v2, /device:TPU:9, one launch (start us, length us, event | category | flops | bytes accessed | tf_op | source)
XLA Modules:
  0.0 49.1 jit_solution(15689366844589735507)
XLA Ops:
  0.0 0.0 copy-start.4
  0.0 0.1 stack.35.ids
  0.1 0.8 %copy-done.4 = f32[8,2048]{1,0:T(8,128)S(1)} copy-done((f32[8,2048]{1,0:T(8,128)S(1)}, f32[8,2048]{1,0:T(8,128)}, u32[]{:S(2)}) %copy-start.4) | copy-done | bytes 65560
  0.8 0.0 copy-start
  0.8 0.9 %copy-done = f32[1,16,4096]{2,1,0:T(8,128)S(1)} copy-done((f32[1,16,4096]{2,1,0:T(8,128)S(1)}, f32[1,16,4096]{2,1,0:T(8,128)}, u32[]{:S(2)}) %copy-start) | copy-done | bytes 262168
  1.8 0.9 %copy-done.1 = f32[16,4096]{1,0:T(8,128)S(1)} copy-done((f32[16,4096]{1,0:T(8,128)S(1)}, f32[16,4096]{1,0:T(8,128)}, u32[]{:S(2)}) %copy-start.1) | copy-done | bytes 262168
  2.7 0.9 %copy-done.2 = f32[16,4096]{1,0:T(8,128)S(1)} copy-done((f32[16,4096]{1,0:T(8,128)S(1)}, f32[16,4096]{1,0:T(8,128)}, u32[]{:S(2)}) %copy-start.2) | copy-done | bytes 262168
  3.7 0.9 %copy-done.3 = f32[16,4096]{1,0:T(8,128)S(1)} copy-done((f32[16,4096]{1,0:T(8,128)S(1)}, f32[16,4096]{1,0:T(8,128)}, u32[]{:S(2)}) %copy-start.3) | copy-done | bytes 262168
  4.6 1.9 %shard_map.55 = (f32[4,16,1152]{2,1,0:T(8,128)}, f32[32,1152]{1,0:T(8,128)S(1)}, f32[32,1152]{1,0:T(8,128)S(1)}, f32[3,16,1152]{2,1,0:T(8,128)S(1)}, f32[8,1152]{1,0:T(8,128)S(1)}) custom-call(s32[7]{0:T(128)S(1)} %stack.35.ids, f32[16,4096]{1,0:T(8,128)S(1)} %bitcast.8, f32[16,4096]{1,0:T(8,128)S(1)} %copy-done.1, f32[16,4096]{1,0:T(8,128)S(1)} %copy-done.2, ...), custom_call_target="tpu_custom_call" | custom-call | tf_op jit(solution)/shard_map/pallas_call | solution.py:364
  6.5 4.1 %all-to-all-start = ((f32[4,16,1152]{2,1,0:T(8,128)}), f32[4,16,1152]{2,1,0:T(8,128)S(1)}, u32[]{:S(2)}, u32[]{:S(2)}) async-start(f32[4,16,1152]{2,1,0:T(8,128)} %get-tuple-element.18), calls=%async_computation | async-start | bytes 589824 | tf_op jit(solution)/shard_map/all_to_all | solution.py:403
  10.6 1.3 %collective-permute-start = (f32[32,1152]{1,0:T(8,128)S(1)}, f32[32,1152]{1,0:T(8,128)S(1)}, u32[]{:S(2)}, u32[]{:S(2)}) collective-permute-start(f32[32,1152]{1,0:T(8,128)S(1)} %get-tuple-element.21), channel_id=1, source_target_pairs={{0,1},{1,0},{2,3},{3,2},{4,5},{5,4},{6,7},{7,6},{8,9},{9,8},{10,11... | collective-permute-start | bytes 442376 | tf_op jit(solution)/shard_map/ppermute | solution.py:402
  11.9 1.9 %collective-permute-start.1 = (f32[32,1152]{1,0:T(8,128)S(1)}, f32[32,1152]{1,0:T(8,128)S(1)}, u32[]{:S(2)}, u32[]{:S(2)}) collective-permute-start(f32[32,1152]{1,0:T(8,128)S(1)} %get-tuple-element.22), channel_id=1, source_target_pairs={{1,2},{2,1},{3,4},{4,3},{5,6},{6,5},{9,10},{10,9},{11,12},{12,11},... | collective-permute-start | bytes 442376 | tf_op jit(solution)/shard_map/ppermute | solution.py:401
  13.8 2.3 %all-to-all-done.fields = f32[4,16,1152]{2,1,0:T(8,128)S(1)} async-done(((f32[4,16,1152]{2,1,0:T(8,128)}), f32[4,16,1152]{2,1,0:T(8,128)S(1)}, u32[]{:S(2)}, u32[]{:S(2)}) %all-to-all-start) | async-done | bytes 294944 | tf_op jit(solution)/shard_map/all_to_all | solution.py:403
  16.1 0.6 %shard_map.57 = (f32[24,1152]{1,0:T(8,128)S(1)}, f32[24,1152]{1,0:T(8,128)S(1)}) custom-call(s32[7]{0:T(128)S(1)} %stack.35.ids, f32[4,16,1152]{2,1,0:T(8,128)S(1)} %all-to-all-done.fields), custom_call_target="tpu_custom_call" | custom-call | tf_op jit(solution)/shard_map/pallas_call | solution.py:364
  16.7 1.3 %collective-permute-start.2 = (f32[24,1152]{1,0:T(8,128)S(1)}, f32[24,1152]{1,0:T(8,128)S(1)}, u32[]{:S(2)}, u32[]{:S(2)}) collective-permute-start(f32[24,1152]{1,0:T(8,128)S(1)} %get-tuple-element.29), channel_id=1, source_target_pairs={{0,1},{1,0},{2,3},{3,2},{4,5},{5,4},{6,7},{7,6},{8,9},{9,8},{10,11... | collective-permute-start | bytes 331784 | tf_op jit(solution)/shard_map/ppermute | solution.py:407
  18.1 1.9 %collective-permute-start.3 = (f32[24,1152]{1,0:T(8,128)S(1)}, f32[24,1152]{1,0:T(8,128)S(1)}, u32[]{:S(2)}, u32[]{:S(2)}) collective-permute-start(f32[24,1152]{1,0:T(8,128)S(1)} %get-tuple-element.30), channel_id=1, source_target_pairs={{1,2},{2,1},{3,4},{4,3},{5,6},{6,5},{9,10},{10,9},{11,12},{12,11},... | collective-permute-start | bytes 331784 | tf_op jit(solution)/shard_map/ppermute | solution.py:406
  20.0 0.0 collective-permute-done.coef_a
  20.0 0.0 collective-permute-done.1.coef_b
  20.0 0.9 %shard_map.56 = (f32[9,48,128]{2,1,0:T(8,128)S(1)}, f32[9,48,128]{2,1,0:T(8,128)S(1)}, f32[9,48,128]{2,1,0:T(8,128)S(1)}, f32[9,48,128]{2,1,0:T(8,128)S(1)}, f32...) custom-call(s32[7]{0:T(128)S(1)} %stack.35.ids, f32[3,16,1152]{2,1,0:T(8,128)S(1)} %get-tuple-element.19.coefs, ...), custom_call_target="tpu_custom_call" | custom-call | tf_op jit(solution)/shard_map/pallas_call | solution.py:364
  20.9 1.7 %collective-permute-done.2.edge_a = f32[24,1152]{1,0:T(8,128)S(1)} collective-permute-done((f32[24,1152]{1,0:T(8,128)S(1)}, f32[24,1152]{1,0:T(8,128)S(1)}, u32[]{:S(2)}, u32[]{:S(2)}) %collective-permute-start.2) | collective-permute-done | bytes 110624 | tf_op jit(solution)/shard_map/ppermute | solution.py:407
  22.6 1.8 %collective-permute-done.3.edge_b = f32[24,1152]{1,0:T(8,128)S(1)} collective-permute-done((f32[24,1152]{1,0:T(8,128)S(1)}, f32[24,1152]{1,0:T(8,128)S(1)}, u32[]{:S(2)}, u32[]{:S(2)}) %collective-permute-start.3) | collective-permute-done | bytes 110624 | tf_op jit(solution)/shard_map/ppermute | solution.py:406
  24.4 14.3 %shard_map.58 = f32[4,16,1024]{2,1,0:T(8,128)S(1)} custom-call(s32[7]{0:T(128)S(1)} %stack.35.ids, f32[4,16,1152]{2,1,0:T(8,128)S(1)} %all-to-all-done.fields, f32[9,48,128]{2,1,0:T(8,128)S(1)} %get-tuple-element.23.cond_x, f32[9,48,128]{2,1,0:T(8,128)S(1)} %get-tuple-element.24.cond_y, f32[9,48,128]{2,1,0:T(8,128)S(1)} %get-tuple-element.25.source, ...), custom_call_target="tpu_custom_call" | custom-call | tf_op jit(solution)/shard_map/pallas_call | solution.py:364
  38.7 9.7 %all_to_all.10.blocks = f32[4,16,1024]{2,1,0:T(8,128)S(1)} all-to-all(f32[4,16,1024]{2,1,0:T(8,128)S(1)} %shard_map.58), channel_id=1, replica_groups=mesh['tm'=4,'space'=8] {'tm'}, dimensions={0} | all-to-all | bytes 524288 | tf_op jit(solution)/shard_map/all_to_all | solution.py:418
  48.4 0.7 %shard_map.59 = f32[1,16,4096]{2,1,0:T(8,128)} custom-call(f32[4,16,1024]{2,1,0:T(8,128)S(1)} %all_to_all.10.blocks), custom_call_target="tpu_custom_call" | custom-call | tf_op jit(solution)/shard_map/pallas_call | solution.py:364
  (3 shorter events, 0.0 us)
Async XLA Ops:
  0.0 0.8 %copy-start.4 = (f32[8,2048]{1,0:T(8,128)S(1)}, f32[8,2048]{1,0:T(8,128)}, u32[]{:S(2)}) copy-start(f32[8,2048]{1,0:T(8,128)} %inflow.1) | copy-start | bytes 196612
  0.8 0.9 %copy-start = (f32[1,16,4096]{2,1,0:T(8,128)S(1)}, f32[1,16,4096]{2,1,0:T(8,128)}, u32[]{:S(2)}) copy-start(f32[1,16,4096]{2,1,0:T(8,128)} %param.5) | copy-start | bytes 786436
  1.8 0.9 %copy-start.1 = (f32[16,4096]{1,0:T(8,128)S(1)}, f32[16,4096]{1,0:T(8,128)}, u32[]{:S(2)}) copy-start(f32[16,4096]{1,0:T(8,128)} %cond_x.1) | copy-start | bytes 786436
  2.7 0.9 %copy-start.2 = (f32[16,4096]{1,0:T(8,128)S(1)}, f32[16,4096]{1,0:T(8,128)}, u32[]{:S(2)}) copy-start(f32[16,4096]{1,0:T(8,128)} %cond_y.1) | copy-start | bytes 786436
  3.7 0.9 %copy-start.3 = (f32[16,4096]{1,0:T(8,128)S(1)}, f32[16,4096]{1,0:T(8,128)}, u32[]{:S(2)}) copy-start(f32[16,4096]{1,0:T(8,128)} %source.1) | copy-start | bytes 786436
  6.5 9.6 %all-to-all-start = ((f32[4,16,1152]{2,1,0:T(8,128)}), f32[4,16,1152]{2,1,0:T(8,128)S(1)}, u32[]{:S(2)}, u32[]{:S(2)}) async-start(f32[4,16,1152]{2,1,0:T(8,128)} %get-tuple-element.18), calls=%async_computation | async-start | bytes 589824 | tf_op jit(solution)/shard_map/all_to_all | solution.py:403
  10.6 9.4 %collective-permute-start = (f32[32,1152]{1,0:T(8,128)S(1)}, f32[32,1152]{1,0:T(8,128)S(1)}, u32[]{:S(2)}, u32[]{:S(2)}) collective-permute-start(f32[32,1152]{1,0:T(8,128)S(1)} %get-tuple-element.21), channel_id=1, source_target_pairs={{0,1},{1,0},{2,3},{3,2},{4,5},{5,4},{6,7},{7,6},{8,9},{9,8},{10,11... | collective-permute-start | bytes 442376 | tf_op jit(solution)/shard_map/ppermute | solution.py:402
  11.9 8.1 %collective-permute-start.1 = (f32[32,1152]{1,0:T(8,128)S(1)}, f32[32,1152]{1,0:T(8,128)S(1)}, u32[]{:S(2)}, u32[]{:S(2)}) collective-permute-start(f32[32,1152]{1,0:T(8,128)S(1)} %get-tuple-element.22), channel_id=1, source_target_pairs={{1,2},{2,1},{3,4},{4,3},{5,6},{6,5},{9,10},{10,9},{11,12},{12,11},... | collective-permute-start | bytes 442376 | tf_op jit(solution)/shard_map/ppermute | solution.py:401
  16.7 5.9 %collective-permute-start.2 = (f32[24,1152]{1,0:T(8,128)S(1)}, f32[24,1152]{1,0:T(8,128)S(1)}, u32[]{:S(2)}, u32[]{:S(2)}) collective-permute-start(f32[24,1152]{1,0:T(8,128)S(1)} %get-tuple-element.29), channel_id=1, source_target_pairs={{0,1},{1,0},{2,3},{3,2},{4,5},{5,4},{6,7},{7,6},{8,9},{9,8},{10,11... | collective-permute-start | bytes 331784 | tf_op jit(solution)/shard_map/ppermute | solution.py:407
  18.1 6.4 %collective-permute-start.3 = (f32[24,1152]{1,0:T(8,128)S(1)}, f32[24,1152]{1,0:T(8,128)S(1)}, u32[]{:S(2)}, u32[]{:S(2)}) collective-permute-start(f32[24,1152]{1,0:T(8,128)S(1)} %get-tuple-element.30), channel_id=1, source_target_pairs={{1,2},{2,1},{3,4},{4,3},{5,6},{6,5},{9,10},{10,9},{11,12},{12,11},... | collective-permute-start | bytes 331784 | tf_op jit(solution)/shard_map/ppermute | solution.py:406

commit v3 on v2

--- a/solution.py
+++ b/solution.py
@@ -188,10 +188,32 @@
     return (value * 0.25).reshape(rows, lanes)
 
 
-def prepare_kernel(ids, coefs, coarse, coef_a, coef_b, cond_x, cond_y, source, coarse_x, coarse_y, error, tall):
+def weights(cond_x, cond_y, chunk, rows, width, limit, out):
+    diagonal, up, east, west = out
+    chunks = cond_x.shape[0]
+    first, count = rows
+    here = slice(first, first + count)
+    own_x, own_y = cond_x[chunk, here], cond_y[chunk, here]
+    above = cond_x[chunk, first - width : first - width + count]
+    lane = lax.broadcasted_iota(jnp.int32, own_x.shape, 1)
+    row = lax.broadcasted_iota(jnp.int32, own_x.shape, 0)
+    before = pltpu.roll(cond_y[chunk - 1, here], width, 1) if chunk else jnp.zeros_like(own_y)
+    beside = jnp.where(lane < width, before, pltpu.roll(own_y, width, 1))
+    diagonal[chunk, here] = 1.0 - ((own_x + above) + (own_y + beside))
+    up[chunk, here] = jnp.where(row < limit - first, above, 0.0)
+    west[chunk, here] = beside
+    east[chunk, here] = jnp.where(lane < LANE - width, own_y, 0.0) if chunk == chunks - 1 else own_y
+
+
+def prepare_kernel(
+    ids, coefs, coarse, coef_a, coef_b,
+    cond_x, source, diagonal, up, east, west, coarse_x, coarse_d, coarse_u, coarse_e, coarse_w, error,
+    cond_y, coarse_y, tall,
+):
     rows, lanes = coefs.shape[1:]
     chunks = lanes // LANE
     low = HALO + rows
+    limit = jnp.where(ids[3] == 1, low, low + HALO)
     targets = (cond_x, cond_y, source)
 
     def assemble(upper, lower):
@@ -216,10 +238,14 @@
     for slot, ref in enumerate(targets):
         for chunk in range(chunks):
             ref[chunk, HALO:low] = coefs[slot, :, piece(chunk)]
+    for chunk in range(chunks):
+        weights(cond_x, cond_y, chunk, reach(rows, 9), 1, limit, (diagonal, up, east, west))
     span = slice(HALO - 8, low + 8)
     for chunk in range(chunks):
         coarse_x[chunk, span] = spread(cond_x[chunk, span])
         coarse_y[chunk, span] = spread(cond_y[chunk, span])
+    for chunk in range(chunks):
+        weights(coarse_x, coarse_y, chunk, reach(rows, 4), 2, limit, (coarse_d, coarse_u, coarse_e, coarse_w))
     high = rows // 2 + 2 * COARSE_ROWS
     half = lax.broadcasted_iota(jnp.int32, (8, LANE), 1) // 2
     twice = lax.broadcasted_iota(jnp.int32, (8, LANE), 0) // 2
@@ -241,34 +267,31 @@
                         error[chunk, at : at + 8] = jnp.take_along_axis(wide, twice + 4 * end, axis=0)
 
 
-def sweep(items, cond_x, cond_y, width, limit):
-    chunks = cond_x.shape[0]
-    states = []
-    for values, put, first, count, added in items:
-        value = values[0, first : first + count]
-        states.append((value, pltpu.roll(value, LANE - width, 1), jnp.zeros_like(value)))
+def sweep(values, put, rows, width, factors, added):
+    diagonal, up, down, east, west = factors
+    chunks = diagonal.shape[0]
+    first, count = rows
+    here = slice(first, first + count)
+    above = slice(first - width, first - width + count)
+    below = slice(first + width, first + width + count)
+    lane = lax.broadcasted_iota(jnp.int32, (count, LANE), 1)
+
+    def load(chunk):
+        value = values[chunk, here]
+        return value, pltpu.roll(value, LANE - width, 1), pltpu.roll(value, width, 1)
+
+    before, now, after = None, load(0), None
     for chunk in range(chunks):
-        for item, (values, put, first, count, added) in enumerate(items):
-            value, east, west_flux = states[item]
-            lane = lax.broadcasted_iota(jnp.int32, value.shape, 1)
-            row = lax.broadcasted_iota(jnp.int32, value.shape, 0)
-            here = slice(first, first + count)
-            above = slice(first - width, first - width + count)
-            below = slice(first + width, first + width + count)
-            if chunk + 1 < chunks:
-                next_value = values[chunk + 1, here]
-                next_east = pltpu.roll(next_value, LANE - width, 1)
-            else:
-                next_value, next_east = None, jnp.zeros_like(value)
-            beside = jnp.where(lane >= LANE - width, next_east, east)
-            flux_y = cond_y[chunk, here] * (beside - value)
-            rolled = pltpu.roll(flux_y, width, 1)
-            flux_w = jnp.where(lane < width, west_flux, rolled)
-            flux_x = cond_x[chunk, here] * (values[chunk, below] - value)
-            flux_u = cond_x[chunk, above] * (value - values[chunk, above])
-            result = value + ((flux_x - flux_u) + (flux_y - flux_w)) + added(chunk, here)
-            put[chunk, here] = jnp.where(row < limit - first, result, 0.0)
-            states[item] = (next_value, next_east, rolled)
+        after = load(chunk + 1) if chunk + 1 < chunks else None
+        value, right, left = now
+        if after is not None:
+            right = jnp.where(lane < LANE - width, right, after[1])
+        if before is not None:
+            left = jnp.where(lane < width, before[2], left)
+        across = east[chunk, here] * right + west[chunk, here] * left
+        along = down[chunk, here] * values[chunk, below] + up[chunk, here] * values[chunk, above]
+        put[chunk, here] = (diagonal[chunk, here] * value + added(chunk, here)) + (across + along)
+        before, now = now, after
 
 
 def reach(rows, deep):
@@ -276,13 +299,14 @@
 
 
 def main_kernel(
-    ids, fields, cond_x, cond_y, source, coarse_x, coarse_y, start_error, edge_a, edge_b, out,
-    guess, work, first_pass, second_pass, error,
+    ids, fields, cond_x, source, diagonal, up, east, west, coarse_x, coarse_d, coarse_u, coarse_e, coarse_w,
+    start_error, edge_a, edge_b, out,
+    guess, work, error,
 ):
     groups, rows, lanes = fields.shape
     chunks = lanes // LANE
     low = HALO + rows
-    limit = jnp.where(ids[3] == 1, low, low + HALO)
+    given = groups - 1
 
     def assemble(upper, lower):
         at = 0
@@ -300,44 +324,48 @@
     def _():
         assemble(edge_a, edge_b)
 
-    for group in range(groups - 1):
+    for group in range(given):
         for chunk in range(chunks):
             guess[group, chunk, HALO:low] = fields[group, :, piece(chunk)]
+    span = slice(HALO - 8, low + 8)
+    error[0, :, span] = start_error[:, span]
+
+    fine = (diagonal, up, cond_x, east, west)
+    coarse = (coarse_d, coarse_u, coarse_x, coarse_e, coarse_w)
 
     def add_source(chunk, here):
         return source[chunk, here]
 
-    def propagate_all(starts, ends, deeps):
+    def propagate(slot, deep):
+        stops = [guess.at[slot], work.at[0], work.at[1], work.at[0], guess.at[slot + given]]
         for number in range(FINE_STEPS):
-            items = []
-            for slot, (start, end, deep) in enumerate(zip(starts, ends, deeps)):
-                before = start if number == 0 else work.at[slot, number % 2]
-                after = end if number == FINE_STEPS - 1 else work.at[slot, (number + 1) % 2]
-                items.append((before, after, *reach(rows, deep + FINE_STEPS - 1 - number), add_source))
-            sweep(items, cond_x, cond_y, 1, limit)
-
-    propagate_all([guess.at[g] for g in range(3)], [first_pass.at[g] for g in range(3)], (6, 4, 0))
-    propagate_all([first_pass.at[g] for g in range(2)], [second_pass.at[g] for g in range(2)], (2, 0))
-
-    ends = (first_pass.at[0], second_pass.at[0], second_pass.at[1])
-    for group in range(1, groups):
-        reached, relaxed = ends[group - 1], first_pass.at[group - 1]
-        before = start_error if group == 1 else error.at[group - 2]
-
-        def residual(chunk, here, reached=reached, relaxed=relaxed):
-            return spread(reached[chunk, here] - relaxed[chunk, here])
-
-        sweep(
-            [(before, error.at[group - 1], *reach(rows, 2 * (groups - 1 - group)), residual)],
-            coarse_x, coarse_y, 2, limit,
-        )
-
-    for group in range(groups):
-        relaxed = guess.at[0] if group == 0 else first_pass.at[group - 1]
-        correction = start_error if group == 0 else error.at[group - 1]
+            reached = reach(rows, deep + FINE_STEPS - 1 - number)
+            sweep(stops[number], stops[number + 1], reached, 1, fine, add_source)
+
+    @pl.loop(0, given)
+    def _(group):
+        propagate(group, 6)
+
+    @pl.loop(given, 2 * given - 1)
+    def _(group):
+        propagate(group, 2)
+
+    @pl.loop(1, groups)
+    def _(group):
+        reached = jnp.where(group == 1, given, 2 * given - 2 + group)
+        relaxed = given - 1 + group
+
+        def residual(chunk, here):
+            return spread(guess[reached, chunk, here] - guess[relaxed, chunk, here])
+
+        sweep(error.at[group - 1], error.at[group], reach(rows, 4), 2, coarse, residual)
+
+    @pl.loop(0, groups)
+    def _(group):
+        relaxed = jnp.where(group == 0, 0, given - 1 + group)
 
         def load(chunk):
-            return relaxed[chunk, HALO:low] + correction[chunk, HALO:low]
+            return guess[relaxed, chunk, HALO:low] + error[group, chunk, HALO:low]
 
         for chunk in range(chunks - 1):
             out[group, :, piece(chunk)] = shifted(load, chunk, ids[1])
@@ -356,7 +384,7 @@
 
 
 def call(kernel, outs, scratch, operands, whole=(), outside=False, copies=0):
-    vmem, smem, anywhere = (pl.BlockSpec(memory_space=space) for space in (pltpu.VMEM, pltpu.SMEM, pl.ANY))
+    vmem, smem, anywhere = (pl.BlockSpec(memory_space=space) for space in (pltpu.VMEM, pltpu.SMEM, pltpu.HBM))
     specs = [
         anywhere if slot in whole else smem if value.dtype == jnp.int32 else vmem
         for slot, value in enumerate(operands)
@@ -407,12 +435,15 @@
     edge_a = lax.ppermute(sent_a, "space", pairs_a)
     buffer = (chunks, rows + 2 * HALO, LANE)
     prepared = call(
-        prepare_kernel, [buffer] * 6, [(rows // 2 + 2 * COARSE_ROWS, lanes)], [ids, coefs, coarse, coef_a, coef_b]
+        prepare_kernel,
+        [buffer] * 12,
+        [buffer, buffer, (rows // 2 + 2 * COARSE_ROWS, lanes)],
+        [ids, coefs, coarse, coef_a, coef_b],
     )
     (blocks,) = call(
         main_kernel,
         [(groups, rows, own)],
-        [(3, *buffer), (3, 2, *buffer), (3, *buffer), (2, *buffer), (3, *buffer)],
+        [(3 * groups - 4, *buffer), (2, *buffer), (groups, *buffer)],
         [ids, fields, *prepared, edge_a, edge_b],
     )
     blocks = lax.all_to_all(blocks, "tm", 0, 0, tiled=True)

time: 49.9 us -> 39.8 us (0.80)
  Pallas kernels: 18.4 us -> 8.48 us
    pallas_call x5, Pallas kernels: 18.4 us -> 8.48 us  [call(): pl.pallas_call(kernel, out_shape=[jax.ShapeDtypeStruct(shape, jnp.float32...]
  transfers between devices with their start and end apart: 5 -> 5, of which waited for: 3 -> 3; matrix products, arithmetic and copies ran while one was open for 0% -> 0% of each run, Pallas kernels for 3% -> 4%
where the time goes in v3:
time: 39.8 us; the launch traced here: 39 us
  starting transfers between devices  10.5 us (26%)
  blocking collectives  9.68 us (24%)
  Pallas kernels  8.48 us (21%)
  waiting for transfers between devices  5.65 us (14%)
  local copies, waits for them, and re-layouts  4.64 us (12%)
    all_to_all x1, blocking collectives, shards(): blocks = lax.all_to_all(blocks, 'tm', 0, 0, tiled=True)  9.68 us
    pallas_call x5, Pallas kernels, call(): pl.pallas_call(kernel, out_shape=[jax.ShapeDtypeStruct(shape, jnp.float32...  8.48 us
    unnamed x10, local copies, waits for them, and re-layouts  4.55 us
    all_to_all x1, starting transfers between devices, shards(): fields = lax.all_to_all(send, 'tm', 0, 0, tiled=True)  4.1 us
    all_to_all x1, waiting for transfers between devices, shards(): fields = lax.all_to_all(send, 'tm', 0, 0, tiled=True)  2.32 us
    ppermute x1, starting transfers between devices, shards(): coef_b = lax.ppermute(halo_b, 'space', pairs_b)  1.91 us
    ppermute x1, starting transfers between devices, shards(): edge_b = lax.ppermute(sent_b, 'space', pairs_b)  1.91 us
    ppermute x1, waiting for transfers between devices, shards(): edge_b = lax.ppermute(sent_b, 'space', pairs_b)  1.79 us
  transfers between devices with their start and end apart: 5, of which 3 were waited for; matrix products, arithmetic and copies ran while one was open for 0% of the time, Pallas kernels for 4%

profile of v3, /device:TPU:9, one launch (start us, length us, event | category | flops | bytes accessed | tf_op | source)
XLA Modules:
  0.0 39.0 jit_solution(2483361304628362859)
XLA Ops:
  0.0 0.0 copy-start.4
  0.0 0.1 stack.35.ids
  0.1 0.8 %copy-done.4 = f32[8,2048]{1,0:T(8,128)S(1)} copy-done((f32[8,2048]{1,0:T(8,128)S(1)}, f32[8,2048]{1,0:T(8,128)}, u32[]{:S(2)}) %copy-start.4) | copy-done | bytes 65560
  0.8 0.0 copy-start
  0.8 0.9 %copy-done = f32[1,16,4096]{2,1,0:T(8,128)S(1)} copy-done((f32[1,16,4096]{2,1,0:T(8,128)S(1)}, f32[1,16,4096]{2,1,0:T(8,128)}, u32[]{:S(2)}) %copy-start) | copy-done | bytes 262168
  1.8 0.9 %copy-done.1 = f32[16,4096]{1,0:T(8,128)S(1)} copy-done((f32[16,4096]{1,0:T(8,128)S(1)}, f32[16,4096]{1,0:T(8,128)}, u32[]{:S(2)}) %copy-start.1) | copy-done | bytes 262168
  2.7 0.9 %copy-done.2 = f32[16,4096]{1,0:T(8,128)S(1)} copy-done((f32[16,4096]{1,0:T(8,128)S(1)}, f32[16,4096]{1,0:T(8,128)}, u32[]{:S(2)}) %copy-start.2) | copy-done | bytes 262168
  3.7 0.9 %copy-done.3 = f32[16,4096]{1,0:T(8,128)S(1)} copy-done((f32[16,4096]{1,0:T(8,128)S(1)}, f32[16,4096]{1,0:T(8,128)}, u32[]{:S(2)}) %copy-start.3) | copy-done | bytes 262168
  4.6 1.9 %shard_map.55 = (f32[4,16,1152]{2,1,0:T(8,128)}, f32[32,1152]{1,0:T(8,128)S(1)}, f32[32,1152]{1,0:T(8,128)S(1)}, f32[3,16,1152]{2,1,0:T(8,128)S(1)}, f32[8,1152]{1,0:T(8,128)S(1)}) custom-call(s32[7]{0:T(128)S(1)} %stack.35.ids, f32[16,4096]{1,0:T(8,128)S(1)} %bitcast.8, f32[16,4096]{1,0:T(8,128)S(1)} %copy-done.1, f32[16,4096]{1,0:T(8,128)S(1)} %copy-done.2, ...), custom_call_target="tpu_custom_call" | custom-call | tf_op jit(solution)/shard_map/pallas_call | solution.py:392
  6.5 4.1 %all-to-all-start = ((f32[4,16,1152]{2,1,0:T(8,128)}), f32[4,16,1152]{2,1,0:T(8,128)S(1)}, u32[]{:S(2)}, u32[]{:S(2)}) async-start(f32[4,16,1152]{2,1,0:T(8,128)} %get-tuple-element.24), calls=%async_computation | async-start | bytes 589824 | tf_op jit(solution)/shard_map/all_to_all | solution.py:431
  10.6 1.3 %collective-permute-start = (f32[32,1152]{1,0:T(8,128)S(1)}, f32[32,1152]{1,0:T(8,128)S(1)}, u32[]{:S(2)}, u32[]{:S(2)}) collective-permute-start(f32[32,1152]{1,0:T(8,128)S(1)} %get-tuple-element.27), channel_id=1, source_target_pairs={{0,1},{1,0},{2,3},{3,2},{4,5},{5,4},{6,7},{7,6},{8,9},{9,8},{10,11... | collective-permute-start | bytes 442376 | tf_op jit(solution)/shard_map/ppermute | solution.py:430
  11.9 1.9 %collective-permute-start.1 = (f32[32,1152]{1,0:T(8,128)S(1)}, f32[32,1152]{1,0:T(8,128)S(1)}, u32[]{:S(2)}, u32[]{:S(2)}) collective-permute-start(f32[32,1152]{1,0:T(8,128)S(1)} %get-tuple-element.28), channel_id=1, source_target_pairs={{1,2},{2,1},{3,4},{4,3},{5,6},{6,5},{9,10},{10,9},{11,12},{12,11},... | collective-permute-start | bytes 442376 | tf_op jit(solution)/shard_map/ppermute | solution.py:429
  13.8 2.3 %all-to-all-done.fields = f32[4,16,1152]{2,1,0:T(8,128)S(1)} async-done(((f32[4,16,1152]{2,1,0:T(8,128)}), f32[4,16,1152]{2,1,0:T(8,128)S(1)}, u32[]{:S(2)}, u32[]{:S(2)}) %all-to-all-start) | async-done | bytes 294944 | tf_op jit(solution)/shard_map/all_to_all | solution.py:431
  16.1 0.6 %shard_map.57 = (f32[24,1152]{1,0:T(8,128)S(1)}, f32[24,1152]{1,0:T(8,128)S(1)}) custom-call(s32[7]{0:T(128)S(1)} %stack.35.ids, f32[4,16,1152]{2,1,0:T(8,128)S(1)} %all-to-all-done.fields), custom_call_target="tpu_custom_call" | custom-call | tf_op jit(solution)/shard_map/pallas_call | solution.py:392
  16.7 1.3 %collective-permute-start.2 = (f32[24,1152]{1,0:T(8,128)S(1)}, f32[24,1152]{1,0:T(8,128)S(1)}, u32[]{:S(2)}, u32[]{:S(2)}) collective-permute-start(f32[24,1152]{1,0:T(8,128)S(1)} %get-tuple-element.41), channel_id=1, source_target_pairs={{0,1},{1,0},{2,3},{3,2},{4,5},{5,4},{6,7},{7,6},{8,9},{9,8},{10,11... | collective-permute-start | bytes 331784 | tf_op jit(solution)/shard_map/ppermute | solution.py:435
  18.1 1.9 %collective-permute-start.3 = (f32[24,1152]{1,0:T(8,128)S(1)}, f32[24,1152]{1,0:T(8,128)S(1)}, u32[]{:S(2)}, u32[]{:S(2)}) collective-permute-start(f32[24,1152]{1,0:T(8,128)S(1)} %get-tuple-element.42), channel_id=1, source_target_pairs={{1,2},{2,1},{3,4},{4,3},{5,6},{6,5},{9,10},{10,9},{11,12},{12,11},... | collective-permute-start | bytes 331784 | tf_op jit(solution)/shard_map/ppermute | solution.py:434
  20.0 0.0 collective-permute-done.coef_a
  20.0 0.0 collective-permute-done.1.coef_b
  20.0 1.1 %shard_map.56 = (f32[9,48,128]{2,1,0:T(8,128)S(1)}, f32[9,48,128]{2,1,0:T(8,128)S(1)}, f32[9,48,128]{2,1,0:T(8,128)S(1)}, f32[9,48,128]{2,1,0:T(8,128)S(1)}, f32...) custom-call(s32[7]{0:T(128)S(1)} %stack.35.ids, ...), custom_call_target="tpu_custom_call" | custom-call | tf_op jit(solution)/shard_map/pallas_call | solution.py:392
  21.1 1.5 %collective-permute-done.2.edge_a = f32[24,1152]{1,0:T(8,128)S(1)} collective-permute-done((f32[24,1152]{1,0:T(8,128)S(1)}, f32[24,1152]{1,0:T(8,128)S(1)}, u32[]{:S(2)}, u32[]{:S(2)}) %collective-permute-start.2) | collective-permute-done | bytes 110624 | tf_op jit(solution)/shard_map/ppermute | solution.py:435
  22.6 1.8 %collective-permute-done.3.edge_b = f32[24,1152]{1,0:T(8,128)S(1)} collective-permute-done((f32[24,1152]{1,0:T(8,128)S(1)}, f32[24,1152]{1,0:T(8,128)S(1)}, u32[]{:S(2)}, u32[]{:S(2)}) %collective-permute-start.3) | collective-permute-done | bytes 110624 | tf_op jit(solution)/shard_map/ppermute | solution.py:434
  24.4 4.2 %shard_map.58 = f32[4,16,1024]{2,1,0:T(8,128)S(1)} custom-call(s32[7]{0:T(128)S(1)} %stack.35.ids, f32[4,16,1152]{2,1,0:T(8,128)S(1)} %all-to-all-done.fields, f32[9,48,128]{2,1,0:T(8,128)S(1)} %get-tuple-element.29.cond_x, f32[9,48,128]{2,1,0:T(8,128)S(1)} %get-tuple-element.30.source, f32[9,48,128]{2,1,0:T(8,128)S(1)} %get-tuple-element.31.diagonal, ...), custom_call_target="tpu_custom_call" | custom-call | tf_op jit(solution)/shard_map/pallas_call | solution.py:392
  28.6 9.7 %all_to_all.10.blocks = f32[4,16,1024]{2,1,0:T(8,128)S(1)} all-to-all(f32[4,16,1024]{2,1,0:T(8,128)S(1)} %shard_map.58), channel_id=1, replica_groups=mesh['tm'=4,'space'=8] {'tm'}, dimensions={0} | all-to-all | bytes 524288 | tf_op jit(solution)/shard_map/all_to_all | solution.py:449
  38.3 0.7 %shard_map.59 = f32[1,16,4096]{2,1,0:T(8,128)} custom-call(f32[4,16,1024]{2,1,0:T(8,128)S(1)} %all_to_all.10.blocks), custom_call_target="tpu_custom_call" | custom-call | tf_op jit(solution)/shard_map/pallas_call | solution.py:392
  (3 shorter events, 0.0 us)
Async XLA Ops:
  0.0 0.8 %copy-start.4 = (f32[8,2048]{1,0:T(8,128)S(1)}, f32[8,2048]{1,0:T(8,128)}, u32[]{:S(2)}) copy-start(f32[8,2048]{1,0:T(8,128)} %inflow.1) | copy-start | bytes 196612
  0.8 0.9 %copy-start = (f32[1,16,4096]{2,1,0:T(8,128)S(1)}, f32[1,16,4096]{2,1,0:T(8,128)}, u32[]{:S(2)}) copy-start(f32[1,16,4096]{2,1,0:T(8,128)} %param.5) | copy-start | bytes 786436
  1.8 0.9 %copy-start.1 = (f32[16,4096]{1,0:T(8,128)S(1)}, f32[16,4096]{1,0:T(8,128)}, u32[]{:S(2)}) copy-start(f32[16,4096]{1,0:T(8,128)} %cond_x.1) | copy-start | bytes 786436
  2.7 0.9 %copy-start.2 = (f32[16,4096]{1,0:T(8,128)S(1)}, f32[16,4096]{1,0:T(8,128)}, u32[]{:S(2)}) copy-start(f32[16,4096]{1,0:T(8,128)} %cond_y.1) | copy-start | bytes 786436
  3.7 0.9 %copy-start.3 = (f32[16,4096]{1,0:T(8,128)S(1)}, f32[16,4096]{1,0:T(8,128)}, u32[]{:S(2)}) copy-start(f32[16,4096]{1,0:T(8,128)} %source.1) | copy-start | bytes 786436
  6.5 9.6 %all-to-all-start = ((f32[4,16,1152]{2,1,0:T(8,128)}), f32[4,16,1152]{2,1,0:T(8,128)S(1)}, u32[]{:S(2)}, u32[]{:S(2)}) async-start(f32[4,16,1152]{2,1,0:T(8,128)} %get-tuple-element.24), calls=%async_computation | async-start | bytes 589824 | tf_op jit(solution)/shard_map/all_to_all | solution.py:431
  10.6 9.4 %collective-permute-start = (f32[32,1152]{1,0:T(8,128)S(1)}, f32[32,1152]{1,0:T(8,128)S(1)}, u32[]{:S(2)}, u32[]{:S(2)}) collective-permute-start(f32[32,1152]{1,0:T(8,128)S(1)} %get-tuple-element.27), channel_id=1, source_target_pairs={{0,1},{1,0},{2,3},{3,2},{4,5},{5,4},{6,7},{7,6},{8,9},{9,8},{10,11... | collective-permute-start | bytes 442376 | tf_op jit(solution)/shard_map/ppermute | solution.py:430
  11.9 8.1 %collective-permute-start.1 = (f32[32,1152]{1,0:T(8,128)S(1)}, f32[32,1152]{1,0:T(8,128)S(1)}, u32[]{:S(2)}, u32[]{:S(2)}) collective-permute-start(f32[32,1152]{1,0:T(8,128)S(1)} %get-tuple-element.28), channel_id=1, source_target_pairs={{1,2},{2,1},{3,4},{4,3},{5,6},{6,5},{9,10},{10,9},{11,12},{12,11},... | collective-permute-start | bytes 442376 | tf_op jit(solution)/shard_map/ppermute | solution.py:429
  16.7 5.9 %collective-permute-start.2 = (f32[24,1152]{1,0:T(8,128)S(1)}, f32[24,1152]{1,0:T(8,128)S(1)}, u32[]{:S(2)}, u32[]{:S(2)}) collective-permute-start(f32[24,1152]{1,0:T(8,128)S(1)} %get-tuple-element.41), channel_id=1, source_target_pairs={{0,1},{1,0},{2,3},{3,2},{4,5},{5,4},{6,7},{7,6},{8,9},{9,8},{10,11... | collective-permute-start | bytes 331784 | tf_op jit(solution)/shard_map/ppermute | solution.py:435
  18.1 6.4 %collective-permute-start.3 = (f32[24,1152]{1,0:T(8,128)S(1)}, f32[24,1152]{1,0:T(8,128)S(1)}, u32[]{:S(2)}, u32[]{:S(2)}) collective-permute-start(f32[24,1152]{1,0:T(8,128)S(1)} %get-tuple-element.42), channel_id=1, source_target_pairs={{1,2},{2,1},{3,4},{4,3},{5,6},{6,5},{9,10},{10,9},{11,12},{12,11},... | collective-permute-start | bytes 331784 | tf_op jit(solution)/shard_map/ppermute | solution.py:434

commit v4 on v3

--- a/solution.py
+++ b/solution.py
@@ -100,8 +100,28 @@
     return (relaxed + widened)[None]
 
 
-def window(index, own, columns, lanes):
-    return jnp.clip(own * index - SIDE, 0, columns - lanes), jnp.clip(own * index - LANE, 0, columns - lanes - LANE)
+def place(groups, strips, columns, member):
+    own = columns // groups
+    lanes = own + 2 * SIDE
+    start = jnp.clip(own * member - SIDE, 0, columns - lanes)
+    around = jnp.clip(own * member - LANE, 0, columns - lanes - LANE)
+    coarse = jnp.minimum(start // 2 // LANE * LANE, columns // 2 - lanes)
+    return around, start - around, coarse, start // 2 - coarse
+
+
+def sides(rows):
+    strip, strips = lax.axis_index("space"), lax.axis_size("space")
+    return lax.rem(strip, 2) == 0, jnp.where(strip == strips - 1, HALO + rows, 2 * HALO + rows)
+
+
+def by_side(even, fill, first, second):
+    @pl.when(even)
+    def _():
+        fill(first, second)
+
+    @pl.when(jnp.logical_not(even))
+    def _():
+        fill(second, first)
 
 
 def shifted(load, chunk, shift):
@@ -117,29 +137,37 @@
 
 
 def pack_kernel(
-    ids, guess, cond_x, cond_y, source, inflow, send, halo_a, halo_b, coefs, coarse,
+    guess, cond_x, cond_y, source, inflow, own, to_core, to_x, to_both, halo_a, halo_b, coefs, coarse,
     guess_in, coefs_in, sems,
 ):
-    blocks, rows, lanes = send.shape
+    rows, lanes = own.shape
     columns = guess.shape[1]
-    own = columns // blocks
-    around = pl.ds(pl.multiple_of(ids[0], LANE), lanes + LANE)
-    coarse_at = pl.ds(pl.multiple_of(ids[4], LANE), lanes)
-    copies = [pltpu.make_async_copy(guess, guess_in, sems.at[0])]
+    chunks = lanes // LANE
+    groups, strips, member = lax.axis_size("tm"), lax.axis_size("space"), lax.axis_index("tm")
+    outs = (own, to_core, to_x, to_both)
+    copies, shifts = [], []
+    for slot in range(groups):
+        around, shift, _, _ = place(groups, strips, columns, member ^ slot)
+        at = pl.ds(pl.multiple_of(around, LANE), lanes + LANE)
+        copies.append(pltpu.make_async_copy(guess.at[:, at], guess_in.at[slot], sems.at[slot]))
+        shifts.append(shift)
+    around, shift, coarse_at, _ = place(groups, strips, columns, member)
+    at = pl.ds(pl.multiple_of(around, LANE), lanes + LANE)
     for slot, ref in enumerate((cond_x, cond_y, source)):
-        copies.append(pltpu.make_async_copy(ref.at[:, around], coefs_in.at[slot], sems.at[1 + slot]))
-    copies.append(pltpu.make_async_copy(inflow.at[:, coarse_at], coarse, sems.at[4]))
+        copies.append(pltpu.make_async_copy(ref.at[:, at], coefs_in.at[slot], sems.at[groups + slot]))
+    at = pl.ds(pl.multiple_of(coarse_at, LANE), lanes)
+    copies.append(pltpu.make_async_copy(inflow.at[:, at], coarse, sems.at[groups + 3]))
     for copy in copies:
         copy.start()
-    copies[0].wait()
-    for block in range(blocks):
-        start = min(max(own * block - SIDE, 0), columns - lanes)
-        send[block] = guess_in[:, start : start + lanes]
-    for copy in copies[1:]:
+    for slot in range(groups):
+        copies[slot].wait()
+        for chunk in range(chunks):
+            outs[slot][:, piece(chunk)] = shifted(lambda k: guess_in[slot, :, piece(k)], chunk, shifts[slot])
+    for copy in copies[groups:]:
         copy.wait()
     for slot in range(3):
-        for chunk in range(lanes // LANE):
-            coefs[slot, :, piece(chunk)] = shifted(lambda k: coefs_in[slot, :, piece(k)], chunk, ids[1])
+        for chunk in range(chunks):
+            coefs[slot, :, piece(chunk)] = shifted(lambda k: coefs_in[slot, :, piece(k)], chunk, shift)
 
     def fill(bottom, top):
         at = 0
@@ -150,17 +178,14 @@
         bottom[at:] = coarse[rows // 2 - COARSE_ROWS :]
         top[at:] = coarse[:COARSE_ROWS]
 
-    @pl.when(ids[2] == 1)
-    def _():
-        fill(halo_a, halo_b)
-
-    @pl.when(ids[2] == 0)
-    def _():
-        fill(halo_b, halo_a)
-
-
-def edge_kernel(ids, fields, edge_a, edge_b):
-    rows = fields.shape[1]
+    by_side(sides(rows)[0], fill, halo_a, halo_b)
+
+
+def edge_kernel(own, from_core, from_x, from_both, edge_a, edge_b, fields):
+    member = lax.axis_index("tm")
+    for slot, ref in enumerate((own, from_core, from_x, from_both)):
+        fields[member ^ slot] = ref[...]
+    rows = own.shape[0]
 
     def fill(bottom, top):
         at = 0
@@ -169,13 +194,7 @@
             top[at : at + deep] = fields[group, :deep]
             at += deep
 
-    @pl.when(ids[2] == 1)
-    def _():
-        fill(edge_a, edge_b)
-
-    @pl.when(ids[2] == 0)
-    def _():
-        fill(edge_b, edge_a)
+    by_side(sides(rows)[0], fill, edge_a, edge_b)
 
 
 def spread(value):
@@ -206,14 +225,14 @@
 
 
 def prepare_kernel(
-    ids, coefs, coarse, coef_a, coef_b,
+    coefs, coarse, coef_a, coef_b,
     cond_x, source, diagonal, up, east, west, coarse_x, coarse_d, coarse_u, coarse_e, coarse_w, error,
     cond_y, coarse_y, tall,
 ):
     rows, lanes = coefs.shape[1:]
     chunks = lanes // LANE
     low = HALO + rows
-    limit = jnp.where(ids[3] == 1, low, low + HALO)
+    even, limit = sides(rows)
     targets = (cond_x, cond_y, source)
 
     def assemble(upper, lower):
@@ -226,13 +245,7 @@
         tall[:COARSE_ROWS] = upper[at:]
         tall[COARSE_ROWS + rows // 2 :] = lower[at:]
 
-    @pl.when(ids[2] == 1)
-    def _():
-        assemble(coef_b, coef_a)
-
-    @pl.when(ids[2] == 0)
-    def _():
-        assemble(coef_a, coef_b)
+    by_side(even, lambda lower, upper: assemble(upper, lower), coef_a, coef_b)
 
     tall[COARSE_ROWS : COARSE_ROWS + rows // 2] = coarse[...]
     for slot, ref in enumerate(targets):
@@ -249,7 +262,9 @@
     high = rows // 2 + 2 * COARSE_ROWS
     half = lax.broadcasted_iota(jnp.int32, (8, LANE), 1) // 2
     twice = lax.broadcasted_iota(jnp.int32, (8, LANE), 0) // 2
-    first, shift = ids[5], ids[6]
+    groups, strips, member = lax.axis_size("tm"), lax.axis_size("space"), lax.axis_index("tm")
+    skip = place(groups, strips, groups * (lanes - 2 * SIDE), member)[3]
+    first, shift = skip // LANE, lax.rem(skip, LANE)
 
     def load(chunk):
         at = jnp.minimum((first + chunk) * LANE, lanes - LANE)
@@ -299,8 +314,8 @@
 
 
 def main_kernel(
-    ids, fields, cond_x, source, diagonal, up, east, west, coarse_x, coarse_d, coarse_u, coarse_e, coarse_w,
-    start_error, edge_a, edge_b, out,
+    fields, cond_x, source, diagonal, up, east, west, coarse_x, coarse_d, coarse_u, coarse_e, coarse_w,
+    start_error, edge_a, edge_b, own, to_core, to_x, to_both,
     guess, work, error,
 ):
     groups, rows, lanes = fields.shape
@@ -316,13 +331,7 @@
                 guess[group, chunk, low : low + deep] = lower[at : at + deep, piece(chunk)]
             at += deep
 
-    @pl.when(ids[2] == 1)
-    def _():
-        assemble(edge_b, edge_a)
-
-    @pl.when(ids[2] == 0)
-    def _():
-        assemble(edge_a, edge_b)
+    by_side(sides(rows)[0], lambda lower, upper: assemble(upper, lower), edge_a, edge_b)
 
     for group in range(given):
         for chunk in range(chunks):
@@ -360,23 +369,26 @@
 
         sweep(error.at[group - 1], error.at[group], reach(rows, 4), 2, coarse, residual)
 
-    @pl.loop(0, groups)
-    def _(group):
+    member = lax.axis_index("tm")
+    shift = place(groups, lax.axis_size("space"), groups * own.shape[1], member)[1]
+    for slot, out in enumerate((own, to_core, to_x, to_both)):
+        group = member ^ slot
         relaxed = jnp.where(group == 0, 0, given - 1 + group)
 
         def load(chunk):
             return guess[relaxed, chunk, HALO:low] + error[group, chunk, HALO:low]
 
         for chunk in range(chunks - 1):
-            out[group, :, piece(chunk)] = shifted(load, chunk, ids[1])
-
-
-def unpack_kernel(blocks, out, sems):
-    own = blocks.shape[2]
+            out[:, piece(chunk)] = shifted(load, chunk, shift)
+
+
+def unpack_kernel(own, from_core, from_x, from_both, out, sems):
+    width = own.shape[1]
+    member = lax.axis_index("tm")
     copies = []
-    for block in range(blocks.shape[0]):
-        target = out.at[0, :, block * own : (block + 1) * own]
-        copies.append(pltpu.make_async_copy(blocks.at[block], target, sems.at[block]))
+    for slot, ref in enumerate((own, from_core, from_x, from_both)):
+        at = pl.ds(pl.multiple_of((member ^ slot) * width, LANE), width)
+        copies.append(pltpu.make_async_copy(ref, out.at[0, :, at], sems.at[slot]))
     for copy in copies:
         copy.start()
     for copy in copies:
@@ -384,9 +396,10 @@
 
 
 def call(kernel, outs, scratch, operands, whole=(), outside=False, copies=0):
-    vmem, smem, anywhere = (pl.BlockSpec(memory_space=space) for space in (pltpu.VMEM, pltpu.SMEM, pltpu.HBM))
-    specs = [
-        anywhere if slot in whole else smem if value.dtype == jnp.int32 else vmem
+    vmem, anywhere = (pl.BlockSpec(memory_space=space) for space in (pltpu.VMEM, pltpu.HBM))
+    specs = [anywhere if slot in whole else vmem for slot in range(len(operands))]
+    operands = [
+        pltpu.with_memory_space_constraint(value, pltpu.HBM) if slot in whole else value
         for slot, value in enumerate(operands)
     ]
     return pl.pallas_call(
@@ -408,46 +421,43 @@
         return general_shards(guesses, cond_x, cond_y, source, inflow)
     own = columns // groups
     lanes = own + 2 * SIDE
-    chunks = lanes // LANE
-    member, strip = lax.axis_index("tm"), lax.axis_index("space")
-    start, around = window(member, own, columns, lanes)
-    coarse_start = jnp.minimum(start // 2 // LANE * LANE, columns // 2 - lanes)
-    coarse_skip = start // 2 - coarse_start
-    last = (strip == strips - 1).astype(jnp.int32)
-    ids = [around, start - around, 1 - strip % 2, last, coarse_start, coarse_skip // LANE, coarse_skip % LANE]
-    ids = jnp.stack([jnp.asarray(value, jnp.int32) for value in ids])
     pairs_a = [(i, i ^ 1) for i in range(strips)]
     pairs_b = [(i, j) for k in range(1, strips - 1, 2) for i, j in ((k, k + 1), (k + 1, k))]
 
+    def trade(blocks):
+        moved = [blocks[0]]
+        for slot in range(1, groups):
+            moved.append(lax.ppermute(blocks[slot], "tm", [(i, i ^ slot) for i in range(groups)]))
+        return moved
+
     travel = sum(COEF_ROWS) + COARSE_ROWS
-    send, halo_a, halo_b, coefs, coarse = call(
+    *blocks, halo_a, halo_b, coefs, coarse = call(
         pack_kernel,
-        [(groups, rows, lanes), (travel, lanes), (travel, lanes), (3, rows, lanes), (rows // 2, lanes)],
-        [(rows, columns), (3, rows, lanes + LANE)],
-        [ids, guesses[0], cond_x, cond_y, source, inflow], whole=range(1, 6), copies=5,
-    )
+        [(rows, lanes)] * groups + [(travel, lanes), (travel, lanes), (3, rows, lanes), (rows // 2, lanes)],
+        [(groups, rows, lanes + LANE), (3, rows, lanes + LANE)],
+        [guesses[0], cond_x, cond_y, source, inflow], whole=range(5), copies=groups + 4,
+    )
+    coef_a = lax.ppermute(halo_a, "space", pairs_a)
     coef_b = lax.ppermute(halo_b, "space", pairs_b)
-    coef_a = lax.ppermute(halo_a, "space", pairs_a)
-    fields = lax.all_to_all(send, "tm", 0, 0, tiled=True)
+    blocks = trade(blocks)
     deep = sum(FIELD_ROWS)
-    sent_a, sent_b = call(edge_kernel, [(deep, lanes)] * 2, [], [ids, fields])
+    sent_a, sent_b, fields = call(edge_kernel, [(deep, lanes)] * 2 + [(groups, rows, lanes)], [], blocks)
+    edge_a = lax.ppermute(sent_a, "space", pairs_a)
     edge_b = lax.ppermute(sent_b, "space", pairs_b)
-    edge_a = lax.ppermute(sent_a, "space", pairs_a)
-    buffer = (chunks, rows + 2 * HALO, LANE)
+    buffer = (lanes // LANE, rows + 2 * HALO, LANE)
     prepared = call(
         prepare_kernel,
         [buffer] * 12,
         [buffer, buffer, (rows // 2 + 2 * COARSE_ROWS, lanes)],
-        [ids, coefs, coarse, coef_a, coef_b],
-    )
-    (blocks,) = call(
+        [coefs, coarse, coef_a, coef_b],
+    )
+    blocks = call(
         main_kernel,
-        [(groups, rows, own)],
+        [(rows, own)] * groups,
         [(3 * groups - 4, *buffer), (2, *buffer), (groups, *buffer)],
-        [ids, fields, *prepared, edge_a, edge_b],
-    )
-    blocks = lax.all_to_all(blocks, "tm", 0, 0, tiled=True)
-    return call(unpack_kernel, [(1, rows, columns)], [], [blocks], outside=True, copies=groups)[0]
+        [fields, *prepared, edge_a, edge_b],
+    )
+    return call(unpack_kernel, [(1, rows, columns)], [], trade(blocks), outside=True, copies=groups)[0]
 
 
 def solution(mesh):

time: 39.8 us -> 29 us (0.73); the launches traced: 39 us -> 28.8 us
  blocking collectives: 9.68 us -> 0 us
  waiting for transfers between devices: 5.65 us -> 10.8 us
  local copies, waits for them, and re-layouts: 4.64 us -> 0 us
  Pallas kernels: 8.48 us -> 6.62 us
  starting transfers between devices: 10.5 us -> 11.3 us
    all_to_all x1 -> x0, blocking collectives: 9.68 us -> none  [shards(): blocks = lax.all_to_all(blocks, 'tm', 0, 0, tiled=True)]
    ppermute x0 -> x6, starting transfers between devices: none -> 4.71 us  [trade(): lax.ppermute(blocks[slot], 'tm', [(i, i ^ slot) for i in range(groups)])]
    ppermute x0 -> x6, waiting for transfers between devices: none -> 4.56 us  [trade(): lax.ppermute(blocks[slot], 'tm', [(i, i ^ slot) for i in range(groups)])]
    unnamed x10 -> x0, local copies, waits for them, and re-layouts: 4.55 us -> none
    all_to_all x1 -> x0, starting transfers between devices: 4.1 us -> none  [shards(): fields = lax.all_to_all(send, 'tm', 0, 0, tiled=True)]
    ppermute x1, waiting for transfers between devices: 1.54 us -> 4.94 us  [shards(): edge_a = lax.ppermute(sent_a, 'space', pairs_a)]
    all_to_all x1 -> x0, waiting for transfers between devices: 2.32 us -> none  [shards(): fields = lax.all_to_all(send, 'tm', 0, 0, tiled=True)]
    pallas_call x5, Pallas kernels: 8.48 us -> 6.62 us  [call(): pl.pallas_call(kernel, out_shape=[jax.ShapeDtypeStruct(shape, jnp.float32...]
  transfers between devices with their start and end apart: 5 -> 10, of which waited for: 3 -> 5; matrix products, arithmetic and copies ran while one was open for 0% -> 0% of each run, Pallas kernels for 4% -> 2%
where the time goes in v4:
time: 29 us; the launch traced here: 28.8 us
  starting transfers between devices  11.3 us (39%)
  waiting for transfers between devices  10.8 us (37%)
  Pallas kernels  6.62 us (23%)
    pallas_call x5, Pallas kernels, call(): pl.pallas_call(kernel, out_shape=[jax.ShapeDtypeStruct(shape, jnp.float32...  6.62 us
    ppermute x1, waiting for transfers between devices, shards(): edge_a = lax.ppermute(sent_a, 'space', pairs_a)  4.94 us
    ppermute x6, starting transfers between devices, trade(): lax.ppermute(blocks[slot], 'tm', [(i, i ^ slot) for i in range(groups)])  4.71 us
    ppermute x6, waiting for transfers between devices, trade(): lax.ppermute(blocks[slot], 'tm', [(i, i ^ slot) for i in range(groups)])  4.56 us
    ppermute x1, starting transfers between devices, shards(): coef_b = lax.ppermute(halo_b, 'space', pairs_b)  1.91 us
    ppermute x1, starting transfers between devices, shards(): edge_b = lax.ppermute(sent_b, 'space', pairs_b)  1.91 us
    ppermute x1, starting transfers between devices, shards(): edge_a = lax.ppermute(sent_a, 'space', pairs_a)  1.55 us
    ppermute x1, waiting for transfers between devices, shards(): coef_b = lax.ppermute(halo_b, 'space', pairs_b)  1.32 us
  transfers between devices with their start and end apart: 10, of which 5 were waited for; matrix products, arithmetic and copies ran while one was open for 0% of the time, Pallas kernels for 2%

profile of v4, /device:TPU:9, one launch (start us, length us, event | category | flops | bytes accessed | tf_op | source)
XLA Modules:
  0.0 28.8 jit_solution(5797414463000474191)
XLA Ops:
  0.0 1.6 %shard_map.55 = (f32[16,1152]{1,0:T(8,128)S(1)}, f32[16,1152]{1,0:T(8,128)S(1)}, f32[16,1152]{1,0:T(8,128)S(1)}, f32[16,1152]{1,0:T(8,128)S(1)}, f32[32,1152]{1,...) custom-call(f32[16,4096]{1,0:T(8,128)} %bitcast.1, f32[16,4096]{1,0:T(8,128)} %cond_x.1, ...), custom_call_target="tpu_custom_call" | custom-call | tf_op jit(solution)/shard_map/pallas_call | solution.py:405
  1.6 0.7 %collective-permute-start = (f32[16,1152]{1,0:T(8,128)S(1)}, f32[16,1152]{1,0:T(8,128)S(1)}, u32[]{:S(2)}, u32[]{:S(2)}) collective-permute-start(f32[16,1152]{1,0:T(8,128)S(1)} %get-tuple-element.33), channel_id=1, source_target_pairs={{0,8},{8,0},{16,24},{24,16},{1,9},{9,1},{17,25},{25,17},{2,10},{10... | collective-permute-start | bytes 221192 | tf_op jit(solution)/shard_map/ppermute | solution.py:430
  2.4 1.2 %collective-permute-start.1 = (f32[16,1152]{1,0:T(8,128)S(1)}, f32[16,1152]{1,0:T(8,128)S(1)}, u32[]{:S(2)}, u32[]{:S(2)}) collective-permute-start(f32[16,1152]{1,0:T(8,128)S(1)} %get-tuple-element.34), channel_id=1, source_target_pairs={{0,16},{8,24},{16,0},{24,8},{1,17},{9,25},{17,1},{25,9},{2,18},{10... | collective-permute-start | bytes 221192 | tf_op jit(solution)/shard_map/ppermute | solution.py:430
  3.6 0.5 %collective-permute-start.2 = (f32[16,1152]{1,0:T(8,128)S(1)}, f32[16,1152]{1,0:T(8,128)S(1)}, u32[]{:S(2)}, u32[]{:S(2)}) collective-permute-start(f32[16,1152]{1,0:T(8,128)S(1)} %get-tuple-element.35), channel_id=1, source_target_pairs={{0,24},{8,16},{16,8},{24,0},{1,25},{9,17},{17,9},{25,1},{2,26},{10... | collective-permute-start | bytes 221192 | tf_op jit(solution)/shard_map/ppermute | solution.py:430
  4.1 1.2 %collective-permute-start.3 = (f32[32,1152]{1,0:T(8,128)S(1)}, f32[32,1152]{1,0:T(8,128)S(1)}, u32[]{:S(2)}, u32[]{:S(2)}) collective-permute-start(f32[32,1152]{1,0:T(8,128)S(1)} %get-tuple-element.39), channel_id=1, source_target_pairs={{0,1},{1,0},{2,3},{3,2},{4,5},{5,4},{6,7},{7,6},{8,9},{9,8},{10,11... | collective-permute-start | bytes 442376 | tf_op jit(solution)/shard_map/ppermute | solution.py:440
  5.3 1.9 %collective-permute-start.4 = (f32[32,1152]{1,0:T(8,128)S(1)}, f32[32,1152]{1,0:T(8,128)S(1)}, u32[]{:S(2)}, u32[]{:S(2)}) collective-permute-start(f32[32,1152]{1,0:T(8,128)S(1)} %get-tuple-element.40), channel_id=1, source_target_pairs={{1,2},{2,1},{3,4},{4,3},{5,6},{6,5},{9,10},{10,9},{11,12},{12,11},... | collective-permute-start | bytes 442376 | tf_op jit(solution)/shard_map/ppermute | solution.py:441
  7.2 0.0 collective-permute-done.from_core
  7.3 0.0 collective-permute-done.1.from_x
  7.3 1.0 %collective-permute-done.2.from_both = f32[16,1152]{1,0:T(8,128)S(1)} collective-permute-done((f32[16,1152]{1,0:T(8,128)S(1)}, f32[16,1152]{1,0:T(8,128)S(1)}, u32[]{:S(2)}, u32[]{:S(2)}) %collective-permute-start.2) | collective-permute-done | bytes 73760 | tf_op jit(solution)/shard_map/ppermute | solution.py:430
  8.3 0.1 shard_map.56
  8.3 1.6 %collective-permute-start.5 = (f32[24,1152]{1,0:T(8,128)S(1)}, f32[24,1152]{1,0:T(8,128)S(1)}, u32[]{:S(2)}, u32[]{:S(2)}) collective-permute-start(f32[24,1152]{1,0:T(8,128)S(1)} %get-tuple-element.53), channel_id=1, source_target_pairs={{0,1},{1,0},{2,3},{3,2},{4,5},{5,4},{6,7},{7,6},{8,9},{9,8},{10,11... | collective-permute-start | bytes 331784 | tf_op jit(solution)/shard_map/ppermute | solution.py:445
  9.9 1.9 %collective-permute-start.6 = (f32[24,1152]{1,0:T(8,128)S(1)}, f32[24,1152]{1,0:T(8,128)S(1)}, u32[]{:S(2)}, u32[]{:S(2)}) collective-permute-start(f32[24,1152]{1,0:T(8,128)S(1)} %get-tuple-element.54), channel_id=1, source_target_pairs={{1,2},{2,1},{3,4},{4,3},{5,6},{6,5},{9,10},{10,9},{11,12},{12,11},... | collective-permute-start | bytes 331784 | tf_op jit(solution)/shard_map/ppermute | solution.py:446
  11.8 0.0 collective-permute-done.3.coef_a
  11.8 1.3 %collective-permute-done.4.coef_b = f32[32,1152]{1,0:T(8,128)S(1)} collective-permute-done((f32[32,1152]{1,0:T(8,128)S(1)}, f32[32,1152]{1,0:T(8,128)S(1)}, u32[]{:S(2)}, u32[]{:S(2)}) %collective-permute-start.4) | collective-permute-done | bytes 147488 | tf_op jit(solution)/shard_map/ppermute | solution.py:441
  13.1 0.6 %shard_map.57 = (f32[9,48,128]{2,1,0:T(8,128)S(1)}, f32[9,48,128]{2,1,0:T(8,128)S(1)}, f32[9,48,128]{2,1,0:T(8,128)S(1)}, f32[9,48,128]{2,1,0:T(8,128)S(1)}, f32...) custom-call(f32[3,16,1152]{2,1,0:T(8,128)S(1)} %get-tuple-element.37, ...), custom_call_target="tpu_custom_call" | custom-call | tf_op jit(solution)/shard_map/pallas_call | solution.py:405
  13.7 4.9 %collective-permute-done.5.edge_a = f32[24,1152]{1,0:T(8,128)S(1)} collective-permute-done((f32[24,1152]{1,0:T(8,128)S(1)}, f32[24,1152]{1,0:T(8,128)S(1)}, u32[]{:S(2)}, u32[]{:S(2)}) %collective-permute-start.5) | collective-permute-done | bytes 110624 | tf_op jit(solution)/shard_map/ppermute | solution.py:445
  18.6 0.0 collective-permute-done.6.edge_b
  18.6 3.6 %shard_map.58 = (f32[16,1024]{1,0:T(8,128)S(1)}, f32[16,1024]{1,0:T(8,128)S(1)}, f32[16,1024]{1,0:T(8,128)S(1)}, f32[16,1024]{1,0:T(8,128)S(1)}) custom-call(f32[4,16,1152]{2,1,0:T(8,128)S(1)} %get-tuple-element.36.fields, f32[9,48,128]{2,1,0:T(8,128)S(1)} %get-tuple-element.41.cond_x, f32[9,48,128]{2,1,0:T(8,128)S(1)} %get-tuple-element.42.source, ...), custom_call_target="tpu_custom_call" | custom-call | tf_op jit(solution)/shard_map/pallas_call | solution.py:405
  22.3 0.5 %collective-permute-start.7 = (f32[16,1024]{1,0:T(8,128)S(1)}, f32[16,1024]{1,0:T(8,128)S(1)}, u32[]{:S(2)}, u32[]{:S(2)}) collective-permute-start(f32[16,1024]{1,0:T(8,128)S(1)} %get-tuple-element.56), channel_id=1, source_target_pairs={{0,8},{8,0},{16,24},{24,16},{1,9},{9,1},{17,25},{25,17},{2,10},{10... | collective-permute-start | bytes 196616 | tf_op jit(solution)/shard_map/ppermute | solution.py:430
  22.8 1.2 %collective-permute-start.8 = (f32[16,1024]{1,0:T(8,128)S(1)}, f32[16,1024]{1,0:T(8,128)S(1)}, u32[]{:S(2)}, u32[]{:S(2)}) collective-permute-start(f32[16,1024]{1,0:T(8,128)S(1)} %get-tuple-element.57), channel_id=1, source_target_pairs={{0,16},{8,24},{16,0},{24,8},{1,17},{9,25},{17,1},{25,9},{2,18},{10... | collective-permute-start | bytes 196616 | tf_op jit(solution)/shard_map/ppermute | solution.py:430
  24.1 0.5 %collective-permute-start.9 = (f32[16,1024]{1,0:T(8,128)S(1)}, f32[16,1024]{1,0:T(8,128)S(1)}, u32[]{:S(2)}, u32[]{:S(2)}) collective-permute-start(f32[16,1024]{1,0:T(8,128)S(1)} %get-tuple-element.58), channel_id=1, source_target_pairs={{0,24},{8,16},{16,8},{24,0},{1,25},{9,17},{17,9},{25,1},{2,26},{10... | collective-permute-start | bytes 196616 | tf_op jit(solution)/shard_map/ppermute | solution.py:430
  24.5 2.0 %collective-permute-done.8.from_x = f32[16,1024]{1,0:T(8,128)S(1)} collective-permute-done((f32[16,1024]{1,0:T(8,128)S(1)}, f32[16,1024]{1,0:T(8,128)S(1)}, u32[]{:S(2)}, u32[]{:S(2)}) %collective-permute-start.8) | collective-permute-done | bytes 65568 | tf_op jit(solution)/shard_map/ppermute | solution.py:430
  26.5 1.6 %collective-permute-done.9.from_both = f32[16,1024]{1,0:T(8,128)S(1)} collective-permute-done((f32[16,1024]{1,0:T(8,128)S(1)}, f32[16,1024]{1,0:T(8,128)S(1)}, u32[]{:S(2)}, u32[]{:S(2)}) %collective-permute-start.9) | collective-permute-done | bytes 65568 | tf_op jit(solution)/shard_map/ppermute | solution.py:430
  28.1 0.7 %shard_map.59 = f32[1,16,4096]{2,1,0:T(8,128)} custom-call(f32[16,1024]{1,0:T(8,128)S(1)} %get-tuple-element.55.own, f32[16,1024]{1,0:T(8,128)S(1)} %collective-permute-done.7.from_core, f32[16,1024]{1,0:T(8,128)S(1)} %collective-permute-done.8.from_x, f32[16,1024]{1,0:T(8,128)S(1)} %collective-permute-done.9.from_both), custom_call_target="tpu_custom_call" | custom-call | tf_op jit(solution)/shard_map/pallas_call | solution.py:405
  (1 shorter events, 0.0 us)
Async XLA Ops:
  1.6 5.6 %collective-permute-start = (f32[16,1152]{1,0:T(8,128)S(1)}, f32[16,1152]{1,0:T(8,128)S(1)}, u32[]{:S(2)}, u32[]{:S(2)}) collective-permute-start(f32[16,1152]{1,0:T(8,128)S(1)} %get-tuple-element.33), channel_id=1, source_target_pairs={{0,8},{8,0},{16,24},{24,16},{1,9},{9,1},{17,25},{25,17},{2,10},{10... | collective-permute-start | bytes 221192 | tf_op jit(solution)/shard_map/ppermute | solution.py:430
  2.4 4.9 %collective-permute-start.1 = (f32[16,1152]{1,0:T(8,128)S(1)}, f32[16,1152]{1,0:T(8,128)S(1)}, u32[]{:S(2)}, u32[]{:S(2)}) collective-permute-start(f32[16,1152]{1,0:T(8,128)S(1)} %get-tuple-element.34), channel_id=1, source_target_pairs={{0,16},{8,24},{16,0},{24,8},{1,17},{9,25},{17,1},{25,9},{2,18},{10... | collective-permute-start | bytes 221192 | tf_op jit(solution)/shard_map/ppermute | solution.py:430
  3.6 4.7 %collective-permute-start.2 = (f32[16,1152]{1,0:T(8,128)S(1)}, f32[16,1152]{1,0:T(8,128)S(1)}, u32[]{:S(2)}, u32[]{:S(2)}) collective-permute-start(f32[16,1152]{1,0:T(8,128)S(1)} %get-tuple-element.35), channel_id=1, source_target_pairs={{0,24},{8,16},{16,8},{24,0},{1,25},{9,17},{17,9},{25,1},{2,26},{10... | collective-permute-start | bytes 221192 | tf_op jit(solution)/shard_map/ppermute | solution.py:430
  4.1 7.7 %collective-permute-start.3 = (f32[32,1152]{1,0:T(8,128)S(1)}, f32[32,1152]{1,0:T(8,128)S(1)}, u32[]{:S(2)}, u32[]{:S(2)}) collective-permute-start(f32[32,1152]{1,0:T(8,128)S(1)} %get-tuple-element.39), channel_id=1, source_target_pairs={{0,1},{1,0},{2,3},{3,2},{4,5},{5,4},{6,7},{7,6},{8,9},{9,8},{10,11... | collective-permute-start | bytes 442376 | tf_op jit(solution)/shard_map/ppermute | solution.py:440
  5.3 7.8 %collective-permute-start.4 = (f32[32,1152]{1,0:T(8,128)S(1)}, f32[32,1152]{1,0:T(8,128)S(1)}, u32[]{:S(2)}, u32[]{:S(2)}) collective-permute-start(f32[32,1152]{1,0:T(8,128)S(1)} %get-tuple-element.40), channel_id=1, source_target_pairs={{1,2},{2,1},{3,4},{4,3},{5,6},{6,5},{9,10},{10,9},{11,12},{12,11},... | collective-permute-start | bytes 442376 | tf_op jit(solution)/shard_map/ppermute | solution.py:441
  8.3 10.3 %collective-permute-start.5 = (f32[24,1152]{1,0:T(8,128)S(1)}, f32[24,1152]{1,0:T(8,128)S(1)}, u32[]{:S(2)}, u32[]{:S(2)}) collective-permute-start(f32[24,1152]{1,0:T(8,128)S(1)} %get-tuple-element.53), channel_id=1, source_target_pairs={{0,1},{1,0},{2,3},{3,2},{4,5},{5,4},{6,7},{7,6},{8,9},{9,8},{10,11... | collective-permute-start | bytes 331784 | tf_op jit(solution)/shard_map/ppermute | solution.py:445
  9.9 8.8 %collective-permute-start.6 = (f32[24,1152]{1,0:T(8,128)S(1)}, f32[24,1152]{1,0:T(8,128)S(1)}, u32[]{:S(2)}, u32[]{:S(2)}) collective-permute-start(f32[24,1152]{1,0:T(8,128)S(1)} %get-tuple-element.54), channel_id=1, source_target_pairs={{1,2},{2,1},{3,4},{4,3},{5,6},{6,5},{9,10},{10,9},{11,12},{12,11},... | collective-permute-start | bytes 331784 | tf_op jit(solution)/shard_map/ppermute | solution.py:446
  22.3 2.3 %collective-permute-start.7 = (f32[16,1024]{1,0:T(8,128)S(1)}, f32[16,1024]{1,0:T(8,128)S(1)}, u32[]{:S(2)}, u32[]{:S(2)}) collective-permute-start(f32[16,1024]{1,0:T(8,128)S(1)} %get-tuple-element.56), channel_id=1, source_target_pairs={{0,8},{8,0},{16,24},{24,16},{1,9},{9,1},{17,25},{25,17},{2,10},{10... | collective-permute-start | bytes 196616 | tf_op jit(solution)/shard_map/ppermute | solution.py:430
  22.8 3.7 %collective-permute-start.8 = (f32[16,1024]{1,0:T(8,128)S(1)}, f32[16,1024]{1,0:T(8,128)S(1)}, u32[]{:S(2)}, u32[]{:S(2)}) collective-permute-start(f32[16,1024]{1,0:T(8,128)S(1)} %get-tuple-element.57), channel_id=1, source_target_pairs={{0,16},{8,24},{16,0},{24,8},{1,17},{9,25},{17,1},{25,9},{2,18},{10... | collective-permute-start | bytes 196616 | tf_op jit(solution)/shard_map/ppermute | solution.py:430
  24.1 4.0 %collective-permute-start.9 = (f32[16,1024]{1,0:T(8,128)S(1)}, f32[16,1024]{1,0:T(8,128)S(1)}, u32[]{:S(2)}, u32[]{:S(2)}) collective-permute-start(f32[16,1024]{1,0:T(8,128)S(1)} %get-tuple-element.58), channel_id=1, source_target_pairs={{0,24},{8,16},{16,8},{24,0},{1,25},{9,17},{17,9},{25,1},{2,26},{10... | collective-permute-start | bytes 196616 | tf_op jit(solution)/shard_map/ppermute | solution.py:430

commit v5 on v4

--- a/solution.py
+++ b/solution.py
@@ -345,29 +345,25 @@
     def add_source(chunk, here):
         return source[chunk, here]
 
-    def propagate(slot, deep):
-        stops = [guess.at[slot], work.at[0], work.at[1], work.at[0], guess.at[slot + given]]
+    def propagate(slots, deeps):
         for number in range(FINE_STEPS):
-            reached = reach(rows, deep + FINE_STEPS - 1 - number)
-            sweep(stops[number], stops[number + 1], reached, 1, fine, add_source)
-
-    @pl.loop(0, given)
-    def _(group):
-        propagate(group, 6)
-
-    @pl.loop(given, 2 * given - 1)
-    def _(group):
-        propagate(group, 2)
-
-    @pl.loop(1, groups)
-    def _(group):
-        reached = jnp.where(group == 1, given, 2 * given - 2 + group)
+            for lane, (slot, deep) in enumerate(zip(slots, deeps)):
+                first, second = work.at[2 * lane], work.at[2 * lane + 1]
+                stops = [guess.at[slot], first, second, first, guess.at[slot + given]]
+                reached = reach(rows, deep + FINE_STEPS - 1 - number)
+                sweep(stops[number], stops[number + 1], reached, 1, fine, add_source)
+
+    propagate((0, 1, 2), (6, 4, 0))
+    propagate((3, 4), (2, 0))
+
+    for group in range(1, groups):
+        reached = given if group == 1 else 2 * given - 2 + group
         relaxed = given - 1 + group
 
-        def residual(chunk, here):
+        def residual(chunk, here, reached=reached, relaxed=relaxed):
             return spread(guess[reached, chunk, here] - guess[relaxed, chunk, here])
 
-        sweep(error.at[group - 1], error.at[group], reach(rows, 4), 2, coarse, residual)
+        sweep(error.at[group - 1], error.at[group], reach(rows, 2 * (groups - 1 - group)), 2, coarse, residual)
 
     member = lax.axis_index("tm")
     shift = place(groups, lax.axis_size("space"), groups * own.shape[1], member)[1]
@@ -454,7 +450,7 @@
     blocks = call(
         main_kernel,
         [(rows, own)] * groups,
-        [(3 * groups - 4, *buffer), (2, *buffer), (groups, *buffer)],
+        [(3 * groups - 4, *buffer), (2 * groups - 2, *buffer), (groups, *buffer)],
         [fields, *prepared, edge_a, edge_b],
     )
     return call(unpack_kernel, [(1, rows, columns)], [], trade(blocks), outside=True, copies=groups)[0]

time: 29 us -> 28 us (0.966)
  Pallas kernels: 6.62 us -> 5.57 us
    pallas_call x5, Pallas kernels: 6.62 us -> 5.57 us  [call(): pl.pallas_call(kernel, out_shape=[jax.ShapeDtypeStruct(shape, jnp.float32...]
where the time goes in v5:
time: 28 us; the launch traced here: 27.8 us
  starting transfers between devices  11.3 us (40%)
  waiting for transfers between devices  10.8 us (39%)
  Pallas kernels  5.57 us (20%)
    pallas_call x5, Pallas kernels, call(): pl.pallas_call(kernel, out_shape=[jax.ShapeDtypeStruct(shape, jnp.float32...  5.57 us
    ppermute x1, waiting for transfers between devices, shards(): edge_a = lax.ppermute(sent_a, 'space', pairs_a)  4.94 us
    ppermute x6, starting transfers between devices, trade(): lax.ppermute(blocks[slot], 'tm', [(i, i ^ slot) for i in range(groups)])  4.71 us
    ppermute x6, waiting for transfers between devices, trade(): lax.ppermute(blocks[slot], 'tm', [(i, i ^ slot) for i in range(groups)])  4.56 us
    ppermute x1, starting transfers between devices, shards(): coef_b = lax.ppermute(halo_b, 'space', pairs_b)  1.91 us
    ppermute x1, starting transfers between devices, shards(): edge_b = lax.ppermute(sent_b, 'space', pairs_b)  1.91 us
    ppermute x1, starting transfers between devices, shards(): edge_a = lax.ppermute(sent_a, 'space', pairs_a)  1.55 us
    ppermute x1, waiting for transfers between devices, shards(): coef_b = lax.ppermute(halo_b, 'space', pairs_b)  1.32 us
  transfers between devices with their start and end apart: 10, of which 5 were waited for; matrix products, arithmetic and copies ran while one was open for 0% of the time, Pallas kernels for 2%

profile of v5, /device:TPU:9, one launch (start us, length us, event | category | flops | bytes accessed | tf_op | source)
XLA Modules:
  0.0 27.8 jit_solution(11990155574109548888)
XLA Ops:
  0.0 1.6 %shard_map.55 = (f32[16,1152]{1,0:T(8,128)S(1)}, f32[16,1152]{1,0:T(8,128)S(1)}, f32[16,1152]{1,0:T(8,128)S(1)}, f32[16,1152]{1,0:T(8,128)S(1)}, f32[32,1152]{1,...) custom-call(f32[16,4096]{1,0:T(8,128)} %bitcast.1, f32[16,4096]{1,0:T(8,128)} %cond_x.1, ...), custom_call_target="tpu_custom_call" | custom-call | tf_op jit(solution)/shard_map/pallas_call | solution.py:401
  1.6 0.7 %collective-permute-start = (f32[16,1152]{1,0:T(8,128)S(1)}, f32[16,1152]{1,0:T(8,128)S(1)}, u32[]{:S(2)}, u32[]{:S(2)}) collective-permute-start(f32[16,1152]{1,0:T(8,128)S(1)} %get-tuple-element.33), channel_id=1, source_target_pairs={{0,8},{8,0},{16,24},{24,16},{1,9},{9,1},{17,25},{25,17},{2,10},{10... | collective-permute-start | bytes 221192 | tf_op jit(solution)/shard_map/ppermute | solution.py:426
  2.4 1.2 %collective-permute-start.1 = (f32[16,1152]{1,0:T(8,128)S(1)}, f32[16,1152]{1,0:T(8,128)S(1)}, u32[]{:S(2)}, u32[]{:S(2)}) collective-permute-start(f32[16,1152]{1,0:T(8,128)S(1)} %get-tuple-element.34), channel_id=1, source_target_pairs={{0,16},{8,24},{16,0},{24,8},{1,17},{9,25},{17,1},{25,9},{2,18},{10... | collective-permute-start | bytes 221192 | tf_op jit(solution)/shard_map/ppermute | solution.py:426
  3.6 0.5 %collective-permute-start.2 = (f32[16,1152]{1,0:T(8,128)S(1)}, f32[16,1152]{1,0:T(8,128)S(1)}, u32[]{:S(2)}, u32[]{:S(2)}) collective-permute-start(f32[16,1152]{1,0:T(8,128)S(1)} %get-tuple-element.35), channel_id=1, source_target_pairs={{0,24},{8,16},{16,8},{24,0},{1,25},{9,17},{17,9},{25,1},{2,26},{10... | collective-permute-start | bytes 221192 | tf_op jit(solution)/shard_map/ppermute | solution.py:426
  4.1 1.2 %collective-permute-start.3 = (f32[32,1152]{1,0:T(8,128)S(1)}, f32[32,1152]{1,0:T(8,128)S(1)}, u32[]{:S(2)}, u32[]{:S(2)}) collective-permute-start(f32[32,1152]{1,0:T(8,128)S(1)} %get-tuple-element.39), channel_id=1, source_target_pairs={{0,1},{1,0},{2,3},{3,2},{4,5},{5,4},{6,7},{7,6},{8,9},{9,8},{10,11... | collective-permute-start | bytes 442376 | tf_op jit(solution)/shard_map/ppermute | solution.py:436
  5.3 1.9 %collective-permute-start.4 = (f32[32,1152]{1,0:T(8,128)S(1)}, f32[32,1152]{1,0:T(8,128)S(1)}, u32[]{:S(2)}, u32[]{:S(2)}) collective-permute-start(f32[32,1152]{1,0:T(8,128)S(1)} %get-tuple-element.40), channel_id=1, source_target_pairs={{1,2},{2,1},{3,4},{4,3},{5,6},{6,5},{9,10},{10,9},{11,12},{12,11},... | collective-permute-start | bytes 442376 | tf_op jit(solution)/shard_map/ppermute | solution.py:437
  7.2 0.0 collective-permute-done.from_core
  7.3 0.0 collective-permute-done.1.from_x
  7.3 1.0 %collective-permute-done.2.from_both = f32[16,1152]{1,0:T(8,128)S(1)} collective-permute-done((f32[16,1152]{1,0:T(8,128)S(1)}, f32[16,1152]{1,0:T(8,128)S(1)}, u32[]{:S(2)}, u32[]{:S(2)}) %collective-permute-start.2) | collective-permute-done | bytes 73760 | tf_op jit(solution)/shard_map/ppermute | solution.py:426
  8.3 0.1 shard_map.56
  8.3 1.6 %collective-permute-start.5 = (f32[24,1152]{1,0:T(8,128)S(1)}, f32[24,1152]{1,0:T(8,128)S(1)}, u32[]{:S(2)}, u32[]{:S(2)}) collective-permute-start(f32[24,1152]{1,0:T(8,128)S(1)} %get-tuple-element.53), channel_id=1, source_target_pairs={{0,1},{1,0},{2,3},{3,2},{4,5},{5,4},{6,7},{7,6},{8,9},{9,8},{10,11... | collective-permute-start | bytes 331784 | tf_op jit(solution)/shard_map/ppermute | solution.py:441
  9.9 1.9 %collective-permute-start.6 = (f32[24,1152]{1,0:T(8,128)S(1)}, f32[24,1152]{1,0:T(8,128)S(1)}, u32[]{:S(2)}, u32[]{:S(2)}) collective-permute-start(f32[24,1152]{1,0:T(8,128)S(1)} %get-tuple-element.54), channel_id=1, source_target_pairs={{1,2},{2,1},{3,4},{4,3},{5,6},{6,5},{9,10},{10,9},{11,12},{12,11},... | collective-permute-start | bytes 331784 | tf_op jit(solution)/shard_map/ppermute | solution.py:442
  11.8 0.0 collective-permute-done.3.coef_a
  11.8 1.3 %collective-permute-done.4.coef_b = f32[32,1152]{1,0:T(8,128)S(1)} collective-permute-done((f32[32,1152]{1,0:T(8,128)S(1)}, f32[32,1152]{1,0:T(8,128)S(1)}, u32[]{:S(2)}, u32[]{:S(2)}) %collective-permute-start.4) | collective-permute-done | bytes 147488 | tf_op jit(solution)/shard_map/ppermute | solution.py:437
  13.1 0.6 %shard_map.57 = (f32[9,48,128]{2,1,0:T(8,128)S(1)}, f32[9,48,128]{2,1,0:T(8,128)S(1)}, f32[9,48,128]{2,1,0:T(8,128)S(1)}, f32[9,48,128]{2,1,0:T(8,128)S(1)}, f32...) custom-call(f32[3,16,1152]{2,1,0:T(8,128)S(1)} %get-tuple-element.37, ...), custom_call_target="tpu_custom_call" | custom-call | tf_op jit(solution)/shard_map/pallas_call | solution.py:401
  13.7 4.9 %collective-permute-done.5.edge_a = f32[24,1152]{1,0:T(8,128)S(1)} collective-permute-done((f32[24,1152]{1,0:T(8,128)S(1)}, f32[24,1152]{1,0:T(8,128)S(1)}, u32[]{:S(2)}, u32[]{:S(2)}) %collective-permute-start.5) | collective-permute-done | bytes 110624 | tf_op jit(solution)/shard_map/ppermute | solution.py:441
  18.6 0.0 collective-permute-done.6.edge_b
  18.6 2.6 %shard_map.58 = (f32[16,1024]{1,0:T(8,128)S(1)}, f32[16,1024]{1,0:T(8,128)S(1)}, f32[16,1024]{1,0:T(8,128)S(1)}, f32[16,1024]{1,0:T(8,128)S(1)}) custom-call(f32[4,16,1152]{2,1,0:T(8,128)S(1)} %get-tuple-element.36.fields, f32[9,48,128]{2,1,0:T(8,128)S(1)} %get-tuple-element.41.cond_x, f32[9,48,128]{2,1,0:T(8,128)S(1)} %get-tuple-element.42.source, ...), custom_call_target="tpu_custom_call" | custom-call | tf_op jit(solution)/shard_map/pallas_call | solution.py:401
  21.2 0.5 %collective-permute-start.7 = (f32[16,1024]{1,0:T(8,128)S(1)}, f32[16,1024]{1,0:T(8,128)S(1)}, u32[]{:S(2)}, u32[]{:S(2)}) collective-permute-start(f32[16,1024]{1,0:T(8,128)S(1)} %get-tuple-element.56), channel_id=1, source_target_pairs={{0,8},{8,0},{16,24},{24,16},{1,9},{9,1},{17,25},{25,17},{2,10},{10... | collective-permute-start | bytes 196616 | tf_op jit(solution)/shard_map/ppermute | solution.py:426
  21.8 1.2 %collective-permute-start.8 = (f32[16,1024]{1,0:T(8,128)S(1)}, f32[16,1024]{1,0:T(8,128)S(1)}, u32[]{:S(2)}, u32[]{:S(2)}) collective-permute-start(f32[16,1024]{1,0:T(8,128)S(1)} %get-tuple-element.57), channel_id=1, source_target_pairs={{0,16},{8,24},{16,0},{24,8},{1,17},{9,25},{17,1},{25,9},{2,18},{10... | collective-permute-start | bytes 196616 | tf_op jit(solution)/shard_map/ppermute | solution.py:426
  23.0 0.5 %collective-permute-start.9 = (f32[16,1024]{1,0:T(8,128)S(1)}, f32[16,1024]{1,0:T(8,128)S(1)}, u32[]{:S(2)}, u32[]{:S(2)}) collective-permute-start(f32[16,1024]{1,0:T(8,128)S(1)} %get-tuple-element.58), channel_id=1, source_target_pairs={{0,24},{8,16},{16,8},{24,0},{1,25},{9,17},{17,9},{25,1},{2,26},{10... | collective-permute-start | bytes 196616 | tf_op jit(solution)/shard_map/ppermute | solution.py:426
  23.5 2.0 %collective-permute-done.8.from_x = f32[16,1024]{1,0:T(8,128)S(1)} collective-permute-done((f32[16,1024]{1,0:T(8,128)S(1)}, f32[16,1024]{1,0:T(8,128)S(1)}, u32[]{:S(2)}, u32[]{:S(2)}) %collective-permute-start.8) | collective-permute-done | bytes 65568 | tf_op jit(solution)/shard_map/ppermute | solution.py:426
  25.5 1.6 %collective-permute-done.9.from_both = f32[16,1024]{1,0:T(8,128)S(1)} collective-permute-done((f32[16,1024]{1,0:T(8,128)S(1)}, f32[16,1024]{1,0:T(8,128)S(1)}, u32[]{:S(2)}, u32[]{:S(2)}) %collective-permute-start.9) | collective-permute-done | bytes 65568 | tf_op jit(solution)/shard_map/ppermute | solution.py:426
  27.1 0.7 %shard_map.59 = f32[1,16,4096]{2,1,0:T(8,128)} custom-call(f32[16,1024]{1,0:T(8,128)S(1)} %get-tuple-element.55.own, f32[16,1024]{1,0:T(8,128)S(1)} %collective-permute-done.7.from_core, f32[16,1024]{1,0:T(8,128)S(1)} %collective-permute-done.8.from_x, f32[16,1024]{1,0:T(8,128)S(1)} %collective-permute-done.9.from_both), custom_call_target="tpu_custom_call" | custom-call | tf_op jit(solution)/shard_map/pallas_call | solution.py:401
  (1 shorter events, 0.0 us)
Async XLA Ops:
  1.6 5.6 %collective-permute-start = (f32[16,1152]{1,0:T(8,128)S(1)}, f32[16,1152]{1,0:T(8,128)S(1)}, u32[]{:S(2)}, u32[]{:S(2)}) collective-permute-start(f32[16,1152]{1,0:T(8,128)S(1)} %get-tuple-element.33), channel_id=1, source_target_pairs={{0,8},{8,0},{16,24},{24,16},{1,9},{9,1},{17,25},{25,17},{2,10},{10... | collective-permute-start | bytes 221192 | tf_op jit(solution)/shard_map/ppermute | solution.py:426
  2.4 4.9 %collective-permute-start.1 = (f32[16,1152]{1,0:T(8,128)S(1)}, f32[16,1152]{1,0:T(8,128)S(1)}, u32[]{:S(2)}, u32[]{:S(2)}) collective-permute-start(f32[16,1152]{1,0:T(8,128)S(1)} %get-tuple-element.34), channel_id=1, source_target_pairs={{0,16},{8,24},{16,0},{24,8},{1,17},{9,25},{17,1},{25,9},{2,18},{10... | collective-permute-start | bytes 221192 | tf_op jit(solution)/shard_map/ppermute | solution.py:426
  3.6 4.7 %collective-permute-start.2 = (f32[16,1152]{1,0:T(8,128)S(1)}, f32[16,1152]{1,0:T(8,128)S(1)}, u32[]{:S(2)}, u32[]{:S(2)}) collective-permute-start(f32[16,1152]{1,0:T(8,128)S(1)} %get-tuple-element.35), channel_id=1, source_target_pairs={{0,24},{8,16},{16,8},{24,0},{1,25},{9,17},{17,9},{25,1},{2,26},{10... | collective-permute-start | bytes 221192 | tf_op jit(solution)/shard_map/ppermute | solution.py:426
  4.1 7.7 %collective-permute-start.3 = (f32[32,1152]{1,0:T(8,128)S(1)}, f32[32,1152]{1,0:T(8,128)S(1)}, u32[]{:S(2)}, u32[]{:S(2)}) collective-permute-start(f32[32,1152]{1,0:T(8,128)S(1)} %get-tuple-element.39), channel_id=1, source_target_pairs={{0,1},{1,0},{2,3},{3,2},{4,5},{5,4},{6,7},{7,6},{8,9},{9,8},{10,11... | collective-permute-start | bytes 442376 | tf_op jit(solution)/shard_map/ppermute | solution.py:436
  5.3 7.8 %collective-permute-start.4 = (f32[32,1152]{1,0:T(8,128)S(1)}, f32[32,1152]{1,0:T(8,128)S(1)}, u32[]{:S(2)}, u32[]{:S(2)}) collective-permute-start(f32[32,1152]{1,0:T(8,128)S(1)} %get-tuple-element.40), channel_id=1, source_target_pairs={{1,2},{2,1},{3,4},{4,3},{5,6},{6,5},{9,10},{10,9},{11,12},{12,11},... | collective-permute-start | bytes 442376 | tf_op jit(solution)/shard_map/ppermute | solution.py:437
  8.3 10.3 %collective-permute-start.5 = (f32[24,1152]{1,0:T(8,128)S(1)}, f32[24,1152]{1,0:T(8,128)S(1)}, u32[]{:S(2)}, u32[]{:S(2)}) collective-permute-start(f32[24,1152]{1,0:T(8,128)S(1)} %get-tuple-element.53), channel_id=1, source_target_pairs={{0,1},{1,0},{2,3},{3,2},{4,5},{5,4},{6,7},{7,6},{8,9},{9,8},{10,11... | collective-permute-start | bytes 331784 | tf_op jit(solution)/shard_map/ppermute | solution.py:441
  9.9 8.8 %collective-permute-start.6 = (f32[24,1152]{1,0:T(8,128)S(1)}, f32[24,1152]{1,0:T(8,128)S(1)}, u32[]{:S(2)}, u32[]{:S(2)}) collective-permute-start(f32[24,1152]{1,0:T(8,128)S(1)} %get-tuple-element.54), channel_id=1, source_target_pairs={{1,2},{2,1},{3,4},{4,3},{5,6},{6,5},{9,10},{10,9},{11,12},{12,11},... | collective-permute-start | bytes 331784 | tf_op jit(solution)/shard_map/ppermute | solution.py:442
  21.2 2.3 %collective-permute-start.7 = (f32[16,1024]{1,0:T(8,128)S(1)}, f32[16,1024]{1,0:T(8,128)S(1)}, u32[]{:S(2)}, u32[]{:S(2)}) collective-permute-start(f32[16,1024]{1,0:T(8,128)S(1)} %get-tuple-element.56), channel_id=1, source_target_pairs={{0,8},{8,0},{16,24},{24,16},{1,9},{9,1},{17,25},{25,17},{2,10},{10... | collective-permute-start | bytes 196616 | tf_op jit(solution)/shard_map/ppermute | solution.py:426
  21.8 3.7 %collective-permute-start.8 = (f32[16,1024]{1,0:T(8,128)S(1)}, f32[16,1024]{1,0:T(8,128)S(1)}, u32[]{:S(2)}, u32[]{:S(2)}) collective-permute-start(f32[16,1024]{1,0:T(8,128)S(1)} %get-tuple-element.57), channel_id=1, source_target_pairs={{0,16},{8,24},{16,0},{24,8},{1,17},{9,25},{17,1},{25,9},{2,18},{10... | collective-permute-start | bytes 196616 | tf_op jit(solution)/shard_map/ppermute | solution.py:426
  23.0 4.0 %collective-permute-start.9 = (f32[16,1024]{1,0:T(8,128)S(1)}, f32[16,1024]{1,0:T(8,128)S(1)}, u32[]{:S(2)}, u32[]{:S(2)}) collective-permute-start(f32[16,1024]{1,0:T(8,128)S(1)} %get-tuple-element.58), channel_id=1, source_target_pairs={{0,24},{8,16},{16,8},{24,0},{1,25},{9,17},{17,9},{25,1},{2,26},{10... | collective-permute-start | bytes 196616 | tf_op jit(solution)/shard_map/ppermute | solution.py:426

commit v6 on v5

v6 whole, which is shorter than its diff:
```python
import functools

import jax
import jax.numpy as jnp
from jax import lax
from jax.experimental import pallas as pl
from jax.experimental.pallas import tpu as pltpu
from jax.sharding import PartitionSpec as P

FINE_STEPS = 4
LANE = 128
FRINGE = 16
HALO = 16
COEF_ROWS = (10, 9, 9)
FIELD_ROWS = (10, 8, 4)
COARSE_ROWS = 3
VMEM_LIMIT = 40 * 1024 * 1024


def padded(value, sides, width):
    for axis, dim in sides:
        devices, length = (lax.axis_size(axis), value.shape[dim])
        up = [(i, (i + 1) % devices) for i in range(devices - 1)]
        down = [(j, i) for i, j in up]
        last = lax.slice_in_dim(value, length - width, length, axis=dim)
        leading = lax.slice_in_dim(value, 0, width, axis=dim)
        before = lax.ppermute(last, axis, up)
        after = lax.ppermute(leading, axis, down)
        value = jnp.concatenate([before, value, after], axis=dim)
    return value


def from_behind(value, axis, steps):
    count = lax.axis_size(axis)
    leading, last = (max(0, -steps), min(count, count - steps))
    return lax.ppermute(value, axis, [(source, source + steps) for source in range(leading, last)])


def interior(field_ext, cond_rows, cond_cols):
    centre = field_ext[1:-1]
    flux_sum = cond_rows[1:-1] * (field_ext[2:] - centre) - cond_rows[:-2] * (
        centre - field_ext[:-2]
    )
    widened = jnp.pad(centre, ((0, 0), (1, 1)))
    cond_own = cond_cols[1:-1]
    cond_west = jnp.pad(cond_own, ((0, 0), (1, 0)))[:, :-1]
    flux_sum = (
        flux_sum + cond_own * (widened[:, 2:] - centre) - cond_west * (centre - widened[:, :-2])
    )
    return centre + flux_sum


def propagate(field, coef_pad):
    strip_rows = field.shape[0]
    cond_rows = coef_pad[0, 3 : strip_rows + 5]
    cond_cols = coef_pad[1, 3 : strip_rows + 5]
    source_rows = coef_pad[2, 4 : strip_rows + 4]
    for section in range(FINE_STEPS):
        extended = padded(field, (("space", 0),), 1)
        field = interior(extended, cond_rows, cond_cols) + source_rows
    return field


def restrict(field):
    lead = field.shape[:-2]
    shaped = field.reshape(lead + (field.shape[-2] // 2, 2, field.shape[-1] // 2, 2))
    return jnp.mean(shaped, axis=(-3, -1))


def general_shards(guesses, cond_x, cond_y, source, inflow):
    strip_rows = cond_x.shape[0]
    columns = cond_x.shape[1]
    stacked = jnp.stack([cond_x, cond_y, source])
    edge_rows = from_behind(cond_x[strip_rows - 2 :], "space", 1)
    cond_upper = jnp.concatenate([jnp.zeros((2, columns), jnp.float32), edge_rows], axis=0)
    blank_rows = jnp.zeros((4, columns), jnp.float32)
    upper = jnp.stack([cond_upper, blank_rows, blank_rows])
    lower = jnp.zeros((3, 4, columns), jnp.float32)
    coef_pad = jnp.concatenate([upper, stacked, lower], axis=1)
    first_group = lax.axis_index("tm") == 0
    c_point = guesses[0]
    first_pass = propagate(c_point, coef_pad)
    received = from_behind(first_pass, "tm", 1)
    relaxed = jnp.where(first_group, c_point, received)
    second_pass = propagate(relaxed, coef_pad)
    fine_next = from_behind(second_pass, "tm", 1)
    residual = restrict(fine_next - relaxed)
    residual = jnp.where(first_group, 0.0, residual)
    coarse_coef = restrict(coef_pad[:2, 2 : strip_rows + 6])

    def chain_round(index, error_field):
        extended = padded(error_field, (("space", 0),), 1)
        stepped = interior(extended, coarse_coef[0], coarse_coef[1])
        arrived = from_behind(stepped, "tm", 1)
        return jnp.where(first_group, inflow, arrived + residual)

    start_error = jnp.where(first_group, inflow, jnp.zeros_like(residual))
    error_field = lax.fori_loop(0, lax.axis_size("tm") - 1, chain_round, start_error)
    widened = jnp.repeat(jnp.repeat(error_field, 2, axis=0), 2, axis=1)
    return (relaxed + widened)[None]


def piece(chunk):
    return slice(chunk * LANE, (chunk + 1) * LANE)


def lanes_of(shape):
    return lax.broadcasted_iota(jnp.int32, shape, len(shape) - 1)


def fringe_of(left, right, member, width):
    lane = lanes_of(left.shape)
    last = lax.axis_size("tm") - 1
    value = jnp.where(lane < jnp.where(member < last, width, 0), right, 0.0)
    return jnp.where(lane >= jnp.where(member > 0, LANE - width, LANE), left, value)


def fold(source, rows):
    part = rows // 4
    total = source[:part]
    for turn in range(1, 4):
        total = total + pltpu.roll(source[turn * part : (turn + 1) * part], 2 * FRINGE * turn, 1)
    return total


def unfold(folded, target, rows):
    part = rows // 4
    lane = lanes_of(folded.shape)
    used = (lane < FRINGE) | (lane >= LANE - FRINGE)
    for turn in range(4):
        turned = pltpu.roll(folded, LANE - 2 * FRINGE * turn, 1) if turn else folded
        target[turn * part : (turn + 1) * part] = jnp.where(used, turned, 0.0)


def sides(rows):
    strip, strips = lax.axis_index("space"), lax.axis_size("space")
    return lax.rem(strip, 2) == 0, jnp.where(strip == strips - 1, HALO + rows, 2 * HALO + rows)


def by_side(even, fill, first, second):
    @pl.when(even)
    def _():
        fill(first, second)

    @pl.when(jnp.logical_not(even))
    def _():
        fill(second, first)


def pack_kernel(
    guess, cond_x, cond_y, source, inflow, own, to_core, to_x, to_both, halo_a, halo_b, coefs, coarse,
    guess_in, coefs_in, inflow_in, spare, sems,
):
    rows, columns = guess.shape
    groups, member = lax.axis_size("tm"), lax.axis_index("tm")
    width = columns // groups
    chunks = width // LANE

    def at(column):
        return pl.ds(pl.multiple_of(column, LANE), LANE)

    around = jnp.clip(width * member - LANE, 0, columns - width - 2 * LANE)
    span = pl.ds(pl.multiple_of(around, LANE), width + 2 * LANE)
    copies = [pltpu.make_async_copy(guess, guess_in, sems.at[0])]
    for slot, ref in enumerate((cond_x, cond_y, source)):
        copies.append(pltpu.make_async_copy(ref.at[:, span], coefs_in.at[slot], sems.at[1 + slot]))
    copies.append(pltpu.make_async_copy(inflow, inflow_in, sems.at[4]))
    for copy in copies:
        copy.start()
    copies[0].wait()
    for slot, out in enumerate((own, to_core, to_x, to_both)):
        target = member ^ slot
        first = width * target
        for chunk in range(chunks):
            out[chunk * rows : (chunk + 1) * rows] = guess_in[:, at(first + chunk * LANE)]
        left = guess_in[:, at(jnp.maximum(first - LANE, 0))]
        right = guess_in[:, at(jnp.minimum(first + width, columns - LANE))]
        spare[:rows] = fringe_of(left, right, target, FRINGE)
        out[chunks * rows : chunks * rows + rows // 4] = fold(spare, rows)
    for copy in copies[1:]:
        copy.wait()
    skip = width * member - around
    for slot in range(3):
        for chunk in range(chunks):
            coefs[slot, chunk] = coefs_in[slot, :, at(skip + chunk * LANE)]
        left = coefs_in[slot, :, at(jnp.maximum(skip - LANE, 0))]
        right = coefs_in[slot, :, at(jnp.minimum(skip + width, width + LANE))]
        coefs[slot, chunks] = fringe_of(left, right, member, FRINGE)
    first, half = width // 2 * member, chunks // 2
    for chunk in range(half):
        coarse[chunk] = inflow_in[:, at(first + chunk * LANE)]
    left = inflow_in[:, at(jnp.maximum(first - LANE, 0))]
    right = inflow_in[:, at(jnp.minimum(first + width // 2, columns // 2 - LANE))]
    coarse[half] = fringe_of(left, right, member, FRINGE // 2)

    def take(halo, bottom):
        base = fringe = 0
        for slot, deep in enumerate(COEF_ROWS):
            edge = slice(rows - deep, rows) if bottom else slice(0, deep)
            for chunk in range(chunks):
                halo[base : base + deep] = coefs[slot, chunk, edge]
                base += deep
            spare[fringe : fringe + deep] = coefs[slot, chunks, edge]
            fringe += deep
        halo[base : base + fringe // 4] = fold(spare, fringe)
        base += fringe // 4
        edge = slice(rows // 2 - COARSE_ROWS, rows // 2) if bottom else slice(0, COARSE_ROWS)
        for chunk in range(half + 1):
            halo[base : base + COARSE_ROWS] = coarse[chunk, edge]
            base += COARSE_ROWS

    def fill(below, above):
        take(below, True)
        take(above, False)

    by_side(sides(rows)[0], fill, halo_a, halo_b)


def edge_kernel(own, from_core, from_x, from_both, edge_a, edge_b, fields, spare):
    member = lax.axis_index("tm")
    chunks, rows = fields.shape[1] - 1, fields.shape[2]
    for slot, ref in enumerate((own, from_core, from_x, from_both)):
        target = fields.at[member ^ slot]
        for chunk in range(chunks):
            target[chunk] = ref[chunk * rows : (chunk + 1) * rows]
        unfold(ref[chunks * rows : chunks * rows + rows // 4], target.at[chunks], rows)

    def take(edge, bottom):
        base = fringe = 0
        for group, deep in enumerate(FIELD_ROWS):
            here = slice(rows - deep, rows) if bottom else slice(0, deep)
            for chunk in range(chunks):
                edge[base : base + deep] = fields[group, chunk, here]
                base += deep
            spare[fringe : fringe + deep] = fields[group, chunks, here]
            fringe += deep
        fringe = (fringe + 3) // 4 * 4
        edge[base : base + fringe // 4] = fold(spare, fringe)

    def fill(below, above):
        take(below, True)
        take(above, False)

    spare[...] = jnp.zeros_like(spare)
    by_side(sides(rows)[0], fill, edge_a, edge_b)


def spread(value):
    rows, lanes = value.shape
    value = value.reshape(rows // 8, 8, lanes)
    row_even = lax.broadcasted_iota(jnp.int32, value.shape, 1) % 2 == 0
    lane_even = lax.broadcasted_iota(jnp.int32, value.shape, 2) % 2 == 0
    value = value + jnp.where(row_even, pltpu.roll(value, 7, 1), pltpu.roll(value, 1, 1))
    value = value + jnp.where(lane_even, pltpu.roll(value, lanes - 1, 2), pltpu.roll(value, 1, 2))
    return (value * 0.25).reshape(rows, lanes)


def weights(cond_x, cond_y, chunk, rows, width, limit, out):
    diagonal, up, west = out
    chunks = cond_x.shape[0]
    first, count = rows
    here = slice(first, first + count)
    own_x, own_y = cond_x[chunk, here], cond_y[chunk, here]
    above = cond_x[chunk, first - width : first - width + count]
    lane = lanes_of(own_x.shape)
    row = lax.broadcasted_iota(jnp.int32, own_x.shape, 0)
    before = pltpu.roll(cond_y[(chunk - 1) % chunks, here], width, 1)
    beside = jnp.where(lane < width, before, pltpu.roll(own_y, width, 1))
    diagonal[chunk, here] = 1.0 - ((own_x + above) + (own_y + beside))
    up[chunk, here] = jnp.where(row < limit - first, above, 0.0)
    if chunk == chunks - 1:
        closed = jnp.where(lax.axis_index("tm") == lax.axis_size("tm") - 1, width, 0)
        beside = jnp.where(lane < closed, 0.0, beside)
    west[chunk, here] = beside


def prepare_kernel(
    coefs, coarse, coef_a, coef_b,
    cond_x, cond_y, source, diagonal, up, west, coarse_x, coarse_y, coarse_d, coarse_u, coarse_w, error,
    tall, spare,
):
    _, chunks, rows, _ = coefs.shape
    chunks, half = chunks - 1, (chunks - 1) // 2
    low = HALO + rows
    even, limit = sides(rows)
    targets = (cond_x, cond_y, source)
    tall[...] = jnp.zeros_like(tall)

    def give(halo, below):
        base = fringe = 0
        for ref, deep in zip(targets, COEF_ROWS):
            first = low if below else HALO - deep
            for chunk in range(chunks):
                ref[chunk, first : first + deep] = halo[base : base + deep]
                base += deep
        total = sum(COEF_ROWS)
        unfold(halo[base : base + total // 4], spare, total)
        base += total // 4
        for ref, deep in zip(targets, COEF_ROWS):
            first = low if below else HALO - deep
            ref[chunks, first : first + deep] = spare[fringe : fringe + deep]
            fringe += deep
        first = 4 + rows // 2 if below else 4 - COARSE_ROWS
        for chunk in range(half + 1):
            tall[chunk, first : first + COARSE_ROWS] = halo[base : base + COARSE_ROWS]
            base += COARSE_ROWS

    def fill(below, above):
        give(below, True)
        give(above, False)

    by_side(even, fill, coef_a, coef_b)
    for slot, ref in enumerate(targets):
        ref[:, HALO:low] = coefs[slot]
    tall[:, 4 : 4 + rows // 2] = coarse[...]
    for chunk in range(chunks + 1):
        weights(cond_x, cond_y, chunk, reach(rows, 9), 1, limit, (diagonal, up, west))
    span = slice(HALO - 8, low + 8)
    for chunk in range(chunks + 1):
        coarse_x[chunk, span] = spread(cond_x[chunk, span])
        coarse_y[chunk, span] = spread(cond_y[chunk, span])
    for chunk in range(chunks + 1):
        weights(coarse_x, coarse_y, chunk, reach(rows, 4), 2, limit, (coarse_d, coarse_u, coarse_w))
    lane = lanes_of((8, LANE))
    twice = lax.broadcasted_iota(jnp.int32, (8, LANE), 0) // 2
    for chunk in range(chunks + 1):
        side = chunk % 2 * (LANE // 2)
        pick = lane // 2 + (side if chunk < chunks else jnp.where(lane < LANE // 2, 0, LANE // 2))
        for part in range((rows // 2 + 8) // 8):
            wide = jnp.take_along_axis(tall[chunk // 2, 8 * part : 8 * part + 8], pick, axis=1)
            for end in range(2):
                at = HALO - 8 + 16 * part + 8 * end
                error[chunk, at : at + 8] = jnp.take_along_axis(wide, twice + 4 * end, axis=0)


def sweep(values, put, rows, width, factors, added):
    diagonal, up, down, east, west = factors
    chunks = diagonal.shape[0]
    first, count = rows
    here = slice(first, first + count)
    above = slice(first - width, first - width + count)
    below = slice(first + width, first + width + count)
    lane = lanes_of((count, LANE))

    def load(chunk):
        value = values[chunk % chunks, here]
        return value, pltpu.roll(value, LANE - width, 1), pltpu.roll(value, width, 1)

    before, now = load(-1), load(0)
    for chunk in range(chunks):
        after = load(chunk + 1)
        right = jnp.where(lane < LANE - width, now[1], after[1])
        left = jnp.where(lane < width, before[2], now[2])
        across = east[chunk, here] * right + west[chunk, here] * left
        along = down[chunk, here] * values[chunk, below] + up[chunk, here] * values[chunk, above]
        put[chunk, here] = (diagonal[chunk, here] * now[0] + added(chunk, here)) + (across + along)
        before, now = now, after


def reach(rows, deep):
    return HALO - deep, (rows + 2 * deep + 7) // 8 * 8


def main_kernel(
    fields, cond_x, cond_y, source, diagonal, up, west, coarse_x, coarse_y, coarse_d, coarse_u, coarse_w,
    start_error, edge_a, edge_b, own, to_core, to_x, to_both,
    guess, work, error, spare,
):
    groups, chunks, rows, _ = fields.shape
    chunks -= 1
    low = HALO + rows
    given = groups - 1

    def give(edge, below):
        base = fringe = 0
        for group, deep in enumerate(FIELD_ROWS):
            first = low if below else HALO - deep
            for chunk in range(chunks):
                guess[group, chunk, first : first + deep] = edge[base : base + deep]
                base += deep
        total = (sum(FIELD_ROWS) + 3) // 4 * 4
        unfold(edge[base : base + total // 4], spare, total)
        for group, deep in enumerate(FIELD_ROWS):
            first = low if below else HALO - deep
            guess[group, chunks, first : first + deep] = spare[fringe : fringe + deep]
            fringe += deep

    def fill(below, above):
        give(below, True)
        give(above, False)

    by_side(sides(rows)[0], fill, edge_a, edge_b)
    for group in range(given):
        guess[group, :, HALO:low] = fields[group]
    span = slice(HALO - 8, low + 8)
    error[0, :, span] = start_error[:, span]

    fine = (diagonal, up, cond_x, cond_y, west)
    coarse = (coarse_d, coarse_u, coarse_x, coarse_y, coarse_w)

    def add_source(chunk, here):
        return source[chunk, here]

    def propagate(slots, deeps):
        for number in range(FINE_STEPS):
            for lane, (slot, deep) in enumerate(zip(slots, deeps)):
                first, second = work.at[2 * lane], work.at[2 * lane + 1]
                stops = [guess.at[slot], first, second, first, guess.at[slot + given]]
                reached = reach(rows, deep + FINE_STEPS - 1 - number)
                sweep(stops[number], stops[number + 1], reached, 1, fine, add_source)

    propagate((0, 1, 2), (6, 4, 0))
    propagate((3, 4), (2, 0))

    for group in range(1, groups):
        reached = given if group == 1 else 2 * given - 2 + group
        relaxed = given - 1 + group

        def residual(chunk, here, reached=reached, relaxed=relaxed):
            return spread(guess[reached, chunk, here] - guess[relaxed, chunk, here])

        sweep(error.at[group - 1], error.at[group], reach(rows, 2 * (groups - 1 - group)), 2, coarse, residual)

    member = lax.axis_index("tm")
    for slot, out in enumerate((own, to_core, to_x, to_both)):
        group = member ^ slot
        relaxed = jnp.where(group == 0, 0, given - 1 + group)
        for chunk in range(chunks):
            out[:, piece(chunk)] = guess[relaxed, chunk, HALO:low] + error[group, chunk, HALO:low]


def unpack_kernel(own, from_core, from_x, from_both, out, sems):
    width = own.shape[1]
    member = lax.axis_index("tm")
    copies = []
    for slot, ref in enumerate((own, from_core, from_x, from_both)):
        at = pl.ds(pl.multiple_of((member ^ slot) * width, LANE), width)
        copies.append(pltpu.make_async_copy(ref, out.at[0, :, at], sems.at[slot]))
    for copy in copies:
        copy.start()
    for copy in copies:
        copy.wait()


def call(kernel, outs, scratch, operands, whole=(), outside=False, copies=0):
    vmem, anywhere = (pl.BlockSpec(memory_space=space) for space in (pltpu.VMEM, pltpu.HBM))
    specs = [anywhere if slot in whole else vmem for slot in range(len(operands))]
    operands = [
        pltpu.with_memory_space_constraint(value, pltpu.HBM) if slot in whole else value
        for slot, value in enumerate(operands)
    ]
    return pl.pallas_call(
        kernel,
        out_shape=[jax.ShapeDtypeStruct(shape, jnp.float32) for shape in outs],
        in_specs=specs,
        out_specs=[anywhere if outside else vmem] * len(outs),
        scratch_shapes=[pltpu.VMEM(shape, jnp.float32) for shape in scratch]
        + ([pltpu.SemaphoreType.DMA((copies,))] if copies else []),
        compiler_params=pltpu.CompilerParams(vmem_limit_bytes=VMEM_LIMIT),
    )(*operands)


def shards(guesses, cond_x, cond_y, source, inflow):
    groups, strips = lax.axis_size("tm"), lax.axis_size("space")
    rows, columns = cond_x.shape
    fits = groups == len(FIELD_ROWS) + 1 and strips % 2 == 0 and rows == 16
    if not fits or columns % (2 * groups * LANE) != 0:
        return general_shards(guesses, cond_x, cond_y, source, inflow)
    own = columns // groups
    chunks = own // LANE
    pairs_a = [(i, i ^ 1) for i in range(strips)]
    pairs_b = [(i, j) for k in range(1, strips - 1, 2) for i, j in ((k, k + 1), (k + 1, k))]

    def trade(blocks):
        moved = [blocks[0]]
        for slot in range(1, groups):
            moved.append(lax.ppermute(blocks[slot], "tm", [(i, i ^ slot) for i in range(groups)]))
        return moved

    def whole(count):
        return (count + 7) // 8 * 8

    def folded(count):
        return count * chunks + (count + 3) // 4

    block = (whole(folded(rows)), LANE)
    halo = (whole(folded(sum(COEF_ROWS)) + (chunks // 2 + 1) * COARSE_ROWS), LANE)
    edge = (whole(folded(sum(FIELD_ROWS))), LANE)
    spare = (32, LANE)
    *blocks, halo_a, halo_b, coefs, coarse = call(
        pack_kernel,
        [block] * groups + [halo, halo, (3, chunks + 1, rows, LANE), (chunks // 2 + 1, rows // 2, LANE)],
        [(rows, columns), (3, rows, own + 2 * LANE), (rows // 2, columns // 2), spare],
        [guesses[0], cond_x, cond_y, source, inflow], whole=range(5), copies=5,
    )
    coef_a = lax.ppermute(halo_a, "space", pairs_a)
    coef_b = lax.ppermute(halo_b, "space", pairs_b)
    blocks = trade(blocks)
    sent_a, sent_b, fields = call(edge_kernel, [edge, edge, (groups, chunks + 1, rows, LANE)], [spare], blocks)
    edge_a = lax.ppermute(sent_a, "space", pairs_a)
    edge_b = lax.ppermute(sent_b, "space", pairs_b)
    buffer = (chunks + 1, rows + 2 * HALO, LANE)
    prepared = call(
        prepare_kernel, [buffer] * 12, [(chunks // 2 + 1, rows // 2 + 8, LANE), spare], [coefs, coarse, coef_a, coef_b]
    )
    blocks = call(
        main_kernel,
        [(rows, own)] * groups,
        [(3 * groups - 4, *buffer), (2 * groups - 2, *buffer), (groups, *buffer), spare],
        [fields, *prepared, edge_a, edge_b],
    )
    return call(unpack_kernel, [(1, rows, columns)], [], trade(blocks), outside=True, copies=groups)[0]


def solution(mesh):
    return jax.shard_map(
        shards,
        mesh=mesh,
        in_specs=(
            P("tm", "space", None),
            P("space", None),
            P("space", None),
            P("space", None),
            P("space", None),
        ),
        out_specs=P("tm", "space", None),
        check_vma=False,
    )
```

time: 28 us -> 27 us (0.964)
  waiting for transfers between devices: 10.8 us -> 8.16 us
  starting transfers between devices: 11.3 us -> 13 us
    ppermute x1, waiting for transfers between devices: 4.94 us -> 2.23 us  [shards(): edge_a = lax.ppermute(sent_a, 'space', pairs_a)]
    ppermute x6, starting transfers between devices: 4.71 us -> 6.26 us  [trade(): lax.ppermute(blocks[slot], 'tm', [(i, i ^ slot) for i in range(groups)])]
    ppermute x1, waiting for transfers between devices: 0.01 us -> 0.77 us  [shards(): edge_b = lax.ppermute(sent_b, 'space', pairs_b)]
    ppermute x1, waiting for transfers between devices: 1.32 us -> 0.78 us  [shards(): coef_b = lax.ppermute(halo_b, 'space', pairs_b)]
  transfers between devices with their start and end apart: 10 -> 10, of which waited for: 5 -> 6; matrix products, arithmetic and copies ran while one was open for 0% -> 0% of each run, Pallas kernels for 2% -> 3%
where the time goes in v6:
time: 27 us; the launch traced here: 26.8 us
  starting transfers between devices  13 us (48%)
  waiting for transfers between devices  8.16 us (30%)
  Pallas kernels  5.57 us (21%)
    ppermute x6, starting transfers between devices, trade(): lax.ppermute(blocks[slot], 'tm', [(i, i ^ slot) for i in range(groups)])  6.26 us
    pallas_call x5, Pallas kernels, call(): pl.pallas_call(kernel, out_shape=[jax.ShapeDtypeStruct(shape, jnp.float32...  5.57 us
    ppermute x6, waiting for transfers between devices, trade(): lax.ppermute(blocks[slot], 'tm', [(i, i ^ slot) for i in range(groups)])  4.39 us
    ppermute x1, waiting for transfers between devices, shards(): edge_a = lax.ppermute(sent_a, 'space', pairs_a)  2.23 us
    ppermute x1, starting transfers between devices, shards(): coef_b = lax.ppermute(halo_b, 'space', pairs_b)  1.91 us
    ppermute x1, starting transfers between devices, shards(): edge_b = lax.ppermute(sent_b, 'space', pairs_b)  1.91 us
    ppermute x1, starting transfers between devices, shards(): edge_a = lax.ppermute(sent_a, 'space', pairs_a)  1.68 us
    ppermute x1, starting transfers between devices, shards(): coef_a = lax.ppermute(halo_a, 'space', pairs_a)  1.24 us
  transfers between devices with their start and end apart: 10, of which 6 were waited for; matrix products, arithmetic and copies ran while one was open for 0% of the time, Pallas kernels for 3%

profile of v6, /device:TPU:9, one launch (start us, length us, event | category | flops | bytes accessed | tf_op | source)
XLA Modules:
  0.0 26.8 jit_solution(6712661431667565859)
XLA Ops:
  0.0 1.2 %shard_map.55 = (f32[136,128]{1,0:T(8,128)S(1)}, f32[136,128]{1,0:T(8,128)S(1)}, f32[136,128]{1,0:T(8,128)S(1)}, f32[136,128]{1,0:T(8,128)S(1)}, f32[248,128]{1,...) custom-call(f32[16,4096]{1,0:T(8,128)} %bitcast.1, ...), custom_call_target="tpu_custom_call" | custom-call | tf_op jit(solution)/shard_map/pallas_call | solution.py:452
  1.3 0.7 %collective-permute-start = (f32[136,128]{1,0:T(8,128)S(1)}, f32[136,128]{1,0:T(8,128)S(1)}, u32[]{:S(2)}, u32[]{:S(2)}) collective-permute-start(f32[136,128]{1,0:T(8,128)S(1)} %get-tuple-element.33), channel_id=1, source_target_pairs={{0,8},{8,0},{16,24},{24,16},{1,9},{9,1},{17,25},{25,17},{2,10},{10... | collective-permute-start | bytes 208904 | tf_op jit(solution)/shard_map/ppermute | solution.py:477
  2.0 1.2 %collective-permute-start.1 = (f32[136,128]{1,0:T(8,128)S(1)}, f32[136,128]{1,0:T(8,128)S(1)}, u32[]{:S(2)}, u32[]{:S(2)}) collective-permute-start(f32[136,128]{1,0:T(8,128)S(1)} %get-tuple-element.34), channel_id=1, source_target_pairs={{0,16},{8,24},{16,0},{24,8},{1,17},{9,25},{17,1},{25,9},{2,18},{10... | collective-permute-start | bytes 208904 | tf_op jit(solution)/shard_map/ppermute | solution.py:477
  3.2 0.5 %collective-permute-start.2 = (f32[136,128]{1,0:T(8,128)S(1)}, f32[136,128]{1,0:T(8,128)S(1)}, u32[]{:S(2)}, u32[]{:S(2)}) collective-permute-start(f32[136,128]{1,0:T(8,128)S(1)} %get-tuple-element.35), channel_id=1, source_target_pairs={{0,24},{8,16},{16,8},{24,0},{1,25},{9,17},{17,9},{25,1},{2,26},{10... | collective-permute-start | bytes 208904 | tf_op jit(solution)/shard_map/ppermute | solution.py:477
  3.7 1.2 %collective-permute-start.3 = (f32[248,128]{1,0:T(8,128)S(1)}, f32[248,128]{1,0:T(8,128)S(1)}, u32[]{:S(2)}, u32[]{:S(2)}) collective-permute-start(f32[248,128]{1,0:T(8,128)S(1)} %get-tuple-element.39), channel_id=1, source_target_pairs={{0,1},{1,0},{2,3},{3,2},{4,5},{5,4},{6,7},{7,6},{8,9},{9,8},{10,11... | collective-permute-start | bytes 380936 | tf_op jit(solution)/shard_map/ppermute | solution.py:496
  4.9 1.9 %collective-permute-start.4 = (f32[248,128]{1,0:T(8,128)S(1)}, f32[248,128]{1,0:T(8,128)S(1)}, u32[]{:S(2)}, u32[]{:S(2)}) collective-permute-start(f32[248,128]{1,0:T(8,128)S(1)} %get-tuple-element.40), channel_id=1, source_target_pairs={{1,2},{2,1},{3,4},{4,3},{5,6},{6,5},{9,10},{10,9},{11,12},{12,11},... | collective-permute-start | bytes 380936 | tf_op jit(solution)/shard_map/ppermute | solution.py:497
  6.9 0.0 collective-permute-done.1.from_x
  6.9 0.8 %collective-permute-done.2.from_both = f32[136,128]{1,0:T(8,128)S(1)} collective-permute-done((f32[136,128]{1,0:T(8,128)S(1)}, f32[136,128]{1,0:T(8,128)S(1)}, u32[]{:S(2)}, u32[]{:S(2)}) %collective-permute-start.2) | collective-permute-done | bytes 69664 | tf_op jit(solution)/shard_map/ppermute | solution.py:477
  7.7 0.2 shard_map.56
  7.9 1.7 %collective-permute-start.5 = (f32[184,128]{1,0:T(8,128)S(1)}, f32[184,128]{1,0:T(8,128)S(1)}, u32[]{:S(2)}, u32[]{:S(2)}) collective-permute-start(f32[184,128]{1,0:T(8,128)S(1)} %get-tuple-element.53), channel_id=1, source_target_pairs={{0,1},{1,0},{2,3},{3,2},{4,5},{5,4},{6,7},{7,6},{8,9},{9,8},{10,11... | collective-permute-start | bytes 282632 | tf_op jit(solution)/shard_map/ppermute | solution.py:500
  9.6 1.9 %collective-permute-start.6 = (f32[184,128]{1,0:T(8,128)S(1)}, f32[184,128]{1,0:T(8,128)S(1)}, u32[]{:S(2)}, u32[]{:S(2)}) collective-permute-start(f32[184,128]{1,0:T(8,128)S(1)} %get-tuple-element.54), channel_id=1, source_target_pairs={{1,2},{2,1},{3,4},{4,3},{5,6},{6,5},{9,10},{10,9},{11,12},{12,11},... | collective-permute-start | bytes 282632 | tf_op jit(solution)/shard_map/ppermute | solution.py:501
  11.5 0.0 collective-permute-done.3.coef_a
  11.5 0.8 %collective-permute-done.4.coef_b = f32[248,128]{1,0:T(8,128)S(1)} collective-permute-done((f32[248,128]{1,0:T(8,128)S(1)}, f32[248,128]{1,0:T(8,128)S(1)}, u32[]{:S(2)}, u32[]{:S(2)}) %collective-permute-start.4) | collective-permute-done | bytes 127008 | tf_op jit(solution)/shard_map/ppermute | solution.py:497
  12.3 0.6 %shard_map.57 = (f32[9,48,128]{2,1,0:T(8,128)S(1)}, f32[9,48,128]{2,1,0:T(8,128)S(1)}, f32[9,48,128]{2,1,0:T(8,128)S(1)}, f32[9,48,128]{2,1,0:T(8,128)S(1)}, f32...) custom-call(f32[3,9,16,128]{3,2,1,0:T(8,128)S(1)} %get-tuple-element, ...), custom_call_target="tpu_custom_call" | custom-call | tf_op jit(solution)/shard_map/pallas_call | solution.py:452
  12.9 2.2 %collective-permute-done.5.edge_a = f32[184,128]{1,0:T(8,128)S(1)} collective-permute-done((f32[184,128]{1,0:T(8,128)S(1)}, f32[184,128]{1,0:T(8,128)S(1)}, u32[]{:S(2)}, u32[]{:S(2)}) %collective-permute-start.5) | collective-permute-done | bytes 94240 | tf_op jit(solution)/shard_map/ppermute | solution.py:500
  15.1 0.8 %collective-permute-done.6.edge_b = f32[184,128]{1,0:T(8,128)S(1)} collective-permute-done((f32[184,128]{1,0:T(8,128)S(1)}, f32[184,128]{1,0:T(8,128)S(1)}, u32[]{:S(2)}, u32[]{:S(2)}) %collective-permute-start.6) | collective-permute-done | bytes 94240 | tf_op jit(solution)/shard_map/ppermute | solution.py:501
  15.9 2.8 %shard_map.58 = (f32[16,1024]{1,0:T(8,128)S(1)}, f32[16,1024]{1,0:T(8,128)S(1)}, f32[16,1024]{1,0:T(8,128)S(1)}, f32[16,1024]{1,0:T(8,128)S(1)}) custom-call(f32[4,9,16,128]{3,2,1,0:T(8,128)S(1)} %get-tuple-element.36.fields, f32[9,48,128]{2,1,0:T(8,128)S(1)} %get-tuple-element.41.cond_x, f32[9,48,128]{2,1,0:T(8,128)S(1)} %get-tuple-element.42.cond_y, ...), custom_call_target="tpu_custom_call" | custom-call | tf_op jit(solution)/shard_map/pallas_call | solution.py:452
  18.7 2.1 %collective-permute-start.7 = (f32[16,1024]{1,0:T(8,128)S(1)}, f32[16,1024]{1,0:T(8,128)S(1)}, u32[]{:S(2)}, u32[]{:S(2)}) collective-permute-start(f32[16,1024]{1,0:T(8,128)S(1)} %get-tuple-element.56), channel_id=1, source_target_pairs={{0,8},{8,0},{16,24},{24,16},{1,9},{9,1},{17,25},{25,17},{2,10},{10... | collective-permute-start | bytes 196616 | tf_op jit(solution)/shard_map/ppermute | solution.py:477
  20.8 1.2 %collective-permute-start.8 = (f32[16,1024]{1,0:T(8,128)S(1)}, f32[16,1024]{1,0:T(8,128)S(1)}, u32[]{:S(2)}, u32[]{:S(2)}) collective-permute-start(f32[16,1024]{1,0:T(8,128)S(1)} %get-tuple-element.57), channel_id=1, source_target_pairs={{0,16},{8,24},{16,0},{24,8},{1,17},{9,25},{17,1},{25,9},{2,18},{10... | collective-permute-start | bytes 196616 | tf_op jit(solution)/shard_map/ppermute | solution.py:477
  22.0 0.5 %collective-permute-start.9 = (f32[16,1024]{1,0:T(8,128)S(1)}, f32[16,1024]{1,0:T(8,128)S(1)}, u32[]{:S(2)}, u32[]{:S(2)}) collective-permute-start(f32[16,1024]{1,0:T(8,128)S(1)} %get-tuple-element.58), channel_id=1, source_target_pairs={{0,24},{8,16},{16,8},{24,0},{1,25},{9,17},{17,9},{25,1},{2,26},{10... | collective-permute-start | bytes 196616 | tf_op jit(solution)/shard_map/ppermute | solution.py:477
  22.5 0.0 collective-permute-done.7.from_core
  22.5 2.0 %collective-permute-done.8.from_x = f32[16,1024]{1,0:T(8,128)S(1)} collective-permute-done((f32[16,1024]{1,0:T(8,128)S(1)}, f32[16,1024]{1,0:T(8,128)S(1)}, u32[]{:S(2)}, u32[]{:S(2)}) %collective-permute-start.8) | collective-permute-done | bytes 65568 | tf_op jit(solution)/shard_map/ppermute | solution.py:477
  24.5 1.6 %collective-permute-done.9.from_both = f32[16,1024]{1,0:T(8,128)S(1)} collective-permute-done((f32[16,1024]{1,0:T(8,128)S(1)}, f32[16,1024]{1,0:T(8,128)S(1)}, u32[]{:S(2)}, u32[]{:S(2)}) %collective-permute-start.9) | collective-permute-done | bytes 65568 | tf_op jit(solution)/shard_map/ppermute | solution.py:477
  26.1 0.7 %shard_map.59 = f32[1,16,4096]{2,1,0:T(8,128)} custom-call(f32[16,1024]{1,0:T(8,128)S(1)} %get-tuple-element.55.own, f32[16,1024]{1,0:T(8,128)S(1)} %collective-permute-done.7.from_core, f32[16,1024]{1,0:T(8,128)S(1)} %collective-permute-done.8.from_x, f32[16,1024]{1,0:T(8,128)S(1)} %collective-permute-done.9.from_both), custom_call_target="tpu_custom_call" | custom-call | tf_op jit(solution)/shard_map/pallas_call | solution.py:452
  (1 shorter events, 0.0 us)
Async XLA Ops:
  1.3 5.6 %collective-permute-start = (f32[136,128]{1,0:T(8,128)S(1)}, f32[136,128]{1,0:T(8,128)S(1)}, u32[]{:S(2)}, u32[]{:S(2)}) collective-permute-start(f32[136,128]{1,0:T(8,128)S(1)} %get-tuple-element.33), channel_id=1, source_target_pairs={{0,8},{8,0},{16,24},{24,16},{1,9},{9,1},{17,25},{25,17},{2,10},{10... | collective-permute-start | bytes 208904 | tf_op jit(solution)/shard_map/ppermute | solution.py:477
  2.0 4.9 %collective-permute-start.1 = (f32[136,128]{1,0:T(8,128)S(1)}, f32[136,128]{1,0:T(8,128)S(1)}, u32[]{:S(2)}, u32[]{:S(2)}) collective-permute-start(f32[136,128]{1,0:T(8,128)S(1)} %get-tuple-element.34), channel_id=1, source_target_pairs={{0,16},{8,24},{16,0},{24,8},{1,17},{9,25},{17,1},{25,9},{2,18},{10... | collective-permute-start | bytes 208904 | tf_op jit(solution)/shard_map/ppermute | solution.py:477
  3.2 4.5 %collective-permute-start.2 = (f32[136,128]{1,0:T(8,128)S(1)}, f32[136,128]{1,0:T(8,128)S(1)}, u32[]{:S(2)}, u32[]{:S(2)}) collective-permute-start(f32[136,128]{1,0:T(8,128)S(1)} %get-tuple-element.35), channel_id=1, source_target_pairs={{0,24},{8,16},{16,8},{24,0},{1,25},{9,17},{17,9},{25,1},{2,26},{10... | collective-permute-start | bytes 208904 | tf_op jit(solution)/shard_map/ppermute | solution.py:477
  3.7 7.8 %collective-permute-start.3 = (f32[248,128]{1,0:T(8,128)S(1)}, f32[248,128]{1,0:T(8,128)S(1)}, u32[]{:S(2)}, u32[]{:S(2)}) collective-permute-start(f32[248,128]{1,0:T(8,128)S(1)} %get-tuple-element.39), channel_id=1, source_target_pairs={{0,1},{1,0},{2,3},{3,2},{4,5},{5,4},{6,7},{7,6},{8,9},{9,8},{10,11... | collective-permute-start | bytes 380936 | tf_op jit(solution)/shard_map/ppermute | solution.py:496
  4.9 7.3 %collective-permute-start.4 = (f32[248,128]{1,0:T(8,128)S(1)}, f32[248,128]{1,0:T(8,128)S(1)}, u32[]{:S(2)}, u32[]{:S(2)}) collective-permute-start(f32[248,128]{1,0:T(8,128)S(1)} %get-tuple-element.40), channel_id=1, source_target_pairs={{1,2},{2,1},{3,4},{4,3},{5,6},{6,5},{9,10},{10,9},{11,12},{12,11},... | collective-permute-start | bytes 380936 | tf_op jit(solution)/shard_map/ppermute | solution.py:497
  7.9 7.2 %collective-permute-start.5 = (f32[184,128]{1,0:T(8,128)S(1)}, f32[184,128]{1,0:T(8,128)S(1)}, u32[]{:S(2)}, u32[]{:S(2)}) collective-permute-start(f32[184,128]{1,0:T(8,128)S(1)} %get-tuple-element.53), channel_id=1, source_target_pairs={{0,1},{1,0},{2,3},{3,2},{4,5},{5,4},{6,7},{7,6},{8,9},{9,8},{10,11... | collective-permute-start | bytes 282632 | tf_op jit(solution)/shard_map/ppermute | solution.py:500
  9.6 6.3 %collective-permute-start.6 = (f32[184,128]{1,0:T(8,128)S(1)}, f32[184,128]{1,0:T(8,128)S(1)}, u32[]{:S(2)}, u32[]{:S(2)}) collective-permute-start(f32[184,128]{1,0:T(8,128)S(1)} %get-tuple-element.54), channel_id=1, source_target_pairs={{1,2},{2,1},{3,4},{4,3},{5,6},{6,5},{9,10},{10,9},{11,12},{12,11},... | collective-permute-start | bytes 282632 | tf_op jit(solution)/shard_map/ppermute | solution.py:501
  18.7 3.8 %collective-permute-start.7 = (f32[16,1024]{1,0:T(8,128)S(1)}, f32[16,1024]{1,0:T(8,128)S(1)}, u32[]{:S(2)}, u32[]{:S(2)}) collective-permute-start(f32[16,1024]{1,0:T(8,128)S(1)} %get-tuple-element.56), channel_id=1, source_target_pairs={{0,8},{8,0},{16,24},{24,16},{1,9},{9,1},{17,25},{25,17},{2,10},{10... | collective-permute-start | bytes 196616 | tf_op jit(solution)/shard_map/ppermute | solution.py:477
  20.8 3.7 %collective-permute-start.8 = (f32[16,1024]{1,0:T(8,128)S(1)}, f32[16,1024]{1,0:T(8,128)S(1)}, u32[]{:S(2)}, u32[]{:S(2)}) collective-permute-start(f32[16,1024]{1,0:T(8,128)S(1)} %get-tuple-element.57), channel_id=1, source_target_pairs={{0,16},{8,24},{16,0},{24,8},{1,17},{9,25},{17,1},{25,9},{2,18},{10... | collective-permute-start | bytes 196616 | tf_op jit(solution)/shard_map/ppermute | solution.py:477
  22.0 4.0 %collective-permute-start.9 = (f32[16,1024]{1,0:T(8,128)S(1)}, f32[16,1024]{1,0:T(8,128)S(1)}, u32[]{:S(2)}, u32[]{:S(2)}) collective-permute-start(f32[16,1024]{1,0:T(8,128)S(1)} %get-tuple-element.58), channel_id=1, source_target_pairs={{0,24},{8,16},{16,8},{24,0},{1,25},{9,17},{17,9},{25,1},{2,26},{10... | collective-permute-start | bytes 196616 | tf_op jit(solution)/shard_map/ppermute | solution.py:477

commit v7 on v6

--- a/solution.py
+++ b/solution.py
@@ -276,8 +276,8 @@
 
 def prepare_kernel(
     coefs, coarse, coef_a, coef_b,
-    cond_x, cond_y, source, diagonal, up, west, coarse_x, coarse_y, coarse_d, coarse_u, coarse_w, error,
-    tall, spare,
+    cond_x, cond_y, response, diagonal, up, west, coarse_x, coarse_y, coarse_d, coarse_u, coarse_w, error, carried,
+    tall, spare, source, work,
 ):
     _, chunks, rows, _ = coefs.shape
     chunks, half = chunks - 1, (chunks - 1) // 2
@@ -315,10 +315,10 @@
     tall[:, 4 : 4 + rows // 2] = coarse[...]
     for chunk in range(chunks + 1):
         weights(cond_x, cond_y, chunk, reach(rows, 9), 1, limit, (diagonal, up, west))
-    span = slice(HALO - 8, low + 8)
+    near = slice(HALO - 8, low + 8)
     for chunk in range(chunks + 1):
-        coarse_x[chunk, span] = spread(cond_x[chunk, span])
-        coarse_y[chunk, span] = spread(cond_y[chunk, span])
+        coarse_x[chunk, near] = spread(cond_x[chunk, near])
+        coarse_y[chunk, near] = spread(cond_y[chunk, near])
     for chunk in range(chunks + 1):
         weights(coarse_x, coarse_y, chunk, reach(rows, 4), 2, limit, (coarse_d, coarse_u, coarse_w))
     lane = lanes_of((8, LANE))
@@ -331,39 +331,59 @@
             for end in range(2):
                 at = HALO - 8 + 16 * part + 8 * end
                 error[chunk, at : at + 8] = jnp.take_along_axis(wide, twice + 4 * end, axis=0)
-
-
-def sweep(values, put, rows, width, factors, added):
+    fine = (diagonal, up, cond_x, cond_y, west)
+    stops = [source] + [work.at[number] for number in range(FINE_STEPS - 1)]
+    for number in range(FINE_STEPS - 1):
+        sweep([(stops[number], stops[number + 1], span(rows, 8 - number), None)], 1, fine)
+    first, count = reach(rows, 6)
+    here = slice(first, first + count)
+    for chunk in range(chunks + 1):
+        total = source[chunk, here]
+        for number in range(FINE_STEPS - 1):
+            total = total + work[number, chunk, here]
+        response[chunk, here] = total
+    sweep([(error, carried, span(rows, 4), None)], 2, (coarse_d, coarse_u, coarse_x, coarse_y, coarse_w))
+
+
+def sweep(items, width, factors):
     diagonal, up, down, east, west = factors
     chunks = diagonal.shape[0]
-    first, count = rows
-    here = slice(first, first + count)
-    above = slice(first - width, first - width + count)
-    below = slice(first + width, first + width + count)
-    lane = lanes_of((count, LANE))
-
-    def load(chunk):
-        value = values[chunk % chunks, here]
-        return value, pltpu.roll(value, LANE - width, 1), pltpu.roll(value, width, 1)
-
-    before, now = load(-1), load(0)
-    for chunk in range(chunks):
-        after = load(chunk + 1)
-        right = jnp.where(lane < LANE - width, now[1], after[1])
-        left = jnp.where(lane < width, before[2], now[2])
-        across = east[chunk, here] * right + west[chunk, here] * left
-        along = down[chunk, here] * values[chunk, below] + up[chunk, here] * values[chunk, above]
-        put[chunk, here] = (diagonal[chunk, here] * now[0] + added(chunk, here)) + (across + along)
-        before, now = now, after
+    lane = lanes_of((8, LANE))
+    origin = min(item[2][0] for item in items)
+    end = max(item[2][1] for item in items)
+    for first in range(origin, end, 8):
+        here, above, below = (slice(first + move, first + move + 8) for move in (0, -width, width))
+        active = [item for item in items if item[2][0] < first + 8 and item[2][1] > first]
+
+        def load(values, chunk):
+            value = values[chunk % chunks, here]
+            return value, pltpu.roll(value, LANE - width, 1), pltpu.roll(value, width, 1)
+
+        states = [[load(item[0], -1), load(item[0], 0)] for item in active]
+        for chunk in range(chunks):
+            own = [ref[chunk, here] for ref in (diagonal, up, down, east, west)]
+            for (values, put, _, added), state in zip(active, states):
+                before, now = state
+                after = load(values, chunk + 1)
+                right = jnp.where(lane < LANE - width, now[1], after[1])
+                left = jnp.where(lane < width, before[2], now[2])
+                total = (own[3] * right + own[4] * left) + (own[2] * values[chunk, below] + own[1] * values[chunk, above])
+                total = own[0] * now[0] + total
+                put[chunk, here] = total if added is None else total + added(chunk, here)
+                state[:] = [now, after]
 
 
 def reach(rows, deep):
     return HALO - deep, (rows + 2 * deep + 7) // 8 * 8
 
 
+def span(rows, deep):
+    return HALO - deep, HALO + rows + deep
+
+
 def main_kernel(
-    fields, cond_x, cond_y, source, diagonal, up, west, coarse_x, coarse_y, coarse_d, coarse_u, coarse_w,
-    start_error, edge_a, edge_b, own, to_core, to_x, to_both,
+    fields, cond_x, cond_y, response, diagonal, up, west, coarse_x, coarse_y, coarse_d, coarse_u, coarse_w,
+    start_error, carried, edge_a, edge_b, own, to_core, to_x, to_both,
     guess, work, error, spare,
 ):
     groups, chunks, rows, _ = fields.shape
@@ -392,34 +412,38 @@
     by_side(sides(rows)[0], fill, edge_a, edge_b)
     for group in range(given):
         guess[group, :, HALO:low] = fields[group]
-    span = slice(HALO - 8, low + 8)
-    error[0, :, span] = start_error[:, span]
-
     fine = (diagonal, up, cond_x, cond_y, west)
     coarse = (coarse_d, coarse_u, coarse_x, coarse_y, coarse_w)
 
-    def add_source(chunk, here):
-        return source[chunk, here]
+    def add_response(chunk, here):
+        return response[chunk, here]
 
     def propagate(slots, deeps):
         for number in range(FINE_STEPS):
-            for lane, (slot, deep) in enumerate(zip(slots, deeps)):
-                first, second = work.at[2 * lane], work.at[2 * lane + 1]
+            items = []
+            for place, (slot, deep) in enumerate(zip(slots, deeps)):
+                first, second = work.at[2 * place], work.at[2 * place + 1]
                 stops = [guess.at[slot], first, second, first, guess.at[slot + given]]
-                reached = reach(rows, deep + FINE_STEPS - 1 - number)
-                sweep(stops[number], stops[number + 1], reached, 1, fine, add_source)
+                needed = span(rows, deep + FINE_STEPS - 1 - number)
+                added = add_response if number == FINE_STEPS - 1 else None
+                items.append((stops[number], stops[number + 1], needed, added))
+            sweep(items, 1, fine)
 
     propagate((0, 1, 2), (6, 4, 0))
     propagate((3, 4), (2, 0))
 
-    for group in range(1, groups):
+    def residual(group, chunk, here):
         reached = given if group == 1 else 2 * given - 2 + group
-        relaxed = given - 1 + group
-
-        def residual(chunk, here, reached=reached, relaxed=relaxed):
-            return spread(guess[reached, chunk, here] - guess[relaxed, chunk, here])
-
-        sweep(error.at[group - 1], error.at[group], reach(rows, 2 * (groups - 1 - group)), 2, coarse, residual)
+        return spread(guess[reached, chunk, here] - guess[given - 1 + group, chunk, here])
+
+    first, count = reach(rows, 2 * (groups - 2))
+    here = slice(first, first + count)
+    for chunk in range(chunks + 1):
+        error[1, chunk, here] = carried[chunk, here] + residual(1, chunk, here)
+    for group in range(2, groups):
+        needed = span(rows, 2 * (groups - 1 - group))
+        sweep([(error.at[group - 1], error.at[group], needed, functools.partial(residual, group))], 2, coarse)
+    error[0, :, HALO:low] = start_error[:, HALO:low]
 
     member = lax.axis_index("tm")
     for slot, out in enumerate((own, to_core, to_x, to_both)):
@@ -501,7 +525,10 @@
     edge_b = lax.ppermute(sent_b, "space", pairs_b)
     buffer = (chunks + 1, rows + 2 * HALO, LANE)
     prepared = call(
-        prepare_kernel, [buffer] * 12, [(chunks // 2 + 1, rows // 2 + 8, LANE), spare], [coefs, coarse, coef_a, coef_b]
+        prepare_kernel,
+        [buffer] * 13,
+        [(chunks // 2 + 1, rows // 2 + 8, LANE), spare, buffer, (FINE_STEPS - 1, *buffer)],
+        [coefs, coarse, coef_a, coef_b],
     )
     blocks = call(
         main_kernel,

time: 27 us -> 26.5 us (0.981)
  waiting for transfers between devices: 8.16 us -> 7.65 us
    ppermute x1, waiting for transfers between devices: 2.23 us -> 1.72 us  [shards(): edge_a = lax.ppermute(sent_a, 'space', pairs_a)]
  transfers between devices with their start and end apart: 10 -> 10, of which waited for: 6 -> 6; matrix products, arithmetic and copies ran while one was open for 0% -> 0% of each run, Pallas kernels for 3% -> 5%
where the time goes in v7:
time: 26.5 us; the launch traced here: 26.4 us
  starting transfers between devices  13 us (49%)
  waiting for transfers between devices  7.65 us (29%)
  Pallas kernels  5.63 us (21%)
    ppermute x6, starting transfers between devices, trade(): lax.ppermute(blocks[slot], 'tm', [(i, i ^ slot) for i in range(groups)])  6.26 us
    pallas_call x5, Pallas kernels, call(): pl.pallas_call(kernel, out_shape=[jax.ShapeDtypeStruct(shape, jnp.float32...  5.63 us
    ppermute x6, waiting for transfers between devices, trade(): lax.ppermute(blocks[slot], 'tm', [(i, i ^ slot) for i in range(groups)])  4.39 us
    ppermute x1, starting transfers between devices, shards(): coef_b = lax.ppermute(halo_b, 'space', pairs_b)  1.91 us
    ppermute x1, starting transfers between devices, shards(): edge_b = lax.ppermute(sent_b, 'space', pairs_b)  1.91 us
    ppermute x1, waiting for transfers between devices, shards(): edge_a = lax.ppermute(sent_a, 'space', pairs_a)  1.72 us
    ppermute x1, starting transfers between devices, shards(): edge_a = lax.ppermute(sent_a, 'space', pairs_a)  1.68 us
    ppermute x1, starting transfers between devices, shards(): coef_a = lax.ppermute(halo_a, 'space', pairs_a)  1.24 us
  transfers between devices with their start and end apart: 10, of which 6 were waited for; matrix products, arithmetic and copies ran while one was open for 0% of the time, Pallas kernels for 5%

profile of v7, /device:TPU:9, one launch (start us, length us, event | category | flops | bytes accessed | tf_op | source)
XLA Modules:
  0.0 26.4 jit_solution(17645535624770926390)
XLA Ops:
  0.0 1.2 %shard_map.55 = (f32[136,128]{1,0:T(8,128)S(1)}, f32[136,128]{1,0:T(8,128)S(1)}, f32[136,128]{1,0:T(8,128)S(1)}, f32[136,128]{1,0:T(8,128)S(1)}, f32[248,128]{1,...) custom-call(f32[16,4096]{1,0:T(8,128)} %bitcast.1, ...), custom_call_target="tpu_custom_call" | custom-call | tf_op jit(solution)/shard_map/pallas_call | solution.py:476
  1.3 0.7 %collective-permute-start = (f32[136,128]{1,0:T(8,128)S(1)}, f32[136,128]{1,0:T(8,128)S(1)}, u32[]{:S(2)}, u32[]{:S(2)}) collective-permute-start(f32[136,128]{1,0:T(8,128)S(1)} %get-tuple-element.34), channel_id=1, source_target_pairs={{0,8},{8,0},{16,24},{24,16},{1,9},{9,1},{17,25},{25,17},{2,10},{10... | collective-permute-start | bytes 208904 | tf_op jit(solution)/shard_map/ppermute | solution.py:501
  2.0 1.2 %collective-permute-start.1 = (f32[136,128]{1,0:T(8,128)S(1)}, f32[136,128]{1,0:T(8,128)S(1)}, u32[]{:S(2)}, u32[]{:S(2)}) collective-permute-start(f32[136,128]{1,0:T(8,128)S(1)} %get-tuple-element.35), channel_id=1, source_target_pairs={{0,16},{8,24},{16,0},{24,8},{1,17},{9,25},{17,1},{25,9},{2,18},{10... | collective-permute-start | bytes 208904 | tf_op jit(solution)/shard_map/ppermute | solution.py:501
  3.2 0.5 %collective-permute-start.2 = (f32[136,128]{1,0:T(8,128)S(1)}, f32[136,128]{1,0:T(8,128)S(1)}, u32[]{:S(2)}, u32[]{:S(2)}) collective-permute-start(f32[136,128]{1,0:T(8,128)S(1)} %get-tuple-element.36), channel_id=1, source_target_pairs={{0,24},{8,16},{16,8},{24,0},{1,25},{9,17},{17,9},{25,1},{2,26},{10... | collective-permute-start | bytes 208904 | tf_op jit(solution)/shard_map/ppermute | solution.py:501
  3.7 1.2 %collective-permute-start.3 = (f32[248,128]{1,0:T(8,128)S(1)}, f32[248,128]{1,0:T(8,128)S(1)}, u32[]{:S(2)}, u32[]{:S(2)}) collective-permute-start(f32[248,128]{1,0:T(8,128)S(1)} %get-tuple-element.40), channel_id=1, source_target_pairs={{0,1},{1,0},{2,3},{3,2},{4,5},{5,4},{6,7},{7,6},{8,9},{9,8},{10,11... | collective-permute-start | bytes 380936 | tf_op jit(solution)/shard_map/ppermute | solution.py:520
  5.0 1.9 %collective-permute-start.4 = (f32[248,128]{1,0:T(8,128)S(1)}, f32[248,128]{1,0:T(8,128)S(1)}, u32[]{:S(2)}, u32[]{:S(2)}) collective-permute-start(f32[248,128]{1,0:T(8,128)S(1)} %get-tuple-element.41), channel_id=1, source_target_pairs={{1,2},{2,1},{3,4},{4,3},{5,6},{6,5},{9,10},{10,9},{11,12},{12,11},... | collective-permute-start | bytes 380936 | tf_op jit(solution)/shard_map/ppermute | solution.py:521
  6.9 0.0 collective-permute-done.from_core
  6.9 0.0 collective-permute-done.1.from_x
  6.9 0.8 %collective-permute-done.2.from_both = f32[136,128]{1,0:T(8,128)S(1)} collective-permute-done((f32[136,128]{1,0:T(8,128)S(1)}, f32[136,128]{1,0:T(8,128)S(1)}, u32[]{:S(2)}, u32[]{:S(2)}) %collective-permute-start.2) | collective-permute-done | bytes 69664 | tf_op jit(solution)/shard_map/ppermute | solution.py:501
  7.7 0.2 shard_map.56
  7.9 1.7 %collective-permute-start.5 = (f32[184,128]{1,0:T(8,128)S(1)}, f32[184,128]{1,0:T(8,128)S(1)}, u32[]{:S(2)}, u32[]{:S(2)}) collective-permute-start(f32[184,128]{1,0:T(8,128)S(1)} %get-tuple-element.55), channel_id=1, source_target_pairs={{0,1},{1,0},{2,3},{3,2},{4,5},{5,4},{6,7},{7,6},{8,9},{9,8},{10,11... | collective-permute-start | bytes 282632 | tf_op jit(solution)/shard_map/ppermute | solution.py:524
  9.6 1.9 %collective-permute-start.6 = (f32[184,128]{1,0:T(8,128)S(1)}, f32[184,128]{1,0:T(8,128)S(1)}, u32[]{:S(2)}, u32[]{:S(2)}) collective-permute-start(f32[184,128]{1,0:T(8,128)S(1)} %get-tuple-element.56), channel_id=1, source_target_pairs={{1,2},{2,1},{3,4},{4,3},{5,6},{6,5},{9,10},{10,9},{11,12},{12,11},... | collective-permute-start | bytes 282632 | tf_op jit(solution)/shard_map/ppermute | solution.py:525
  11.5 0.0 collective-permute-done.3.coef_a
  11.5 0.8 %collective-permute-done.4.coef_b = f32[248,128]{1,0:T(8,128)S(1)} collective-permute-done((f32[248,128]{1,0:T(8,128)S(1)}, f32[248,128]{1,0:T(8,128)S(1)}, u32[]{:S(2)}, u32[]{:S(2)}) %collective-permute-start.4) | collective-permute-done | bytes 127008 | tf_op jit(solution)/shard_map/ppermute | solution.py:521
  12.3 1.1 %shard_map.57 = (f32[9,48,128]{2,1,0:T(8,128)S(1)}, f32[9,48,128]{2,1,0:T(8,128)S(1)}, f32[9,48,128]{2,1,0:T(8,128)S(1)}, f32[9,48,128]{2,1,0:T(8,128)S(1)}, f32...) custom-call(f32[3,9,16,128]{3,2,1,0:T(8,128)S(1)} %get-tuple-element, ...), custom_call_target="tpu_custom_call" | custom-call | tf_op jit(solution)/shard_map/pallas_call | solution.py:476
  13.4 1.7 %collective-permute-done.5.edge_a = f32[184,128]{1,0:T(8,128)S(1)} collective-permute-done((f32[184,128]{1,0:T(8,128)S(1)}, f32[184,128]{1,0:T(8,128)S(1)}, u32[]{:S(2)}, u32[]{:S(2)}) %collective-permute-start.5) | collective-permute-done | bytes 94240 | tf_op jit(solution)/shard_map/ppermute | solution.py:524
  15.1 0.8 %collective-permute-done.6.edge_b = f32[184,128]{1,0:T(8,128)S(1)} collective-permute-done((f32[184,128]{1,0:T(8,128)S(1)}, f32[184,128]{1,0:T(8,128)S(1)}, u32[]{:S(2)}, u32[]{:S(2)}) %collective-permute-start.6) | collective-permute-done | bytes 94240 | tf_op jit(solution)/shard_map/ppermute | solution.py:525
  15.9 2.4 %shard_map.58 = (f32[16,1024]{1,0:T(8,128)S(1)}, f32[16,1024]{1,0:T(8,128)S(1)}, f32[16,1024]{1,0:T(8,128)S(1)}, f32[16,1024]{1,0:T(8,128)S(1)}) custom-call(f32[4,9,16,128]{3,2,1,0:T(8,128)S(1)} %get-tuple-element.37.fields, f32[9,48,128]{2,1,0:T(8,128)S(1)} %get-tuple-element.42.cond_x, f32[9,48,128]{2,1,0:T(8,128)S(1)} %get-tuple-element.43.cond_y, ...), custom_call_target="tpu_custom_call" | custom-call | tf_op jit(solution)/shard_map/pallas_call | solution.py:476
  18.2 2.1 %collective-permute-start.7 = (f32[16,1024]{1,0:T(8,128)S(1)}, f32[16,1024]{1,0:T(8,128)S(1)}, u32[]{:S(2)}, u32[]{:S(2)}) collective-permute-start(f32[16,1024]{1,0:T(8,128)S(1)} %get-tuple-element.58), channel_id=1, source_target_pairs={{0,8},{8,0},{16,24},{24,16},{1,9},{9,1},{17,25},{25,17},{2,10},{10... | collective-permute-start | bytes 196616 | tf_op jit(solution)/shard_map/ppermute | solution.py:501
  20.4 1.2 %collective-permute-start.8 = (f32[16,1024]{1,0:T(8,128)S(1)}, f32[16,1024]{1,0:T(8,128)S(1)}, u32[]{:S(2)}, u32[]{:S(2)}) collective-permute-start(f32[16,1024]{1,0:T(8,128)S(1)} %get-tuple-element.59), channel_id=1, source_target_pairs={{0,16},{8,24},{16,0},{24,8},{1,17},{9,25},{17,1},{25,9},{2,18},{10... | collective-permute-start | bytes 196616 | tf_op jit(solution)/shard_map/ppermute | solution.py:501
  21.6 0.5 %collective-permute-start.9 = (f32[16,1024]{1,0:T(8,128)S(1)}, f32[16,1024]{1,0:T(8,128)S(1)}, u32[]{:S(2)}, u32[]{:S(2)}) collective-permute-start(f32[16,1024]{1,0:T(8,128)S(1)} %get-tuple-element.60), channel_id=1, source_target_pairs={{0,24},{8,16},{16,8},{24,0},{1,25},{9,17},{17,9},{25,1},{2,26},{10... | collective-permute-start | bytes 196616 | tf_op jit(solution)/shard_map/ppermute | solution.py:501
  22.1 2.0 %collective-permute-done.8.from_x = f32[16,1024]{1,0:T(8,128)S(1)} collective-permute-done((f32[16,1024]{1,0:T(8,128)S(1)}, f32[16,1024]{1,0:T(8,128)S(1)}, u32[]{:S(2)}, u32[]{:S(2)}) %collective-permute-start.8) | collective-permute-done | bytes 65568 | tf_op jit(solution)/shard_map/ppermute | solution.py:501
  24.0 1.6 %collective-permute-done.9.from_both = f32[16,1024]{1,0:T(8,128)S(1)} collective-permute-done((f32[16,1024]{1,0:T(8,128)S(1)}, f32[16,1024]{1,0:T(8,128)S(1)}, u32[]{:S(2)}, u32[]{:S(2)}) %collective-permute-start.9) | collective-permute-done | bytes 65568 | tf_op jit(solution)/shard_map/ppermute | solution.py:501
  25.6 0.7 %shard_map.59 = f32[1,16,4096]{2,1,0:T(8,128)} custom-call(f32[16,1024]{1,0:T(8,128)S(1)} %get-tuple-element.57.own, f32[16,1024]{1,0:T(8,128)S(1)} %collective-permute-done.7.from_core, f32[16,1024]{1,0:T(8,128)S(1)} %collective-permute-done.8.from_x, f32[16,1024]{1,0:T(8,128)S(1)} %collective-permute-done.9.from_both), custom_call_target="tpu_custom_call" | custom-call | tf_op jit(solution)/shard_map/pallas_call | solution.py:476
  (1 shorter events, 0.0 us)
Async XLA Ops:
  1.3 5.6 %collective-permute-start = (f32[136,128]{1,0:T(8,128)S(1)}, f32[136,128]{1,0:T(8,128)S(1)}, u32[]{:S(2)}, u32[]{:S(2)}) collective-permute-start(f32[136,128]{1,0:T(8,128)S(1)} %get-tuple-element.34), channel_id=1, source_target_pairs={{0,8},{8,0},{16,24},{24,16},{1,9},{9,1},{17,25},{25,17},{2,10},{10... | collective-permute-start | bytes 208904 | tf_op jit(solution)/shard_map/ppermute | solution.py:501
  2.0 4.9 %collective-permute-start.1 = (f32[136,128]{1,0:T(8,128)S(1)}, f32[136,128]{1,0:T(8,128)S(1)}, u32[]{:S(2)}, u32[]{:S(2)}) collective-permute-start(f32[136,128]{1,0:T(8,128)S(1)} %get-tuple-element.35), channel_id=1, source_target_pairs={{0,16},{8,24},{16,0},{24,8},{1,17},{9,25},{17,1},{25,9},{2,18},{10... | collective-permute-start | bytes 208904 | tf_op jit(solution)/shard_map/ppermute | solution.py:501
  3.2 4.5 %collective-permute-start.2 = (f32[136,128]{1,0:T(8,128)S(1)}, f32[136,128]{1,0:T(8,128)S(1)}, u32[]{:S(2)}, u32[]{:S(2)}) collective-permute-start(f32[136,128]{1,0:T(8,128)S(1)} %get-tuple-element.36), channel_id=1, source_target_pairs={{0,24},{8,16},{16,8},{24,0},{1,25},{9,17},{17,9},{25,1},{2,26},{10... | collective-permute-start | bytes 208904 | tf_op jit(solution)/shard_map/ppermute | solution.py:501
  3.7 7.8 %collective-permute-start.3 = (f32[248,128]{1,0:T(8,128)S(1)}, f32[248,128]{1,0:T(8,128)S(1)}, u32[]{:S(2)}, u32[]{:S(2)}) collective-permute-start(f32[248,128]{1,0:T(8,128)S(1)} %get-tuple-element.40), channel_id=1, source_target_pairs={{0,1},{1,0},{2,3},{3,2},{4,5},{5,4},{6,7},{7,6},{8,9},{9,8},{10,11... | collective-permute-start | bytes 380936 | tf_op jit(solution)/shard_map/ppermute | solution.py:520
  5.0 7.3 %collective-permute-start.4 = (f32[248,128]{1,0:T(8,128)S(1)}, f32[248,128]{1,0:T(8,128)S(1)}, u32[]{:S(2)}, u32[]{:S(2)}) collective-permute-start(f32[248,128]{1,0:T(8,128)S(1)} %get-tuple-element.41), channel_id=1, source_target_pairs={{1,2},{2,1},{3,4},{4,3},{5,6},{6,5},{9,10},{10,9},{11,12},{12,11},... | collective-permute-start | bytes 380936 | tf_op jit(solution)/shard_map/ppermute | solution.py:521
  7.9 7.2 %collective-permute-start.5 = (f32[184,128]{1,0:T(8,128)S(1)}, f32[184,128]{1,0:T(8,128)S(1)}, u32[]{:S(2)}, u32[]{:S(2)}) collective-permute-start(f32[184,128]{1,0:T(8,128)S(1)} %get-tuple-element.55), channel_id=1, source_target_pairs={{0,1},{1,0},{2,3},{3,2},{4,5},{5,4},{6,7},{7,6},{8,9},{9,8},{10,11... | collective-permute-start | bytes 282632 | tf_op jit(solution)/shard_map/ppermute | solution.py:524
  9.6 6.3 %collective-permute-start.6 = (f32[184,128]{1,0:T(8,128)S(1)}, f32[184,128]{1,0:T(8,128)S(1)}, u32[]{:S(2)}, u32[]{:S(2)}) collective-permute-start(f32[184,128]{1,0:T(8,128)S(1)} %get-tuple-element.56), channel_id=1, source_target_pairs={{1,2},{2,1},{3,4},{4,3},{5,6},{6,5},{9,10},{10,9},{11,12},{12,11},... | collective-permute-start | bytes 282632 | tf_op jit(solution)/shard_map/ppermute | solution.py:525
  18.2 3.8 %collective-permute-start.7 = (f32[16,1024]{1,0:T(8,128)S(1)}, f32[16,1024]{1,0:T(8,128)S(1)}, u32[]{:S(2)}, u32[]{:S(2)}) collective-permute-start(f32[16,1024]{1,0:T(8,128)S(1)} %get-tuple-element.58), channel_id=1, source_target_pairs={{0,8},{8,0},{16,24},{24,16},{1,9},{9,1},{17,25},{25,17},{2,10},{10... | collective-permute-start | bytes 196616 | tf_op jit(solution)/shard_map/ppermute | solution.py:501
  20.4 3.7 %collective-permute-start.8 = (f32[16,1024]{1,0:T(8,128)S(1)}, f32[16,1024]{1,0:T(8,128)S(1)}, u32[]{:S(2)}, u32[]{:S(2)}) collective-permute-start(f32[16,1024]{1,0:T(8,128)S(1)} %get-tuple-element.59), channel_id=1, source_target_pairs={{0,16},{8,24},{16,0},{24,8},{1,17},{9,25},{17,1},{25,9},{2,18},{10... | collective-permute-start | bytes 196616 | tf_op jit(solution)/shard_map/ppermute | solution.py:501
  21.6 4.0 %collective-permute-start.9 = (f32[16,1024]{1,0:T(8,128)S(1)}, f32[16,1024]{1,0:T(8,128)S(1)}, u32[]{:S(2)}, u32[]{:S(2)}) collective-permute-start(f32[16,1024]{1,0:T(8,128)S(1)} %get-tuple-element.60), channel_id=1, source_target_pairs={{0,24},{8,16},{16,8},{24,0},{1,25},{9,17},{17,9},{25,1},{2,26},{10... | collective-permute-start | bytes 196616 | tf_op jit(solution)/shard_map/ppermute | solution.py:501

commit v8 on v7

--- a/solution.py
+++ b/solution.py
@@ -360,11 +360,12 @@
             return value, pltpu.roll(value, LANE - width, 1), pltpu.roll(value, width, 1)
 
         states = [[load(item[0], -1), load(item[0], 0)] for item in active]
+        ends = [tuple(state) for state in states]
         for chunk in range(chunks):
             own = [ref[chunk, here] for ref in (diagonal, up, down, east, west)]
-            for (values, put, _, added), state in zip(active, states):
+            for (values, put, _, added), state, (last, start) in zip(active, states, ends):
                 before, now = state
-                after = load(values, chunk + 1)
+                after = start if chunk + 1 == chunks else last if chunk + 2 == chunks else load(values, chunk + 1)
                 right = jnp.where(lane < LANE - width, now[1], after[1])
                 left = jnp.where(lane < width, before[2], now[2])
                 total = (own[3] * right + own[4] * left) + (own[2] * values[chunk, below] + own[1] * values[chunk, above])

time: 26.5 us -> 26.4 us (level)
  no operation moved by 1% of the time
where the time goes in v8:
time: 26.4 us; the launch traced here: 26.2 us
  starting transfers between devices  13 us (49%)
  waiting for transfers between devices  7.7 us (29%)
  Pallas kernels  5.44 us (21%)
    ppermute x6, starting transfers between devices, trade(): lax.ppermute(blocks[slot], 'tm', [(i, i ^ slot) for i in range(groups)])  6.27 us
    pallas_call x5, Pallas kernels, call(): pl.pallas_call(kernel, out_shape=[jax.ShapeDtypeStruct(shape, jnp.float32...  5.44 us
    ppermute x6, waiting for transfers between devices, trade(): lax.ppermute(blocks[slot], 'tm', [(i, i ^ slot) for i in range(groups)])  4.39 us
    ppermute x1, starting transfers between devices, shards(): coef_b = lax.ppermute(halo_b, 'space', pairs_b)  1.91 us
    ppermute x1, starting transfers between devices, shards(): edge_b = lax.ppermute(sent_b, 'space', pairs_b)  1.91 us
    ppermute x1, waiting for transfers between devices, shards(): edge_a = lax.ppermute(sent_a, 'space', pairs_a)  1.76 us
    ppermute x1, starting transfers between devices, shards(): edge_a = lax.ppermute(sent_a, 'space', pairs_a)  1.68 us
    ppermute x1, starting transfers between devices, shards(): coef_a = lax.ppermute(halo_a, 'space', pairs_a)  1.24 us
  transfers between devices with their start and end apart: 10, of which 6 were waited for; matrix products, arithmetic and copies ran while one was open for 0% of the time, Pallas kernels for 5%

profile of v8, /device:TPU:9, one launch (start us, length us, event | category | flops | bytes accessed | tf_op | source)
XLA Modules:
  0.0 26.2 jit_solution(2187206909737750729)
XLA Ops:
  0.0 1.2 %shard_map.55 = (f32[136,128]{1,0:T(8,128)S(1)}, f32[136,128]{1,0:T(8,128)S(1)}, f32[136,128]{1,0:T(8,128)S(1)}, f32[136,128]{1,0:T(8,128)S(1)}, f32[248,128]{1,...) custom-call(f32[16,4096]{1,0:T(8,128)} %bitcast.1, ...), custom_call_target="tpu_custom_call" | custom-call | tf_op jit(solution)/shard_map/pallas_call | solution.py:477
  1.3 0.7 %collective-permute-start = (f32[136,128]{1,0:T(8,128)S(1)}, f32[136,128]{1,0:T(8,128)S(1)}, u32[]{:S(2)}, u32[]{:S(2)}) collective-permute-start(f32[136,128]{1,0:T(8,128)S(1)} %get-tuple-element.34), channel_id=1, source_target_pairs={{0,8},{8,0},{16,24},{24,16},{1,9},{9,1},{17,25},{25,17},{2,10},{10... | collective-permute-start | bytes 208904 | tf_op jit(solution)/shard_map/ppermute | solution.py:502
  2.0 1.2 %collective-permute-start.1 = (f32[136,128]{1,0:T(8,128)S(1)}, f32[136,128]{1,0:T(8,128)S(1)}, u32[]{:S(2)}, u32[]{:S(2)}) collective-permute-start(f32[136,128]{1,0:T(8,128)S(1)} %get-tuple-element.35), channel_id=1, source_target_pairs={{0,16},{8,24},{16,0},{24,8},{1,17},{9,25},{17,1},{25,9},{2,18},{10... | collective-permute-start | bytes 208904 | tf_op jit(solution)/shard_map/ppermute | solution.py:502
  3.2 0.5 %collective-permute-start.2 = (f32[136,128]{1,0:T(8,128)S(1)}, f32[136,128]{1,0:T(8,128)S(1)}, u32[]{:S(2)}, u32[]{:S(2)}) collective-permute-start(f32[136,128]{1,0:T(8,128)S(1)} %get-tuple-element.36), channel_id=1, source_target_pairs={{0,24},{8,16},{16,8},{24,0},{1,25},{9,17},{17,9},{25,1},{2,26},{10... | collective-permute-start | bytes 208904 | tf_op jit(solution)/shard_map/ppermute | solution.py:502
  3.7 1.2 %collective-permute-start.3 = (f32[248,128]{1,0:T(8,128)S(1)}, f32[248,128]{1,0:T(8,128)S(1)}, u32[]{:S(2)}, u32[]{:S(2)}) collective-permute-start(f32[248,128]{1,0:T(8,128)S(1)} %get-tuple-element.40), channel_id=1, source_target_pairs={{0,1},{1,0},{2,3},{3,2},{4,5},{5,4},{6,7},{7,6},{8,9},{9,8},{10,11... | collective-permute-start | bytes 380936 | tf_op jit(solution)/shard_map/ppermute | solution.py:521
  5.0 1.9 %collective-permute-start.4 = (f32[248,128]{1,0:T(8,128)S(1)}, f32[248,128]{1,0:T(8,128)S(1)}, u32[]{:S(2)}, u32[]{:S(2)}) collective-permute-start(f32[248,128]{1,0:T(8,128)S(1)} %get-tuple-element.41), channel_id=1, source_target_pairs={{1,2},{2,1},{3,4},{4,3},{5,6},{6,5},{9,10},{10,9},{11,12},{12,11},... | collective-permute-start | bytes 380936 | tf_op jit(solution)/shard_map/ppermute | solution.py:522
  6.9 0.0 collective-permute-done.from_core
  6.9 0.0 collective-permute-done.1.from_x
  6.9 0.8 %collective-permute-done.2.from_both = f32[136,128]{1,0:T(8,128)S(1)} collective-permute-done((f32[136,128]{1,0:T(8,128)S(1)}, f32[136,128]{1,0:T(8,128)S(1)}, u32[]{:S(2)}, u32[]{:S(2)}) %collective-permute-start.2) | collective-permute-done | bytes 69664 | tf_op jit(solution)/shard_map/ppermute | solution.py:502
  7.7 0.2 shard_map.56
  7.9 1.7 %collective-permute-start.5 = (f32[184,128]{1,0:T(8,128)S(1)}, f32[184,128]{1,0:T(8,128)S(1)}, u32[]{:S(2)}, u32[]{:S(2)}) collective-permute-start(f32[184,128]{1,0:T(8,128)S(1)} %get-tuple-element.55), channel_id=1, source_target_pairs={{0,1},{1,0},{2,3},{3,2},{4,5},{5,4},{6,7},{7,6},{8,9},{9,8},{10,11... | collective-permute-start | bytes 282632 | tf_op jit(solution)/shard_map/ppermute | solution.py:525
  9.6 1.9 %collective-permute-start.6 = (f32[184,128]{1,0:T(8,128)S(1)}, f32[184,128]{1,0:T(8,128)S(1)}, u32[]{:S(2)}, u32[]{:S(2)}) collective-permute-start(f32[184,128]{1,0:T(8,128)S(1)} %get-tuple-element.56), channel_id=1, source_target_pairs={{1,2},{2,1},{3,4},{4,3},{5,6},{6,5},{9,10},{10,9},{11,12},{12,11},... | collective-permute-start | bytes 282632 | tf_op jit(solution)/shard_map/ppermute | solution.py:526
  11.5 0.0 collective-permute-done.3.coef_a
  11.5 0.8 %collective-permute-done.4.coef_b = f32[248,128]{1,0:T(8,128)S(1)} collective-permute-done((f32[248,128]{1,0:T(8,128)S(1)}, f32[248,128]{1,0:T(8,128)S(1)}, u32[]{:S(2)}, u32[]{:S(2)}) %collective-permute-start.4) | collective-permute-done | bytes 127008 | tf_op jit(solution)/shard_map/ppermute | solution.py:522
  12.3 1.1 %shard_map.57 = (f32[9,48,128]{2,1,0:T(8,128)S(1)}, f32[9,48,128]{2,1,0:T(8,128)S(1)}, f32[9,48,128]{2,1,0:T(8,128)S(1)}, f32[9,48,128]{2,1,0:T(8,128)S(1)}, f32...) custom-call(f32[3,9,16,128]{3,2,1,0:T(8,128)S(1)} %get-tuple-element, ...), custom_call_target="tpu_custom_call" | custom-call | tf_op jit(solution)/shard_map/pallas_call | solution.py:477
  13.3 1.8 %collective-permute-done.5.edge_a = f32[184,128]{1,0:T(8,128)S(1)} collective-permute-done((f32[184,128]{1,0:T(8,128)S(1)}, f32[184,128]{1,0:T(8,128)S(1)}, u32[]{:S(2)}, u32[]{:S(2)}) %collective-permute-start.5) | collective-permute-done | bytes 94240 | tf_op jit(solution)/shard_map/ppermute | solution.py:525
  15.1 0.8 %collective-permute-done.6.edge_b = f32[184,128]{1,0:T(8,128)S(1)} collective-permute-done((f32[184,128]{1,0:T(8,128)S(1)}, f32[184,128]{1,0:T(8,128)S(1)}, u32[]{:S(2)}, u32[]{:S(2)}) %collective-permute-start.6) | collective-permute-done | bytes 94240 | tf_op jit(solution)/shard_map/ppermute | solution.py:526
  15.9 2.2 %shard_map.58 = (f32[16,1024]{1,0:T(8,128)S(1)}, f32[16,1024]{1,0:T(8,128)S(1)}, f32[16,1024]{1,0:T(8,128)S(1)}, f32[16,1024]{1,0:T(8,128)S(1)}) custom-call(f32[4,9,16,128]{3,2,1,0:T(8,128)S(1)} %get-tuple-element.37.fields, f32[9,48,128]{2,1,0:T(8,128)S(1)} %get-tuple-element.42.cond_x, f32[9,48,128]{2,1,0:T(8,128)S(1)} %get-tuple-element.43.cond_y, ...), custom_call_target="tpu_custom_call" | custom-call | tf_op jit(solution)/shard_map/pallas_call | solution.py:477
  18.1 2.1 %collective-permute-start.7 = (f32[16,1024]{1,0:T(8,128)S(1)}, f32[16,1024]{1,0:T(8,128)S(1)}, u32[]{:S(2)}, u32[]{:S(2)}) collective-permute-start(f32[16,1024]{1,0:T(8,128)S(1)} %get-tuple-element.58), channel_id=1, source_target_pairs={{0,8},{8,0},{16,24},{24,16},{1,9},{9,1},{17,25},{25,17},{2,10},{10... | collective-permute-start | bytes 196616 | tf_op jit(solution)/shard_map/ppermute | solution.py:502
  20.2 1.2 %collective-permute-start.8 = (f32[16,1024]{1,0:T(8,128)S(1)}, f32[16,1024]{1,0:T(8,128)S(1)}, u32[]{:S(2)}, u32[]{:S(2)}) collective-permute-start(f32[16,1024]{1,0:T(8,128)S(1)} %get-tuple-element.59), channel_id=1, source_target_pairs={{0,16},{8,24},{16,0},{24,8},{1,17},{9,25},{17,1},{25,9},{2,18},{10... | collective-permute-start | bytes 196616 | tf_op jit(solution)/shard_map/ppermute | solution.py:502
  21.4 0.5 %collective-permute-start.9 = (f32[16,1024]{1,0:T(8,128)S(1)}, f32[16,1024]{1,0:T(8,128)S(1)}, u32[]{:S(2)}, u32[]{:S(2)}) collective-permute-start(f32[16,1024]{1,0:T(8,128)S(1)} %get-tuple-element.60), channel_id=1, source_target_pairs={{0,24},{8,16},{16,8},{24,0},{1,25},{9,17},{17,9},{25,1},{2,26},{10... | collective-permute-start | bytes 196616 | tf_op jit(solution)/shard_map/ppermute | solution.py:502
  21.9 2.0 %collective-permute-done.8.from_x = f32[16,1024]{1,0:T(8,128)S(1)} collective-permute-done((f32[16,1024]{1,0:T(8,128)S(1)}, f32[16,1024]{1,0:T(8,128)S(1)}, u32[]{:S(2)}, u32[]{:S(2)}) %collective-permute-start.8) | collective-permute-done | bytes 65568 | tf_op jit(solution)/shard_map/ppermute | solution.py:502
  23.9 1.6 %collective-permute-done.9.from_both = f32[16,1024]{1,0:T(8,128)S(1)} collective-permute-done((f32[16,1024]{1,0:T(8,128)S(1)}, f32[16,1024]{1,0:T(8,128)S(1)}, u32[]{:S(2)}, u32[]{:S(2)}) %collective-permute-start.9) | collective-permute-done | bytes 65568 | tf_op jit(solution)/shard_map/ppermute | solution.py:502
  25.5 0.7 %shard_map.59 = f32[1,16,4096]{2,1,0:T(8,128)} custom-call(f32[16,1024]{1,0:T(8,128)S(1)} %get-tuple-element.57.own, f32[16,1024]{1,0:T(8,128)S(1)} %collective-permute-done.7.from_core, f32[16,1024]{1,0:T(8,128)S(1)} %collective-permute-done.8.from_x, f32[16,1024]{1,0:T(8,128)S(1)} %collective-permute-done.9.from_both), custom_call_target="tpu_custom_call" | custom-call | tf_op jit(solution)/shard_map/pallas_call | solution.py:477
  (1 shorter events, 0.0 us)
Async XLA Ops:
  1.3 5.6 %collective-permute-start = (f32[136,128]{1,0:T(8,128)S(1)}, f32[136,128]{1,0:T(8,128)S(1)}, u32[]{:S(2)}, u32[]{:S(2)}) collective-permute-start(f32[136,128]{1,0:T(8,128)S(1)} %get-tuple-element.34), channel_id=1, source_target_pairs={{0,8},{8,0},{16,24},{24,16},{1,9},{9,1},{17,25},{25,17},{2,10},{10... | collective-permute-start | bytes 208904 | tf_op jit(solution)/shard_map/ppermute | solution.py:502
  2.0 4.9 %collective-permute-start.1 = (f32[136,128]{1,0:T(8,128)S(1)}, f32[136,128]{1,0:T(8,128)S(1)}, u32[]{:S(2)}, u32[]{:S(2)}) collective-permute-start(f32[136,128]{1,0:T(8,128)S(1)} %get-tuple-element.35), channel_id=1, source_target_pairs={{0,16},{8,24},{16,0},{24,8},{1,17},{9,25},{17,1},{25,9},{2,18},{10... | collective-permute-start | bytes 208904 | tf_op jit(solution)/shard_map/ppermute | solution.py:502
  3.2 4.5 %collective-permute-start.2 = (f32[136,128]{1,0:T(8,128)S(1)}, f32[136,128]{1,0:T(8,128)S(1)}, u32[]{:S(2)}, u32[]{:S(2)}) collective-permute-start(f32[136,128]{1,0:T(8,128)S(1)} %get-tuple-element.36), channel_id=1, source_target_pairs={{0,24},{8,16},{16,8},{24,0},{1,25},{9,17},{17,9},{25,1},{2,26},{10... | collective-permute-start | bytes 208904 | tf_op jit(solution)/shard_map/ppermute | solution.py:502
  3.7 7.8 %collective-permute-start.3 = (f32[248,128]{1,0:T(8,128)S(1)}, f32[248,128]{1,0:T(8,128)S(1)}, u32[]{:S(2)}, u32[]{:S(2)}) collective-permute-start(f32[248,128]{1,0:T(8,128)S(1)} %get-tuple-element.40), channel_id=1, source_target_pairs={{0,1},{1,0},{2,3},{3,2},{4,5},{5,4},{6,7},{7,6},{8,9},{9,8},{10,11... | collective-permute-start | bytes 380936 | tf_op jit(solution)/shard_map/ppermute | solution.py:521
  5.0 7.3 %collective-permute-start.4 = (f32[248,128]{1,0:T(8,128)S(1)}, f32[248,128]{1,0:T(8,128)S(1)}, u32[]{:S(2)}, u32[]{:S(2)}) collective-permute-start(f32[248,128]{1,0:T(8,128)S(1)} %get-tuple-element.41), channel_id=1, source_target_pairs={{1,2},{2,1},{3,4},{4,3},{5,6},{6,5},{9,10},{10,9},{11,12},{12,11},... | collective-permute-start | bytes 380936 | tf_op jit(solution)/shard_map/ppermute | solution.py:522
  7.9 7.2 %collective-permute-start.5 = (f32[184,128]{1,0:T(8,128)S(1)}, f32[184,128]{1,0:T(8,128)S(1)}, u32[]{:S(2)}, u32[]{:S(2)}) collective-permute-start(f32[184,128]{1,0:T(8,128)S(1)} %get-tuple-element.55), channel_id=1, source_target_pairs={{0,1},{1,0},{2,3},{3,2},{4,5},{5,4},{6,7},{7,6},{8,9},{9,8},{10,11... | collective-permute-start | bytes 282632 | tf_op jit(solution)/shard_map/ppermute | solution.py:525
  9.6 6.3 %collective-permute-start.6 = (f32[184,128]{1,0:T(8,128)S(1)}, f32[184,128]{1,0:T(8,128)S(1)}, u32[]{:S(2)}, u32[]{:S(2)}) collective-permute-start(f32[184,128]{1,0:T(8,128)S(1)} %get-tuple-element.56), channel_id=1, source_target_pairs={{1,2},{2,1},{3,4},{4,3},{5,6},{6,5},{9,10},{10,9},{11,12},{12,11},... | collective-permute-start | bytes 282632 | tf_op jit(solution)/shard_map/ppermute | solution.py:526
  18.1 3.8 %collective-permute-start.7 = (f32[16,1024]{1,0:T(8,128)S(1)}, f32[16,1024]{1,0:T(8,128)S(1)}, u32[]{:S(2)}, u32[]{:S(2)}) collective-permute-start(f32[16,1024]{1,0:T(8,128)S(1)} %get-tuple-element.58), channel_id=1, source_target_pairs={{0,8},{8,0},{16,24},{24,16},{1,9},{9,1},{17,25},{25,17},{2,10},{10... | collective-permute-start | bytes 196616 | tf_op jit(solution)/shard_map/ppermute | solution.py:502
  20.2 3.7 %collective-permute-start.8 = (f32[16,1024]{1,0:T(8,128)S(1)}, f32[16,1024]{1,0:T(8,128)S(1)}, u32[]{:S(2)}, u32[]{:S(2)}) collective-permute-start(f32[16,1024]{1,0:T(8,128)S(1)} %get-tuple-element.59), channel_id=1, source_target_pairs={{0,16},{8,24},{16,0},{24,8},{1,17},{9,25},{17,1},{25,9},{2,18},{10... | collective-permute-start | bytes 196616 | tf_op jit(solution)/shard_map/ppermute | solution.py:502
  21.4 4.0 %collective-permute-start.9 = (f32[16,1024]{1,0:T(8,128)S(1)}, f32[16,1024]{1,0:T(8,128)S(1)}, u32[]{:S(2)}, u32[]{:S(2)}) collective-permute-start(f32[16,1024]{1,0:T(8,128)S(1)} %get-tuple-element.60), channel_id=1, source_target_pairs={{0,24},{8,16},{16,8},{24,0},{1,25},{9,17},{17,9},{25,1},{2,26},{10... | collective-permute-start | bytes 196616 | tf_op jit(solution)/shard_map/ppermute | solution.py:502

commit v9 on v8

--- a/solution.py
+++ b/solution.py
@@ -334,7 +334,7 @@
     fine = (diagonal, up, cond_x, cond_y, west)
     stops = [source] + [work.at[number] for number in range(FINE_STEPS - 1)]
     for number in range(FINE_STEPS - 1):
-        sweep([(stops[number], stops[number + 1], span(rows, 8 - number), None)], 1, fine)
+        sweep([(stops[number], stops[number + 1], span(rows, 8 - number), None, False)], 1, fine)
     first, count = reach(rows, 6)
     here = slice(first, first + count)
     for chunk in range(chunks + 1):
@@ -342,7 +342,7 @@
         for number in range(FINE_STEPS - 1):
             total = total + work[number, chunk, here]
         response[chunk, here] = total
-    sweep([(error, carried, span(rows, 4), None)], 2, (coarse_d, coarse_u, coarse_x, coarse_y, coarse_w))
+    sweep([(error, carried, span(rows, 4), None, False)], 2, (coarse_d, coarse_u, coarse_x, coarse_y, coarse_w))
 
 
 def sweep(items, width, factors):
@@ -351,7 +351,7 @@
     lane = lanes_of((8, LANE))
     origin = min(item[2][0] for item in items)
     end = max(item[2][1] for item in items)
-    for first in range(origin, end, 8):
+    for first in reversed(range(origin, end, 8)):
         here, above, below = (slice(first + move, first + move + 8) for move in (0, -width, width))
         active = [item for item in items if item[2][0] < first + 8 and item[2][1] > first]
 
@@ -363,7 +363,9 @@
         ends = [tuple(state) for state in states]
         for chunk in range(chunks):
             own = [ref[chunk, here] for ref in (diagonal, up, down, east, west)]
-            for (values, put, _, added), state, (last, start) in zip(active, states, ends):
+            for (values, put, _, added, inner), state, (last, start) in zip(active, states, ends):
+                if inner and chunk == chunks - 1:
+                    continue
                 before, now = state
                 after = start if chunk + 1 == chunks else last if chunk + 2 == chunks else load(values, chunk + 1)
                 right = jnp.where(lane < LANE - width, now[1], after[1])
@@ -427,7 +429,8 @@
                 stops = [guess.at[slot], first, second, first, guess.at[slot + given]]
                 needed = span(rows, deep + FINE_STEPS - 1 - number)
                 added = add_response if number == FINE_STEPS - 1 else None
-                items.append((stops[number], stops[number + 1], needed, added))
+                inner = deep == 0 and number == FINE_STEPS - 1
+                items.append((stops[number], stops[number + 1], needed, added, inner))
             sweep(items, 1, fine)
 
     propagate((0, 1, 2), (6, 4, 0))
@@ -443,7 +446,8 @@
         error[1, chunk, here] = carried[chunk, here] + residual(1, chunk, here)
     for group in range(2, groups):
         needed = span(rows, 2 * (groups - 1 - group))
-        sweep([(error.at[group - 1], error.at[group], needed, functools.partial(residual, group))], 2, coarse)
+        inner = group == groups - 1
+        sweep([(error.at[group - 1], error.at[group], needed, functools.partial(residual, group), inner)], 2, coarse)
     error[0, :, HALO:low] = start_error[:, HALO:low]
 
     member = lax.axis_index("tm")

time: 26.4 us -> 26.3 us (level)
  no operation moved by 1% of the time
where the time goes in v9:
time: 26.3 us; the launch traced here: 26.1 us
  starting transfers between devices  13 us (49%)
  waiting for transfers between devices  7.73 us (29%)
  Pallas kernels  5.31 us (20%)
    ppermute x6, starting transfers between devices, trade(): lax.ppermute(blocks[slot], 'tm', [(i, i ^ slot) for i in range(groups)])  6.26 us
    pallas_call x5, Pallas kernels, call(): pl.pallas_call(kernel, out_shape=[jax.ShapeDtypeStruct(shape, jnp.float32...  5.31 us
    ppermute x6, waiting for transfers between devices, trade(): lax.ppermute(blocks[slot], 'tm', [(i, i ^ slot) for i in range(groups)])  4.39 us
    ppermute x1, starting transfers between devices, shards(): coef_b = lax.ppermute(halo_b, 'space', pairs_b)  1.91 us
    ppermute x1, starting transfers between devices, shards(): edge_b = lax.ppermute(sent_b, 'space', pairs_b)  1.91 us
    ppermute x1, waiting for transfers between devices, shards(): edge_a = lax.ppermute(sent_a, 'space', pairs_a)  1.8 us
    ppermute x1, starting transfers between devices, shards(): edge_a = lax.ppermute(sent_a, 'space', pairs_a)  1.68 us
    ppermute x1, starting transfers between devices, shards(): coef_a = lax.ppermute(halo_a, 'space', pairs_a)  1.24 us
  transfers between devices with their start and end apart: 10, of which 6 were waited for; matrix products, arithmetic and copies ran while one was open for 0% of the time, Pallas kernels for 5%

profile of v9, /device:TPU:9, one launch (start us, length us, event | category | flops | bytes accessed | tf_op | source)
XLA Modules:
  0.0 26.1 jit_solution(751247529453338075)
XLA Ops:
  0.0 1.2 %shard_map.55 = (f32[136,128]{1,0:T(8,128)S(1)}, f32[136,128]{1,0:T(8,128)S(1)}, f32[136,128]{1,0:T(8,128)S(1)}, f32[136,128]{1,0:T(8,128)S(1)}, f32[248,128]{1,...) custom-call(f32[16,4096]{1,0:T(8,128)} %bitcast.1, ...), custom_call_target="tpu_custom_call" | custom-call | tf_op jit(solution)/shard_map/pallas_call | solution.py:481
  1.3 0.7 %collective-permute-start = (f32[136,128]{1,0:T(8,128)S(1)}, f32[136,128]{1,0:T(8,128)S(1)}, u32[]{:S(2)}, u32[]{:S(2)}) collective-permute-start(f32[136,128]{1,0:T(8,128)S(1)} %get-tuple-element.34), channel_id=1, source_target_pairs={{0,8},{8,0},{16,24},{24,16},{1,9},{9,1},{17,25},{25,17},{2,10},{10... | collective-permute-start | bytes 208904 | tf_op jit(solution)/shard_map/ppermute | solution.py:506
  2.0 1.2 %collective-permute-start.1 = (f32[136,128]{1,0:T(8,128)S(1)}, f32[136,128]{1,0:T(8,128)S(1)}, u32[]{:S(2)}, u32[]{:S(2)}) collective-permute-start(f32[136,128]{1,0:T(8,128)S(1)} %get-tuple-element.35), channel_id=1, source_target_pairs={{0,16},{8,24},{16,0},{24,8},{1,17},{9,25},{17,1},{25,9},{2,18},{10... | collective-permute-start | bytes 208904 | tf_op jit(solution)/shard_map/ppermute | solution.py:506
  3.2 0.5 %collective-permute-start.2 = (f32[136,128]{1,0:T(8,128)S(1)}, f32[136,128]{1,0:T(8,128)S(1)}, u32[]{:S(2)}, u32[]{:S(2)}) collective-permute-start(f32[136,128]{1,0:T(8,128)S(1)} %get-tuple-element.36), channel_id=1, source_target_pairs={{0,24},{8,16},{16,8},{24,0},{1,25},{9,17},{17,9},{25,1},{2,26},{10... | collective-permute-start | bytes 208904 | tf_op jit(solution)/shard_map/ppermute | solution.py:506
  3.7 1.2 %collective-permute-start.3 = (f32[248,128]{1,0:T(8,128)S(1)}, f32[248,128]{1,0:T(8,128)S(1)}, u32[]{:S(2)}, u32[]{:S(2)}) collective-permute-start(f32[248,128]{1,0:T(8,128)S(1)} %get-tuple-element.40), channel_id=1, source_target_pairs={{0,1},{1,0},{2,3},{3,2},{4,5},{5,4},{6,7},{7,6},{8,9},{9,8},{10,11... | collective-permute-start | bytes 380936 | tf_op jit(solution)/shard_map/ppermute | solution.py:525
  5.0 1.9 %collective-permute-start.4 = (f32[248,128]{1,0:T(8,128)S(1)}, f32[248,128]{1,0:T(8,128)S(1)}, u32[]{:S(2)}, u32[]{:S(2)}) collective-permute-start(f32[248,128]{1,0:T(8,128)S(1)} %get-tuple-element.41), channel_id=1, source_target_pairs={{1,2},{2,1},{3,4},{4,3},{5,6},{6,5},{9,10},{10,9},{11,12},{12,11},... | collective-permute-start | bytes 380936 | tf_op jit(solution)/shard_map/ppermute | solution.py:526
  6.9 0.0 collective-permute-done.from_core
  6.9 0.0 collective-permute-done.1.from_x
  6.9 0.8 %collective-permute-done.2.from_both = f32[136,128]{1,0:T(8,128)S(1)} collective-permute-done((f32[136,128]{1,0:T(8,128)S(1)}, f32[136,128]{1,0:T(8,128)S(1)}, u32[]{:S(2)}, u32[]{:S(2)}) %collective-permute-start.2) | collective-permute-done | bytes 69664 | tf_op jit(solution)/shard_map/ppermute | solution.py:506
  7.7 0.2 shard_map.56
  7.9 1.7 %collective-permute-start.5 = (f32[184,128]{1,0:T(8,128)S(1)}, f32[184,128]{1,0:T(8,128)S(1)}, u32[]{:S(2)}, u32[]{:S(2)}) collective-permute-start(f32[184,128]{1,0:T(8,128)S(1)} %get-tuple-element.55), channel_id=1, source_target_pairs={{0,1},{1,0},{2,3},{3,2},{4,5},{5,4},{6,7},{7,6},{8,9},{9,8},{10,11... | collective-permute-start | bytes 282632 | tf_op jit(solution)/shard_map/ppermute | solution.py:529
  9.6 1.9 %collective-permute-start.6 = (f32[184,128]{1,0:T(8,128)S(1)}, f32[184,128]{1,0:T(8,128)S(1)}, u32[]{:S(2)}, u32[]{:S(2)}) collective-permute-start(f32[184,128]{1,0:T(8,128)S(1)} %get-tuple-element.56), channel_id=1, source_target_pairs={{1,2},{2,1},{3,4},{4,3},{5,6},{6,5},{9,10},{10,9},{11,12},{12,11},... | collective-permute-start | bytes 282632 | tf_op jit(solution)/shard_map/ppermute | solution.py:530
  11.5 0.0 collective-permute-done.3.coef_a
  11.5 0.8 %collective-permute-done.4.coef_b = f32[248,128]{1,0:T(8,128)S(1)} collective-permute-done((f32[248,128]{1,0:T(8,128)S(1)}, f32[248,128]{1,0:T(8,128)S(1)}, u32[]{:S(2)}, u32[]{:S(2)}) %collective-permute-start.4) | collective-permute-done | bytes 127008 | tf_op jit(solution)/shard_map/ppermute | solution.py:526
  12.3 1.0 %shard_map.57 = (f32[9,48,128]{2,1,0:T(8,128)S(1)}, f32[9,48,128]{2,1,0:T(8,128)S(1)}, f32[9,48,128]{2,1,0:T(8,128)S(1)}, f32[9,48,128]{2,1,0:T(8,128)S(1)}, f32...) custom-call(f32[3,9,16,128]{3,2,1,0:T(8,128)S(1)} %get-tuple-element, ...), custom_call_target="tpu_custom_call" | custom-call | tf_op jit(solution)/shard_map/pallas_call | solution.py:481
  13.3 1.8 %collective-permute-done.5.edge_a = f32[184,128]{1,0:T(8,128)S(1)} collective-permute-done((f32[184,128]{1,0:T(8,128)S(1)}, f32[184,128]{1,0:T(8,128)S(1)}, u32[]{:S(2)}, u32[]{:S(2)}) %collective-permute-start.5) | collective-permute-done | bytes 94240 | tf_op jit(solution)/shard_map/ppermute | solution.py:529
  15.1 0.8 %collective-permute-done.6.edge_b = f32[184,128]{1,0:T(8,128)S(1)} collective-permute-done((f32[184,128]{1,0:T(8,128)S(1)}, f32[184,128]{1,0:T(8,128)S(1)}, u32[]{:S(2)}, u32[]{:S(2)}) %collective-permute-start.6) | collective-permute-done | bytes 94240 | tf_op jit(solution)/shard_map/ppermute | solution.py:530
  15.9 2.1 %shard_map.58 = (f32[16,1024]{1,0:T(8,128)S(1)}, f32[16,1024]{1,0:T(8,128)S(1)}, f32[16,1024]{1,0:T(8,128)S(1)}, f32[16,1024]{1,0:T(8,128)S(1)}) custom-call(f32[4,9,16,128]{3,2,1,0:T(8,128)S(1)} %get-tuple-element.37.fields, f32[9,48,128]{2,1,0:T(8,128)S(1)} %get-tuple-element.42.cond_x, f32[9,48,128]{2,1,0:T(8,128)S(1)} %get-tuple-element.43.cond_y, ...), custom_call_target="tpu_custom_call" | custom-call | tf_op jit(solution)/shard_map/pallas_call | solution.py:481
  18.0 2.1 %collective-permute-start.7 = (f32[16,1024]{1,0:T(8,128)S(1)}, f32[16,1024]{1,0:T(8,128)S(1)}, u32[]{:S(2)}, u32[]{:S(2)}) collective-permute-start(f32[16,1024]{1,0:T(8,128)S(1)} %get-tuple-element.58), channel_id=1, source_target_pairs={{0,8},{8,0},{16,24},{24,16},{1,9},{9,1},{17,25},{25,17},{2,10},{10... | collective-permute-start | bytes 196616 | tf_op jit(solution)/shard_map/ppermute | solution.py:506
  20.1 1.2 %collective-permute-start.8 = (f32[16,1024]{1,0:T(8,128)S(1)}, f32[16,1024]{1,0:T(8,128)S(1)}, u32[]{:S(2)}, u32[]{:S(2)}) collective-permute-start(f32[16,1024]{1,0:T(8,128)S(1)} %get-tuple-element.59), channel_id=1, source_target_pairs={{0,16},{8,24},{16,0},{24,8},{1,17},{9,25},{17,1},{25,9},{2,18},{10... | collective-permute-start | bytes 196616 | tf_op jit(solution)/shard_map/ppermute | solution.py:506
  21.3 0.5 %collective-permute-start.9 = (f32[16,1024]{1,0:T(8,128)S(1)}, f32[16,1024]{1,0:T(8,128)S(1)}, u32[]{:S(2)}, u32[]{:S(2)}) collective-permute-start(f32[16,1024]{1,0:T(8,128)S(1)} %get-tuple-element.60), channel_id=1, source_target_pairs={{0,24},{8,16},{16,8},{24,0},{1,25},{9,17},{17,9},{25,1},{2,26},{10... | collective-permute-start | bytes 196616 | tf_op jit(solution)/shard_map/ppermute | solution.py:506
  21.8 2.0 %collective-permute-done.8.from_x = f32[16,1024]{1,0:T(8,128)S(1)} collective-permute-done((f32[16,1024]{1,0:T(8,128)S(1)}, f32[16,1024]{1,0:T(8,128)S(1)}, u32[]{:S(2)}, u32[]{:S(2)}) %collective-permute-start.8) | collective-permute-done | bytes 65568 | tf_op jit(solution)/shard_map/ppermute | solution.py:506
  23.8 1.6 %collective-permute-done.9.from_both = f32[16,1024]{1,0:T(8,128)S(1)} collective-permute-done((f32[16,1024]{1,0:T(8,128)S(1)}, f32[16,1024]{1,0:T(8,128)S(1)}, u32[]{:S(2)}, u32[]{:S(2)}) %collective-permute-start.9) | collective-permute-done | bytes 65568 | tf_op jit(solution)/shard_map/ppermute | solution.py:506
  25.4 0.7 %shard_map.59 = f32[1,16,4096]{2,1,0:T(8,128)} custom-call(f32[16,1024]{1,0:T(8,128)S(1)} %get-tuple-element.57.own, f32[16,1024]{1,0:T(8,128)S(1)} %collective-permute-done.7.from_core, f32[16,1024]{1,0:T(8,128)S(1)} %collective-permute-done.8.from_x, f32[16,1024]{1,0:T(8,128)S(1)} %collective-permute-done.9.from_both), custom_call_target="tpu_custom_call" | custom-call | tf_op jit(solution)/shard_map/pallas_call | solution.py:481
  (1 shorter events, 0.0 us)
Async XLA Ops:
  1.3 5.6 %collective-permute-start = (f32[136,128]{1,0:T(8,128)S(1)}, f32[136,128]{1,0:T(8,128)S(1)}, u32[]{:S(2)}, u32[]{:S(2)}) collective-permute-start(f32[136,128]{1,0:T(8,128)S(1)} %get-tuple-element.34), channel_id=1, source_target_pairs={{0,8},{8,0},{16,24},{24,16},{1,9},{9,1},{17,25},{25,17},{2,10},{10... | collective-permute-start | bytes 208904 | tf_op jit(solution)/shard_map/ppermute | solution.py:506
  2.0 4.9 %collective-permute-start.1 = (f32[136,128]{1,0:T(8,128)S(1)}, f32[136,128]{1,0:T(8,128)S(1)}, u32[]{:S(2)}, u32[]{:S(2)}) collective-permute-start(f32[136,128]{1,0:T(8,128)S(1)} %get-tuple-element.35), channel_id=1, source_target_pairs={{0,16},{8,24},{16,0},{24,8},{1,17},{9,25},{17,1},{25,9},{2,18},{10... | collective-permute-start | bytes 208904 | tf_op jit(solution)/shard_map/ppermute | solution.py:506
  3.2 4.5 %collective-permute-start.2 = (f32[136,128]{1,0:T(8,128)S(1)}, f32[136,128]{1,0:T(8,128)S(1)}, u32[]{:S(2)}, u32[]{:S(2)}) collective-permute-start(f32[136,128]{1,0:T(8,128)S(1)} %get-tuple-element.36), channel_id=1, source_target_pairs={{0,24},{8,16},{16,8},{24,0},{1,25},{9,17},{17,9},{25,1},{2,26},{10... | collective-permute-start | bytes 208904 | tf_op jit(solution)/shard_map/ppermute | solution.py:506
  3.7 7.8 %collective-permute-start.3 = (f32[248,128]{1,0:T(8,128)S(1)}, f32[248,128]{1,0:T(8,128)S(1)}, u32[]{:S(2)}, u32[]{:S(2)}) collective-permute-start(f32[248,128]{1,0:T(8,128)S(1)} %get-tuple-element.40), channel_id=1, source_target_pairs={{0,1},{1,0},{2,3},{3,2},{4,5},{5,4},{6,7},{7,6},{8,9},{9,8},{10,11... | collective-permute-start | bytes 380936 | tf_op jit(solution)/shard_map/ppermute | solution.py:525
  5.0 7.3 %collective-permute-start.4 = (f32[248,128]{1,0:T(8,128)S(1)}, f32[248,128]{1,0:T(8,128)S(1)}, u32[]{:S(2)}, u32[]{:S(2)}) collective-permute-start(f32[248,128]{1,0:T(8,128)S(1)} %get-tuple-element.41), channel_id=1, source_target_pairs={{1,2},{2,1},{3,4},{4,3},{5,6},{6,5},{9,10},{10,9},{11,12},{12,11},... | collective-permute-start | bytes 380936 | tf_op jit(solution)/shard_map/ppermute | solution.py:526
  7.9 7.2 %collective-permute-start.5 = (f32[184,128]{1,0:T(8,128)S(1)}, f32[184,128]{1,0:T(8,128)S(1)}, u32[]{:S(2)}, u32[]{:S(2)}) collective-permute-start(f32[184,128]{1,0:T(8,128)S(1)} %get-tuple-element.55), channel_id=1, source_target_pairs={{0,1},{1,0},{2,3},{3,2},{4,5},{5,4},{6,7},{7,6},{8,9},{9,8},{10,11... | collective-permute-start | bytes 282632 | tf_op jit(solution)/shard_map/ppermute | solution.py:529
  9.6 6.3 %collective-permute-start.6 = (f32[184,128]{1,0:T(8,128)S(1)}, f32[184,128]{1,0:T(8,128)S(1)}, u32[]{:S(2)}, u32[]{:S(2)}) collective-permute-start(f32[184,128]{1,0:T(8,128)S(1)} %get-tuple-element.56), channel_id=1, source_target_pairs={{1,2},{2,1},{3,4},{4,3},{5,6},{6,5},{9,10},{10,9},{11,12},{12,11},... | collective-permute-start | bytes 282632 | tf_op jit(solution)/shard_map/ppermute | solution.py:530
  18.0 3.8 %collective-permute-start.7 = (f32[16,1024]{1,0:T(8,128)S(1)}, f32[16,1024]{1,0:T(8,128)S(1)}, u32[]{:S(2)}, u32[]{:S(2)}) collective-permute-start(f32[16,1024]{1,0:T(8,128)S(1)} %get-tuple-element.58), channel_id=1, source_target_pairs={{0,8},{8,0},{16,24},{24,16},{1,9},{9,1},{17,25},{25,17},{2,10},{10... | collective-permute-start | bytes 196616 | tf_op jit(solution)/shard_map/ppermute | solution.py:506
  20.1 3.7 %collective-permute-start.8 = (f32[16,1024]{1,0:T(8,128)S(1)}, f32[16,1024]{1,0:T(8,128)S(1)}, u32[]{:S(2)}, u32[]{:S(2)}) collective-permute-start(f32[16,1024]{1,0:T(8,128)S(1)} %get-tuple-element.59), channel_id=1, source_target_pairs={{0,16},{8,24},{16,0},{24,8},{1,17},{9,25},{17,1},{25,9},{2,18},{10... | collective-permute-start | bytes 196616 | tf_op jit(solution)/shard_map/ppermute | solution.py:506
  21.3 4.0 %collective-permute-start.9 = (f32[16,1024]{1,0:T(8,128)S(1)}, f32[16,1024]{1,0:T(8,128)S(1)}, u32[]{:S(2)}, u32[]{:S(2)}) collective-permute-start(f32[16,1024]{1,0:T(8,128)S(1)} %get-tuple-element.60), channel_id=1, source_target_pairs={{0,24},{8,16},{16,8},{24,0},{1,25},{9,17},{17,9},{25,1},{2,26},{10... | collective-permute-start | bytes 196616 | tf_op jit(solution)/shard_map/ppermute | solution.py:506

commit v10 on v9

--- a/solution.py
+++ b/solution.py
@@ -214,6 +214,11 @@
         take(above, False)
 
     by_side(sides(rows)[0], fill, halo_a, halo_b)
+    strip = lax.axis_index("space")
+
+    @pl.when((strip == 0) | (strip == lax.axis_size("space") - 1))
+    def _():
+        halo_b[...] = jnp.zeros_like(halo_b)
 
 
 def edge_kernel(own, from_core, from_x, from_both, edge_a, edge_b, fields, spare):
@@ -499,6 +504,7 @@
     chunks = own // LANE
     pairs_a = [(i, i ^ 1) for i in range(strips)]
     pairs_b = [(i, j) for k in range(1, strips - 1, 2) for i, j in ((k, k + 1), (k + 1, k))]
+    ring_b = [(i, j) for k in range(1, strips, 2) for i, j in ((k, (k + 1) % strips), ((k + 1) % strips, k))]
 
     def trade(blocks):
         moved = [blocks[0]]
@@ -523,7 +529,7 @@
         [guesses[0], cond_x, cond_y, source, inflow], whole=range(5), copies=5,
     )
     coef_a = lax.ppermute(halo_a, "space", pairs_a)
-    coef_b = lax.ppermute(halo_b, "space", pairs_b)
+    coef_b = lax.ppermute(halo_b, "space", ring_b)
     blocks = trade(blocks)
     sent_a, sent_b, fields = call(edge_kernel, [edge, edge, (groups, chunks + 1, rows, LANE)], [spare], blocks)
     edge_a = lax.ppermute(sent_a, "space", pairs_a)

time: 26.3 us -> 25.4 us (0.966)
  starting transfers between devices: 13 us -> 10.4 us
  waiting for transfers between devices: 7.73 us -> 9.42 us
    ppermute x6, waiting for transfers between devices: 4.39 us -> 6.3 us  [trade(): lax.ppermute(blocks[slot], 'tm', [(i, i ^ slot) for i in range(groups)])]
    ppermute x1, starting transfers between devices: 1.91 us -> 0.01 us  [shards(): coef_b = lax.ppermute(halo_b, 'space', ring_b)]
    ppermute x1, waiting for transfers between devices: 0.77 us -> 2.41 us  [shards(): edge_b = lax.ppermute(sent_b, 'space', pairs_b)]
    ppermute x1, waiting for transfers between devices: 1.8 us -> 0.71 us  [shards(): edge_a = lax.ppermute(sent_a, 'space', pairs_a)]
    ppermute x6, starting transfers between devices: 6.26 us -> 5.41 us  [trade(): lax.ppermute(blocks[slot], 'tm', [(i, i ^ slot) for i in range(groups)])]
    ppermute x1, waiting for transfers between devices: 0.78 us -> 0.01 us  [shards(): coef_b = lax.ppermute(halo_b, 'space', ring_b)]
    ppermute x1, starting transfers between devices: 1.91 us -> 2.52 us  [shards(): edge_b = lax.ppermute(sent_b, 'space', pairs_b)]
    ppermute x1, starting transfers between devices: 1.68 us -> 1.27 us  [shards(): edge_a = lax.ppermute(sent_a, 'space', pairs_a)]
where the time goes in v10:
time: 25.4 us; the launch traced here: 25.2 us
  starting transfers between devices  10.4 us (41%)
  waiting for transfers between devices  9.42 us (37%)
  Pallas kernels  5.33 us (21%)
    ppermute x6, waiting for transfers between devices, trade(): lax.ppermute(blocks[slot], 'tm', [(i, i ^ slot) for i in range(groups)])  6.3 us
    ppermute x6, starting transfers between devices, trade(): lax.ppermute(blocks[slot], 'tm', [(i, i ^ slot) for i in range(groups)])  5.41 us
    pallas_call x5, Pallas kernels, call(): pl.pallas_call(kernel, out_shape=[jax.ShapeDtypeStruct(shape, jnp.float32...  5.33 us
    ppermute x1, starting transfers between devices, shards(): edge_b = lax.ppermute(sent_b, 'space', pairs_b)  2.52 us
    ppermute x1, waiting for transfers between devices, shards(): edge_b = lax.ppermute(sent_b, 'space', pairs_b)  2.41 us
    ppermute x1, starting transfers between devices, shards(): edge_a = lax.ppermute(sent_a, 'space', pairs_a)  1.27 us
    ppermute x1, starting transfers between devices, shards(): coef_a = lax.ppermute(halo_a, 'space', pairs_a)  1.24 us
    ppermute x1, waiting for transfers between devices, shards(): edge_a = lax.ppermute(sent_a, 'space', pairs_a)  0.71 us
  transfers between devices with their start and end apart: 10, of which 6 were waited for; matrix products, arithmetic and copies ran while one was open for 0% of the time, Pallas kernels for 5%

profile of v10, /device:TPU:9, one launch (start us, length us, event | category | flops | bytes accessed | tf_op | source)
XLA Modules:
  0.0 25.2 jit_solution(3888258212232406117)
XLA Ops:
  0.0 1.2 %shard_map.55 = (f32[136,128]{1,0:T(8,128)S(1)}, f32[136,128]{1,0:T(8,128)S(1)}, f32[136,128]{1,0:T(8,128)S(1)}, f32[136,128]{1,0:T(8,128)S(1)}, f32[248,128]{1,...) custom-call(f32[16,4096]{1,0:T(8,128)} %bitcast.1, ...), custom_call_target="tpu_custom_call" | custom-call | tf_op jit(solution)/shard_map/pallas_call | solution.py:486
  1.3 0.7 %collective-permute-start = (f32[136,128]{1,0:T(8,128)S(1)}, f32[136,128]{1,0:T(8,128)S(1)}, u32[]{:S(2)}, u32[]{:S(2)}) collective-permute-start(f32[136,128]{1,0:T(8,128)S(1)} %get-tuple-element.34), channel_id=1, source_target_pairs={{0,8},{8,0},{16,24},{24,16},{1,9},{9,1},{17,25},{25,17},{2,10},{10... | collective-permute-start | bytes 208904 | tf_op jit(solution)/shard_map/ppermute | solution.py:512
  2.0 1.2 %collective-permute-start.1 = (f32[136,128]{1,0:T(8,128)S(1)}, f32[136,128]{1,0:T(8,128)S(1)}, u32[]{:S(2)}, u32[]{:S(2)}) collective-permute-start(f32[136,128]{1,0:T(8,128)S(1)} %get-tuple-element.35), channel_id=1, source_target_pairs={{0,16},{8,24},{16,0},{24,8},{1,17},{9,25},{17,1},{25,9},{2,18},{10... | collective-permute-start | bytes 208904 | tf_op jit(solution)/shard_map/ppermute | solution.py:512
  3.2 0.5 %collective-permute-start.2 = (f32[136,128]{1,0:T(8,128)S(1)}, f32[136,128]{1,0:T(8,128)S(1)}, u32[]{:S(2)}, u32[]{:S(2)}) collective-permute-start(f32[136,128]{1,0:T(8,128)S(1)} %get-tuple-element.36), channel_id=1, source_target_pairs={{0,24},{8,16},{16,8},{24,0},{1,25},{9,17},{17,9},{25,1},{2,26},{10... | collective-permute-start | bytes 208904 | tf_op jit(solution)/shard_map/ppermute | solution.py:512
  3.7 1.2 %collective-permute-start.3 = (f32[248,128]{1,0:T(8,128)S(1)}, f32[248,128]{1,0:T(8,128)S(1)}, u32[]{:S(2)}, u32[]{:S(2)}) collective-permute-start(f32[248,128]{1,0:T(8,128)S(1)} %get-tuple-element.40), channel_id=1, source_target_pairs={{0,1},{1,0},{2,3},{3,2},{4,5},{5,4},{6,7},{7,6},{8,9},{9,8},{10,11... | collective-permute-start | bytes 380936 | tf_op jit(solution)/shard_map/ppermute | solution.py:531
  5.0 0.0 collective-permute-start.4
  5.0 0.0 collective-permute-done.from_core
  5.0 0.8 %collective-permute-done.1.from_x = f32[136,128]{1,0:T(8,128)S(1)} collective-permute-done((f32[136,128]{1,0:T(8,128)S(1)}, f32[136,128]{1,0:T(8,128)S(1)}, u32[]{:S(2)}, u32[]{:S(2)}) %collective-permute-start.1) | collective-permute-done | bytes 69664 | tf_op jit(solution)/shard_map/ppermute | solution.py:512
  5.8 1.9 %collective-permute-done.2.from_both = f32[136,128]{1,0:T(8,128)S(1)} collective-permute-done((f32[136,128]{1,0:T(8,128)S(1)}, f32[136,128]{1,0:T(8,128)S(1)}, u32[]{:S(2)}, u32[]{:S(2)}) %collective-permute-start.2) | collective-permute-done | bytes 69664 | tf_op jit(solution)/shard_map/ppermute | solution.py:512
  7.7 0.2 shard_map.56
  7.9 1.3 %collective-permute-start.5 = (f32[184,128]{1,0:T(8,128)S(1)}, f32[184,128]{1,0:T(8,128)S(1)}, u32[]{:S(2)}, u32[]{:S(2)}) collective-permute-start(f32[184,128]{1,0:T(8,128)S(1)} %get-tuple-element.55), channel_id=1, source_target_pairs={{0,1},{1,0},{2,3},{3,2},{4,5},{5,4},{6,7},{7,6},{8,9},{9,8},{10,11... | collective-permute-start | bytes 282632 | tf_op jit(solution)/shard_map/ppermute | solution.py:535
  9.2 2.5 %collective-permute-start.6 = (f32[184,128]{1,0:T(8,128)S(1)}, f32[184,128]{1,0:T(8,128)S(1)}, u32[]{:S(2)}, u32[]{:S(2)}) collective-permute-start(f32[184,128]{1,0:T(8,128)S(1)} %get-tuple-element.56), channel_id=1, source_target_pairs={{1,2},{2,1},{3,4},{4,3},{5,6},{6,5},{9,10},{10,9},{11,12},{12,11},... | collective-permute-start | bytes 282632 | tf_op jit(solution)/shard_map/ppermute | solution.py:536
  11.7 0.0 collective-permute-done.3.coef_a
  11.7 1.0 %shard_map.57 = (f32[9,48,128]{2,1,0:T(8,128)S(1)}, f32[9,48,128]{2,1,0:T(8,128)S(1)}, f32[9,48,128]{2,1,0:T(8,128)S(1)}, f32[9,48,128]{2,1,0:T(8,128)S(1)}, f32...) custom-call(f32[3,9,16,128]{3,2,1,0:T(8,128)S(1)} %get-tuple-element, ...), custom_call_target="tpu_custom_call" | custom-call | tf_op jit(solution)/shard_map/pallas_call | solution.py:486
  12.8 0.7 %collective-permute-done.5.edge_a = f32[184,128]{1,0:T(8,128)S(1)} collective-permute-done((f32[184,128]{1,0:T(8,128)S(1)}, f32[184,128]{1,0:T(8,128)S(1)}, u32[]{:S(2)}, u32[]{:S(2)}) %collective-permute-start.5) | collective-permute-done | bytes 94240 | tf_op jit(solution)/shard_map/ppermute | solution.py:535
  13.5 2.4 %collective-permute-done.6.edge_b = f32[184,128]{1,0:T(8,128)S(1)} collective-permute-done((f32[184,128]{1,0:T(8,128)S(1)}, f32[184,128]{1,0:T(8,128)S(1)}, u32[]{:S(2)}, u32[]{:S(2)}) %collective-permute-start.6) | collective-permute-done | bytes 94240 | tf_op jit(solution)/shard_map/ppermute | solution.py:536
  15.9 2.1 %shard_map.58 = (f32[16,1024]{1,0:T(8,128)S(1)}, f32[16,1024]{1,0:T(8,128)S(1)}, f32[16,1024]{1,0:T(8,128)S(1)}, f32[16,1024]{1,0:T(8,128)S(1)}) custom-call(f32[4,9,16,128]{3,2,1,0:T(8,128)S(1)} %get-tuple-element.37.fields, f32[9,48,128]{2,1,0:T(8,128)S(1)} %get-tuple-element.42.cond_x, f32[9,48,128]{2,1,0:T(8,128)S(1)} %get-tuple-element.43.cond_y, ...), custom_call_target="tpu_custom_call" | custom-call | tf_op jit(solution)/shard_map/pallas_call | solution.py:486
  18.0 1.3 %collective-permute-start.7 = (f32[16,1024]{1,0:T(8,128)S(1)}, f32[16,1024]{1,0:T(8,128)S(1)}, u32[]{:S(2)}, u32[]{:S(2)}) collective-permute-start(f32[16,1024]{1,0:T(8,128)S(1)} %get-tuple-element.58), channel_id=1, source_target_pairs={{0,8},{8,0},{16,24},{24,16},{1,9},{9,1},{17,25},{25,17},{2,10},{10... | collective-permute-start | bytes 196616 | tf_op jit(solution)/shard_map/ppermute | solution.py:512
  19.3 1.2 %collective-permute-start.8 = (f32[16,1024]{1,0:T(8,128)S(1)}, f32[16,1024]{1,0:T(8,128)S(1)}, u32[]{:S(2)}, u32[]{:S(2)}) collective-permute-start(f32[16,1024]{1,0:T(8,128)S(1)} %get-tuple-element.59), channel_id=1, source_target_pairs={{0,16},{8,24},{16,0},{24,8},{1,17},{9,25},{17,1},{25,9},{2,18},{10... | collective-permute-start | bytes 196616 | tf_op jit(solution)/shard_map/ppermute | solution.py:512
  20.5 0.5 %collective-permute-start.9 = (f32[16,1024]{1,0:T(8,128)S(1)}, f32[16,1024]{1,0:T(8,128)S(1)}, u32[]{:S(2)}, u32[]{:S(2)}) collective-permute-start(f32[16,1024]{1,0:T(8,128)S(1)} %get-tuple-element.60), channel_id=1, source_target_pairs={{0,24},{8,16},{16,8},{24,0},{1,25},{9,17},{17,9},{25,1},{2,26},{10... | collective-permute-start | bytes 196616 | tf_op jit(solution)/shard_map/ppermute | solution.py:512
  21.0 0.0 collective-permute-done.7.from_core
  21.0 2.0 %collective-permute-done.8.from_x = f32[16,1024]{1,0:T(8,128)S(1)} collective-permute-done((f32[16,1024]{1,0:T(8,128)S(1)}, f32[16,1024]{1,0:T(8,128)S(1)}, u32[]{:S(2)}, u32[]{:S(2)}) %collective-permute-start.8) | collective-permute-done | bytes 65568 | tf_op jit(solution)/shard_map/ppermute | solution.py:512
  22.9 1.6 %collective-permute-done.9.from_both = f32[16,1024]{1,0:T(8,128)S(1)} collective-permute-done((f32[16,1024]{1,0:T(8,128)S(1)}, f32[16,1024]{1,0:T(8,128)S(1)}, u32[]{:S(2)}, u32[]{:S(2)}) %collective-permute-start.9) | collective-permute-done | bytes 65568 | tf_op jit(solution)/shard_map/ppermute | solution.py:512
  24.5 0.7 %shard_map.59 = f32[1,16,4096]{2,1,0:T(8,128)} custom-call(f32[16,1024]{1,0:T(8,128)S(1)} %get-tuple-element.57.own, f32[16,1024]{1,0:T(8,128)S(1)} %collective-permute-done.7.from_core, f32[16,1024]{1,0:T(8,128)S(1)} %collective-permute-done.8.from_x, f32[16,1024]{1,0:T(8,128)S(1)} %collective-permute-done.9.from_both), custom_call_target="tpu_custom_call" | custom-call | tf_op jit(solution)/shard_map/pallas_call | solution.py:486
  (1 shorter events, 0.0 us)
Async XLA Ops:
  1.3 3.7 %collective-permute-start = (f32[136,128]{1,0:T(8,128)S(1)}, f32[136,128]{1,0:T(8,128)S(1)}, u32[]{:S(2)}, u32[]{:S(2)}) collective-permute-start(f32[136,128]{1,0:T(8,128)S(1)} %get-tuple-element.34), channel_id=1, source_target_pairs={{0,8},{8,0},{16,24},{24,16},{1,9},{9,1},{17,25},{25,17},{2,10},{10... | collective-permute-start | bytes 208904 | tf_op jit(solution)/shard_map/ppermute | solution.py:512
  2.0 3.8 %collective-permute-start.1 = (f32[136,128]{1,0:T(8,128)S(1)}, f32[136,128]{1,0:T(8,128)S(1)}, u32[]{:S(2)}, u32[]{:S(2)}) collective-permute-start(f32[136,128]{1,0:T(8,128)S(1)} %get-tuple-element.35), channel_id=1, source_target_pairs={{0,16},{8,24},{16,0},{24,8},{1,17},{9,25},{17,1},{25,9},{2,18},{10... | collective-permute-start | bytes 208904 | tf_op jit(solution)/shard_map/ppermute | solution.py:512
  3.2 4.5 %collective-permute-start.2 = (f32[136,128]{1,0:T(8,128)S(1)}, f32[136,128]{1,0:T(8,128)S(1)}, u32[]{:S(2)}, u32[]{:S(2)}) collective-permute-start(f32[136,128]{1,0:T(8,128)S(1)} %get-tuple-element.36), channel_id=1, source_target_pairs={{0,24},{8,16},{16,8},{24,0},{1,25},{9,17},{17,9},{25,1},{2,26},{10... | collective-permute-start | bytes 208904 | tf_op jit(solution)/shard_map/ppermute | solution.py:512
  3.7 8.0 %collective-permute-start.3 = (f32[248,128]{1,0:T(8,128)S(1)}, f32[248,128]{1,0:T(8,128)S(1)}, u32[]{:S(2)}, u32[]{:S(2)}) collective-permute-start(f32[248,128]{1,0:T(8,128)S(1)} %get-tuple-element.40), channel_id=1, source_target_pairs={{0,1},{1,0},{2,3},{3,2},{4,5},{5,4},{6,7},{7,6},{8,9},{9,8},{10,11... | collective-permute-start | bytes 380936 | tf_op jit(solution)/shard_map/ppermute | solution.py:531
  5.0 6.7 %collective-permute-start.4 = (f32[248,128]{1,0:T(8,128)S(1)}, f32[248,128]{1,0:T(8,128)S(1)}, u32[]{:S(2)}, u32[]{:S(2)}) collective-permute-start(f32[248,128]{1,0:T(8,128)S(1)} %get-tuple-element.41), channel_id=1, source_target_pairs={{1,2},{2,1},{3,4},{4,3},{5,6},{6,5},{7,0},{0,7},{9,10},{10,9},{11,... | collective-permute-start | bytes 380936 | tf_op jit(solution)/shard_map/ppermute | solution.py:532
  7.9 5.6 %collective-permute-start.5 = (f32[184,128]{1,0:T(8,128)S(1)}, f32[184,128]{1,0:T(8,128)S(1)}, u32[]{:S(2)}, u32[]{:S(2)}) collective-permute-start(f32[184,128]{1,0:T(8,128)S(1)} %get-tuple-element.55), channel_id=1, source_target_pairs={{0,1},{1,0},{2,3},{3,2},{4,5},{5,4},{6,7},{7,6},{8,9},{9,8},{10,11... | collective-permute-start | bytes 282632 | tf_op jit(solution)/shard_map/ppermute | solution.py:535
  9.2 6.7 %collective-permute-start.6 = (f32[184,128]{1,0:T(8,128)S(1)}, f32[184,128]{1,0:T(8,128)S(1)}, u32[]{:S(2)}, u32[]{:S(2)}) collective-permute-start(f32[184,128]{1,0:T(8,128)S(1)} %get-tuple-element.56), channel_id=1, source_target_pairs={{1,2},{2,1},{3,4},{4,3},{5,6},{6,5},{9,10},{10,9},{11,12},{12,11},... | collective-permute-start | bytes 282632 | tf_op jit(solution)/shard_map/ppermute | solution.py:536
  18.0 3.0 %collective-permute-start.7 = (f32[16,1024]{1,0:T(8,128)S(1)}, f32[16,1024]{1,0:T(8,128)S(1)}, u32[]{:S(2)}, u32[]{:S(2)}) collective-permute-start(f32[16,1024]{1,0:T(8,128)S(1)} %get-tuple-element.58), channel_id=1, source_target_pairs={{0,8},{8,0},{16,24},{24,16},{1,9},{9,1},{17,25},{25,17},{2,10},{10... | collective-permute-start | bytes 196616 | tf_op jit(solution)/shard_map/ppermute | solution.py:512
  19.3 3.7 %collective-permute-start.8 = (f32[16,1024]{1,0:T(8,128)S(1)}, f32[16,1024]{1,0:T(8,128)S(1)}, u32[]{:S(2)}, u32[]{:S(2)}) collective-permute-start(f32[16,1024]{1,0:T(8,128)S(1)} %get-tuple-element.59), channel_id=1, source_target_pairs={{0,16},{8,24},{16,0},{24,8},{1,17},{9,25},{17,1},{25,9},{2,18},{10... | collective-permute-start | bytes 196616 | tf_op jit(solution)/shard_map/ppermute | solution.py:512
  20.5 4.0 %collective-permute-start.9 = (f32[16,1024]{1,0:T(8,128)S(1)}, f32[16,1024]{1,0:T(8,128)S(1)}, u32[]{:S(2)}, u32[]{:S(2)}) collective-permute-start(f32[16,1024]{1,0:T(8,128)S(1)} %get-tuple-element.60), channel_id=1, source_target_pairs={{0,24},{8,16},{16,8},{24,0},{1,25},{9,17},{17,9},{25,1},{2,26},{10... | collective-permute-start | bytes 196616 | tf_op jit(solution)/shard_map/ppermute | solution.py:512

commit v11 on v10

--- a/solution.py
+++ b/solution.py
@@ -14,6 +14,7 @@
 COEF_ROWS = (10, 9, 9)
 FIELD_ROWS = (10, 8, 4)
 COARSE_ROWS = 3
+SLOTS = (0, 2, 3, 1)
 VMEM_LIMIT = 40 * 1024 * 1024
 
 
@@ -148,7 +149,7 @@
 
 
 def pack_kernel(
-    guess, cond_x, cond_y, source, inflow, own, to_core, to_x, to_both, halo_a, halo_b, coefs, coarse,
+    guess, cond_x, cond_y, source, inflow, own, to_x, to_both, to_core, halo_a, halo_b, coefs, coarse,
     guess_in, coefs_in, inflow_in, spare, sems,
 ):
     rows, columns = guess.shape
@@ -168,7 +169,7 @@
     for copy in copies:
         copy.start()
     copies[0].wait()
-    for slot, out in enumerate((own, to_core, to_x, to_both)):
+    for slot, out in zip(SLOTS, (own, to_x, to_both, to_core)):
         target = member ^ slot
         first = width * target
         for chunk in range(chunks):
@@ -221,10 +222,10 @@
         halo_b[...] = jnp.zeros_like(halo_b)
 
 
-def edge_kernel(own, from_core, from_x, from_both, edge_a, edge_b, fields, spare):
+def edge_kernel(own, from_x, from_both, from_core, edge_a, edge_b, fields, spare):
     member = lax.axis_index("tm")
     chunks, rows = fields.shape[1] - 1, fields.shape[2]
-    for slot, ref in enumerate((own, from_core, from_x, from_both)):
+    for slot, ref in zip(SLOTS, (own, from_x, from_both, from_core)):
         target = fields.at[member ^ slot]
         for chunk in range(chunks):
             target[chunk] = ref[chunk * rows : (chunk + 1) * rows]
@@ -391,7 +392,7 @@
 
 def main_kernel(
     fields, cond_x, cond_y, response, diagonal, up, west, coarse_x, coarse_y, coarse_d, coarse_u, coarse_w,
-    start_error, carried, edge_a, edge_b, own, to_core, to_x, to_both,
+    start_error, carried, edge_a, edge_b, own, to_x, to_both, to_core,
     guess, work, error, spare,
 ):
     groups, chunks, rows, _ = fields.shape
@@ -456,18 +457,18 @@
     error[0, :, HALO:low] = start_error[:, HALO:low]
 
     member = lax.axis_index("tm")
-    for slot, out in enumerate((own, to_core, to_x, to_both)):
+    for slot, out in zip(SLOTS, (own, to_x, to_both, to_core)):
         group = member ^ slot
         relaxed = jnp.where(group == 0, 0, given - 1 + group)
         for chunk in range(chunks):
             out[:, piece(chunk)] = guess[relaxed, chunk, HALO:low] + error[group, chunk, HALO:low]
 
 
-def unpack_kernel(own, from_core, from_x, from_both, out, sems):
+def unpack_kernel(own, from_x, from_both, from_core, out, sems):
     width = own.shape[1]
     member = lax.axis_index("tm")
     copies = []
-    for slot, ref in enumerate((own, from_core, from_x, from_both)):
+    for slot, ref in zip(SLOTS, (own, from_x, from_both, from_core)):
         at = pl.ds(pl.multiple_of((member ^ slot) * width, LANE), width)
         copies.append(pltpu.make_async_copy(ref, out.at[0, :, at], sems.at[slot]))
     for copy in copies:
@@ -497,7 +498,7 @@
 def shards(guesses, cond_x, cond_y, source, inflow):
     groups, strips = lax.axis_size("tm"), lax.axis_size("space")
     rows, columns = cond_x.shape
-    fits = groups == len(FIELD_ROWS) + 1 and strips % 2 == 0 and rows == 16
+    fits = groups == len(SLOTS) and strips % 2 == 0 and rows == 16
     if not fits or columns % (2 * groups * LANE) != 0:
         return general_shards(guesses, cond_x, cond_y, source, inflow)
     own = columns // groups
@@ -508,8 +509,8 @@
 
     def trade(blocks):
         moved = [blocks[0]]
-        for slot in range(1, groups):
-            moved.append(lax.ppermute(blocks[slot], "tm", [(i, i ^ slot) for i in range(groups)]))
+        for slot, block in zip(SLOTS[1:], blocks[1:]):
+            moved.append(lax.ppermute(block, "tm", [(i, i ^ slot) for i in range(groups)]))
         return moved
 
     def whole(count):

time: 25.4 us -> 25.4 us (level)
  waiting for transfers between devices: 9.42 us -> 8.19 us
  starting transfers between devices: 10.4 us -> 11.5 us
    ppermute x1, waiting for transfers between devices: 2.41 us -> 1.51 us  [shards(): edge_b = lax.ppermute(sent_b, 'space', pairs_b)]
    ppermute x6, starting transfers between devices: 5.41 us -> 6.05 us  [trade(): lax.ppermute(block, 'tm', [(i, i ^ slot) for i in range(groups)])]
    ppermute x1, starting transfers between devices: 2.52 us -> 2.91 us  [shards(): edge_b = lax.ppermute(sent_b, 'space', pairs_b)]
    ppermute x6, waiting for transfers between devices: 6.3 us -> 5.97 us  [trade(): lax.ppermute(block, 'tm', [(i, i ^ slot) for i in range(groups)])]
  transfers between devices with their start and end apart: 10 -> 10, of which waited for: 6 -> 5; matrix products, arithmetic and copies ran while one was open for 0% -> 0% of each run, Pallas kernels for 5% -> 5%
where the time goes in v11:
time: 25.4 us; the launch traced here: 25 us
  starting transfers between devices  11.5 us (45%)
  waiting for transfers between devices  8.19 us (32%)
  Pallas kernels  5.33 us (21%)
    ppermute x6, starting transfers between devices, trade(): lax.ppermute(block, 'tm', [(i, i ^ slot) for i in range(groups)])  6.05 us
    ppermute x6, waiting for transfers between devices, trade(): lax.ppermute(block, 'tm', [(i, i ^ slot) for i in range(groups)])  5.97 us
    pallas_call x5, Pallas kernels, call(): pl.pallas_call(kernel, out_shape=[jax.ShapeDtypeStruct(shape, jnp.float32...  5.33 us
    ppermute x1, starting transfers between devices, shards(): edge_b = lax.ppermute(sent_b, 'space', pairs_b)  2.91 us
    ppermute x1, waiting for transfers between devices, shards(): edge_b = lax.ppermute(sent_b, 'space', pairs_b)  1.51 us
    ppermute x1, starting transfers between devices, shards(): edge_a = lax.ppermute(sent_a, 'space', pairs_a)  1.26 us
    ppermute x1, starting transfers between devices, shards(): coef_a = lax.ppermute(halo_a, 'space', pairs_a)  1.24 us
    ppermute x1, waiting for transfers between devices, shards(): edge_a = lax.ppermute(sent_a, 'space', pairs_a)  0.71 us
  transfers between devices with their start and end apart: 10, of which 5 were waited for; matrix products, arithmetic and copies ran while one was open for 0% of the time, Pallas kernels for 5%

profile of v11, /device:TPU:9, one launch (start us, length us, event | category | flops | bytes accessed | tf_op | source)
XLA Modules:
  0.0 25.0 jit_solution(7940641300255732426)
XLA Ops:
  0.0 1.2 %shard_map.55 = (f32[136,128]{1,0:T(8,128)S(1)}, f32[136,128]{1,0:T(8,128)S(1)}, f32[136,128]{1,0:T(8,128)S(1)}, f32[136,128]{1,0:T(8,128)S(1)}, f32[248,128]{1,...) custom-call(f32[16,4096]{1,0:T(8,128)} %bitcast.1, ...), custom_call_target="tpu_custom_call" | custom-call | tf_op jit(solution)/shard_map/pallas_call | solution.py:487
  1.3 1.3 %collective-permute-start = (f32[136,128]{1,0:T(8,128)S(1)}, f32[136,128]{1,0:T(8,128)S(1)}, u32[]{:S(2)}, u32[]{:S(2)}) collective-permute-start(f32[136,128]{1,0:T(8,128)S(1)} %get-tuple-element.34), channel_id=1, source_target_pairs={{0,16},{8,24},{16,0},{24,8},{1,17},{9,25},{17,1},{25,9},{2,18},{10... | collective-permute-start | bytes 208904 | tf_op jit(solution)/shard_map/ppermute | solution.py:513
  2.5 1.1 %collective-permute-start.1 = (f32[136,128]{1,0:T(8,128)S(1)}, f32[136,128]{1,0:T(8,128)S(1)}, u32[]{:S(2)}, u32[]{:S(2)}) collective-permute-start(f32[136,128]{1,0:T(8,128)S(1)} %get-tuple-element.35), channel_id=1, source_target_pairs={{0,24},{8,16},{16,8},{24,0},{1,25},{9,17},{17,9},{25,1},{2,26},{10... | collective-permute-start | bytes 208904 | tf_op jit(solution)/shard_map/ppermute | solution.py:513
  3.6 0.0 collective-permute-start.2
  3.6 1.2 %collective-permute-start.3 = (f32[248,128]{1,0:T(8,128)S(1)}, f32[248,128]{1,0:T(8,128)S(1)}, u32[]{:S(2)}, u32[]{:S(2)}) collective-permute-start(f32[248,128]{1,0:T(8,128)S(1)} %get-tuple-element.40), channel_id=1, source_target_pairs={{0,1},{1,0},{2,3},{3,2},{4,5},{5,4},{6,7},{7,6},{8,9},{9,8},{10,11... | collective-permute-start | bytes 380936 | tf_op jit(solution)/shard_map/ppermute | solution.py:532
  4.9 0.0 collective-permute-start.4
  4.9 0.0 collective-permute-done.from_x
  4.9 2.4 %collective-permute-done.1.from_both = f32[136,128]{1,0:T(8,128)S(1)} collective-permute-done((f32[136,128]{1,0:T(8,128)S(1)}, f32[136,128]{1,0:T(8,128)S(1)}, u32[]{:S(2)}, u32[]{:S(2)}) %collective-permute-start.1) | collective-permute-done | bytes 69664 | tf_op jit(solution)/shard_map/ppermute | solution.py:513
  7.2 0.0 collective-permute-done.2.from_core
  7.2 0.2 shard_map.56
  7.4 1.3 %collective-permute-start.5 = (f32[184,128]{1,0:T(8,128)S(1)}, f32[184,128]{1,0:T(8,128)S(1)}, u32[]{:S(2)}, u32[]{:S(2)}) collective-permute-start(f32[184,128]{1,0:T(8,128)S(1)} %get-tuple-element.55), channel_id=1, source_target_pairs={{0,1},{1,0},{2,3},{3,2},{4,5},{5,4},{6,7},{7,6},{8,9},{9,8},{10,11... | collective-permute-start | bytes 282632 | tf_op jit(solution)/shard_map/ppermute | solution.py:536
  8.7 2.9 %collective-permute-start.6 = (f32[184,128]{1,0:T(8,128)S(1)}, f32[184,128]{1,0:T(8,128)S(1)}, u32[]{:S(2)}, u32[]{:S(2)}) collective-permute-start(f32[184,128]{1,0:T(8,128)S(1)} %get-tuple-element.56), channel_id=1, source_target_pairs={{1,2},{2,1},{3,4},{4,3},{5,6},{6,5},{9,10},{10,9},{11,12},{12,11},... | collective-permute-start | bytes 282632 | tf_op jit(solution)/shard_map/ppermute | solution.py:537
  11.6 0.0 collective-permute-done.3.coef_a
  11.6 0.0 collective-permute-done.4.coef_b
  11.6 1.0 %shard_map.57 = (f32[9,48,128]{2,1,0:T(8,128)S(1)}, f32[9,48,128]{2,1,0:T(8,128)S(1)}, f32[9,48,128]{2,1,0:T(8,128)S(1)}, f32[9,48,128]{2,1,0:T(8,128)S(1)}, f32...) custom-call(f32[3,9,16,128]{3,2,1,0:T(8,128)S(1)} %get-tuple-element, ...), custom_call_target="tpu_custom_call" | custom-call | tf_op jit(solution)/shard_map/pallas_call | solution.py:487
  12.7 0.7 %collective-permute-done.5.edge_a = f32[184,128]{1,0:T(8,128)S(1)} collective-permute-done((f32[184,128]{1,0:T(8,128)S(1)}, f32[184,128]{1,0:T(8,128)S(1)}, u32[]{:S(2)}, u32[]{:S(2)}) %collective-permute-start.5) | collective-permute-done | bytes 94240 | tf_op jit(solution)/shard_map/ppermute | solution.py:536
  13.4 1.5 %collective-permute-done.6.edge_b = f32[184,128]{1,0:T(8,128)S(1)} collective-permute-done((f32[184,128]{1,0:T(8,128)S(1)}, f32[184,128]{1,0:T(8,128)S(1)}, u32[]{:S(2)}, u32[]{:S(2)}) %collective-permute-start.6) | collective-permute-done | bytes 94240 | tf_op jit(solution)/shard_map/ppermute | solution.py:537
  14.9 2.1 %shard_map.58 = (f32[16,1024]{1,0:T(8,128)S(1)}, f32[16,1024]{1,0:T(8,128)S(1)}, f32[16,1024]{1,0:T(8,128)S(1)}, f32[16,1024]{1,0:T(8,128)S(1)}) custom-call(f32[4,9,16,128]{3,2,1,0:T(8,128)S(1)} %get-tuple-element.37.fields, f32[9,48,128]{2,1,0:T(8,128)S(1)} %get-tuple-element.42.cond_x, f32[9,48,128]{2,1,0:T(8,128)S(1)} %get-tuple-element.43.cond_y, ...), custom_call_target="tpu_custom_call" | custom-call | tf_op jit(solution)/shard_map/pallas_call | solution.py:487
  17.0 2.3 %collective-permute-start.7 = (f32[16,1024]{1,0:T(8,128)S(1)}, f32[16,1024]{1,0:T(8,128)S(1)}, u32[]{:S(2)}, u32[]{:S(2)}) collective-permute-start(f32[16,1024]{1,0:T(8,128)S(1)} %get-tuple-element.58), channel_id=1, source_target_pairs={{0,16},{8,24},{16,0},{24,8},{1,17},{9,25},{17,1},{25,9},{2,18},{10... | collective-permute-start | bytes 196616 | tf_op jit(solution)/shard_map/ppermute | solution.py:513
  19.3 1.4 %collective-permute-start.8 = (f32[16,1024]{1,0:T(8,128)S(1)}, f32[16,1024]{1,0:T(8,128)S(1)}, u32[]{:S(2)}, u32[]{:S(2)}) collective-permute-start(f32[16,1024]{1,0:T(8,128)S(1)} %get-tuple-element.59), channel_id=1, source_target_pairs={{0,24},{8,16},{16,8},{24,0},{1,25},{9,17},{17,9},{25,1},{2,26},{10... | collective-permute-start | bytes 196616 | tf_op jit(solution)/shard_map/ppermute | solution.py:513
  20.7 0.2 collective-permute-done.7.from_x
  20.9 3.4 %collective-permute-done.8.from_both = f32[16,1024]{1,0:T(8,128)S(1)} collective-permute-done((f32[16,1024]{1,0:T(8,128)S(1)}, f32[16,1024]{1,0:T(8,128)S(1)}, u32[]{:S(2)}, u32[]{:S(2)}) %collective-permute-start.8) | collective-permute-done | bytes 65568 | tf_op jit(solution)/shard_map/ppermute | solution.py:513
  24.3 0.0 collective-permute-done.9.from_core
  24.3 0.7 %shard_map.59 = f32[1,16,4096]{2,1,0:T(8,128)} custom-call(f32[16,1024]{1,0:T(8,128)S(1)} %get-tuple-element.57.own, f32[16,1024]{1,0:T(8,128)S(1)} %collective-permute-done.7.from_x, f32[16,1024]{1,0:T(8,128)S(1)} %collective-permute-done.8.from_both, f32[16,1024]{1,0:T(8,128)S(1)} %collective-permute-done.9.from_core), custom_call_target="tpu_custom_call" | custom-call | tf_op jit(solution)/shard_map/pallas_call | solution.py:487
  (1 shorter events, 0.0 us)
Async XLA Ops:
  1.3 3.6 %collective-permute-start = (f32[136,128]{1,0:T(8,128)S(1)}, f32[136,128]{1,0:T(8,128)S(1)}, u32[]{:S(2)}, u32[]{:S(2)}) collective-permute-start(f32[136,128]{1,0:T(8,128)S(1)} %get-tuple-element.34), channel_id=1, source_target_pairs={{0,16},{8,24},{16,0},{24,8},{1,17},{9,25},{17,1},{25,9},{2,18},{10... | collective-permute-start | bytes 208904 | tf_op jit(solution)/shard_map/ppermute | solution.py:513
  2.5 4.7 %collective-permute-start.1 = (f32[136,128]{1,0:T(8,128)S(1)}, f32[136,128]{1,0:T(8,128)S(1)}, u32[]{:S(2)}, u32[]{:S(2)}) collective-permute-start(f32[136,128]{1,0:T(8,128)S(1)} %get-tuple-element.35), channel_id=1, source_target_pairs={{0,24},{8,16},{16,8},{24,0},{1,25},{9,17},{17,9},{25,1},{2,26},{10... | collective-permute-start | bytes 208904 | tf_op jit(solution)/shard_map/ppermute | solution.py:513
  3.6 3.6 %collective-permute-start.2 = (f32[136,128]{1,0:T(8,128)S(1)}, f32[136,128]{1,0:T(8,128)S(1)}, u32[]{:S(2)}, u32[]{:S(2)}) collective-permute-start(f32[136,128]{1,0:T(8,128)S(1)} %get-tuple-element.36), channel_id=1, source_target_pairs={{0,8},{8,0},{16,24},{24,16},{1,9},{9,1},{17,25},{25,17},{2,10},{10... | collective-permute-start | bytes 208904 | tf_op jit(solution)/shard_map/ppermute | solution.py:513
  3.6 8.0 %collective-permute-start.3 = (f32[248,128]{1,0:T(8,128)S(1)}, f32[248,128]{1,0:T(8,128)S(1)}, u32[]{:S(2)}, u32[]{:S(2)}) collective-permute-start(f32[248,128]{1,0:T(8,128)S(1)} %get-tuple-element.40), channel_id=1, source_target_pairs={{0,1},{1,0},{2,3},{3,2},{4,5},{5,4},{6,7},{7,6},{8,9},{9,8},{10,11... | collective-permute-start | bytes 380936 | tf_op jit(solution)/shard_map/ppermute | solution.py:532
  4.9 6.7 %collective-permute-start.4 = (f32[248,128]{1,0:T(8,128)S(1)}, f32[248,128]{1,0:T(8,128)S(1)}, u32[]{:S(2)}, u32[]{:S(2)}) collective-permute-start(f32[248,128]{1,0:T(8,128)S(1)} %get-tuple-element.41), channel_id=1, source_target_pairs={{1,2},{2,1},{3,4},{4,3},{5,6},{6,5},{7,0},{0,7},{9,10},{10,9},{11,... | collective-permute-start | bytes 380936 | tf_op jit(solution)/shard_map/ppermute | solution.py:533
  7.4 6.0 %collective-permute-start.5 = (f32[184,128]{1,0:T(8,128)S(1)}, f32[184,128]{1,0:T(8,128)S(1)}, u32[]{:S(2)}, u32[]{:S(2)}) collective-permute-start(f32[184,128]{1,0:T(8,128)S(1)} %get-tuple-element.55), channel_id=1, source_target_pairs={{0,1},{1,0},{2,3},{3,2},{4,5},{5,4},{6,7},{7,6},{8,9},{9,8},{10,11... | collective-permute-start | bytes 282632 | tf_op jit(solution)/shard_map/ppermute | solution.py:536
  8.7 6.2 %collective-permute-start.6 = (f32[184,128]{1,0:T(8,128)S(1)}, f32[184,128]{1,0:T(8,128)S(1)}, u32[]{:S(2)}, u32[]{:S(2)}) collective-permute-start(f32[184,128]{1,0:T(8,128)S(1)} %get-tuple-element.56), channel_id=1, source_target_pairs={{1,2},{2,1},{3,4},{4,3},{5,6},{6,5},{9,10},{10,9},{11,12},{12,11},... | collective-permute-start | bytes 282632 | tf_op jit(solution)/shard_map/ppermute | solution.py:537
  17.0 3.9 %collective-permute-start.7 = (f32[16,1024]{1,0:T(8,128)S(1)}, f32[16,1024]{1,0:T(8,128)S(1)}, u32[]{:S(2)}, u32[]{:S(2)}) collective-permute-start(f32[16,1024]{1,0:T(8,128)S(1)} %get-tuple-element.58), channel_id=1, source_target_pairs={{0,16},{8,24},{16,0},{24,8},{1,17},{9,25},{17,1},{25,9},{2,18},{10... | collective-permute-start | bytes 196616 | tf_op jit(solution)/shard_map/ppermute | solution.py:513
  19.3 5.0 %collective-permute-start.8 = (f32[16,1024]{1,0:T(8,128)S(1)}, f32[16,1024]{1,0:T(8,128)S(1)}, u32[]{:S(2)}, u32[]{:S(2)}) collective-permute-start(f32[16,1024]{1,0:T(8,128)S(1)} %get-tuple-element.59), channel_id=1, source_target_pairs={{0,24},{8,16},{16,8},{24,0},{1,25},{9,17},{17,9},{25,1},{2,26},{10... | collective-permute-start | bytes 196616 | tf_op jit(solution)/shard_map/ppermute | solution.py:513
  20.7 3.6 %collective-permute-start.9 = (f32[16,1024]{1,0:T(8,128)S(1)}, f32[16,1024]{1,0:T(8,128)S(1)}, u32[]{:S(2)}, u32[]{:S(2)}) collective-permute-start(f32[16,1024]{1,0:T(8,128)S(1)} %get-tuple-element.60), channel_id=1, source_target_pairs={{0,8},{8,0},{16,24},{24,16},{1,9},{9,1},{17,25},{25,17},{2,10},{10... | collective-permute-start | bytes 196616 | tf_op jit(solution)/shard_map/ppermute | solution.py:513
